TPU v7x, 32 devices: a whole 2x2x4 slice. The times are simulated.
32 devices in a mesh: cand: 16 (over z, y, core), img: 2 (over x).
Axes of the slice: x: 2, y: 2, z: 4, core: 2. Of those that a mesh axis runs over, the one named last changes fastest.
Arguments:
- first_maps: float32 [2, 256, 344], P('img', 'cand'), may hold values from -6 to 6
- layer_of: int32 [16], P('cand'), may hold values from 0 to 1, as said below
- expand_half: int32 [16], P('cand'), may hold values from 1 to 2
- radius: int32 [16], P('cand'), may hold values from 1 to 2
- teach_up: bfloat16 [2, 344, 2064], replicated, may hold values from -0.3125 to 0.3125
- teach_dw: float32 [2, 25, 2064], replicated, may hold values from -1.25 to 1.25
- teach_down: bfloat16 [2, 344, 2064], replicated, may hold values from -0.125 to 0.125
- cand_up: bfloat16 [16, 344, 2064], P('cand'), may hold values from -0.3125 to 0.3125
- cand_dw: float32 [16, 25, 2064], P('cand'), may hold values from -1.25 to 1.25
- cand_down: bfloat16 [16, 344, 2064], P('cand'), may hold values from -0.125 to 0.125
Outputs:
- grad_up: float32 [16, 344, 2064], P('cand', None, 'img')
- grad_dw: float32 [16, 25, 2064], P('cand', None, 'img')
- grad_down: float32 [16, 344, 2064], P('cand', None, 'img')
Inputs may be any that keep to these rules, and one draw needn't show every extreme that they name: `layer_of`: both layers have at least one candidate.
All inputs are finite; a program needn't handle non-finite values.
Results may differ from a plain program's by a relative error of at most 0.014.
Values may be sent and summed in bfloat16 or wider, within the bound.
No kernel may reach another device: no remote copies, remote signals or barrier semaphores. Data moves between devices by JAX's collectives and lax.ppermute only.
A program may use at most 192 MiB of HBM per device.

v0:
```python
import functools

import jax
import jax.numpy as jnp
import ml_dtypes
import numpy as np
from jax import lax
from jax.experimental import pallas as pl
from jax.experimental.pallas import tpu as pltpu
from jax.sharding import PartitionSpec as P

F32 = jnp.float32
BF16 = jnp.bfloat16
LANES = 128
TILE = 1024


def round_up(value, step):
    return -(-value // step) * step


def dft_matrices(side, taps):
    width = int(round(taps**0.5))
    reach = width // 2
    period = side + reach
    kept = []
    for u in range(period):
        for v in range(period):
            if (u, v) <= ((-u) % period, (-v) % period):
                kept.append((u, v))
    freqs = np.array(kept)
    count = len(kept)
    rows = round_up(count, 8)
    mirrored = ((-freqs) % period == freqs).all(axis=1)
    weight = np.where(mirrored, 1.0, 2.0) / period**2
    cell = np.stack(np.meshgrid(np.arange(side), np.arange(side), indexing="ij"), -1).reshape(-1, 2)
    half = len(cell) // 2
    cell = np.concatenate([cell[:half], cell[half:][::-1]]) - (side - 1) / 2
    tap = np.stack(np.meshgrid(np.arange(width), np.arange(width), indexing="ij"), -1).reshape(-1, 2) - reach
    cell_angle = 2 * np.pi * (freqs @ cell.T) / period
    tap_angle = 2 * np.pi * ((freqs @ tap.T) % period) / period
    tap_rows = round_up(taps, 16)

    analysis = np.zeros((2 * rows, side * side))
    analysis[:count] = np.cos(cell_angle)
    analysis[rows : rows + count] = -np.sin(cell_angle)
    even = np.zeros((half, rows))
    even[:, :count] = (weight[:, None] * np.cos(cell_angle)).T[:half]
    odd = np.zeros((half, rows))
    odd[:, :count] = -(weight[:, None] * np.sin(cell_angle)).T[:half]
    spectrum = np.zeros((2 * rows, tap_rows))
    spectrum[:count, :taps] = np.cos(tap_angle)
    spectrum[rows : rows + count, :taps] = np.sin(tap_angle)
    gather = np.zeros((tap_rows, 2 * rows))
    gather[:taps, :count] = (weight[:, None] * np.cos(tap_angle)).T
    gather[:taps, rows : rows + count] = -(weight[:, None] * np.sin(tap_angle)).T

    coarse = spectrum.astype(ml_dtypes.bfloat16).astype(np.float64)
    spectrum = np.concatenate([coarse, coarse, spectrum - coarse], axis=1)
    return rows, [jnp.asarray(m.astype(ml_dtypes.bfloat16)) for m in (analysis, even, odd, spectrum, gather)]


def dot(a, b):
    return jnp.dot(a, b, preferred_element_type=F32)


def dot_nt(a, b):
    return lax.dot_general(a, b, (((1,), (1,)), ((), ())), preferred_element_type=F32)


def grads_kernel(
    dims,
    offsets,
    layer_ref,
    half_ref,
    radius_ref,
    place_ref,
    *refs,
):
    x_refs, refs = refs[: len(offsets)], refs[len(offsets) :]
    (
    analysis_ref,
    even_ref,
    odd_ref,
    spectrum_ref,
    gather_ref,
    teach_up,
    teach_dw,
    teach_down,
    cand_up,
    cand_dw,
    cand_down,
    grad_up,
    grad_dw,
    grad_down,
    up_buf,
    dw_buf,
    cand_dw_buf,
    down_buf,
    up_tail,
    dw_pad,
    down_pad,
    act,
    spec,
    slope_e,
    slope_k,
    x_first,
    x_now,
    x_turned,
    err_now,
    err_turned,
    target,
    wide_up,
    wide_dw,
    wide_down,
    sems,
    ) = refs
    maps, cells, channels, hid, taps, rows, parts, scale = dims
    main = hid // TILE * TILE
    tail = hid - main
    padded = round_up(hid, LANES)
    own = hid // parts
    window = wide_up.shape[1]

    def copies(slot):
        if slot < 2:
            sources = (teach_up.at[slot], teach_dw, teach_down.at[slot])
            targets = (up_buf.at[slot], dw_buf, down_buf.at[slot])
        else:
            sources = (cand_up.at[0], cand_dw, cand_down.at[0])
            targets = (up_buf.at[slot], cand_dw_buf, down_buf.at[slot])
        if slot == 1:
            sources, targets = sources[::2], targets[::2]
        return [
            pltpu.make_async_copy(src, dst, sems.at[slot, n])
            for n, (src, dst) in enumerate(zip(sources, targets))
        ]

    for slot in (0, 2):
        for copy in copies(slot):
            copy.start()

    @pl.when(layer_ref[0] != 0)
    def _():
        for copy in copies(1):
            copy.start()

    analysis = analysis_ref[...]
    even, odd = even_ref[...], odd_ref[...]
    spectrum = spectrum_ref[...]
    dw_pad[...] = jnp.zeros_like(dw_pad)
    up_tail[...] = jnp.zeros_like(up_tail)
    down_pad[:, main:] = jnp.zeros((channels, padded - main), BF16)

    half_cells = cells // 2

    def synthesis(re, im):
        same, other = dot(even, re.astype(BF16)), dot(odd, im.astype(BF16))
        return jnp.concatenate([same + other, same - other], axis=0)

    def tap_spectrum(cols):
        weights = dw_pad[:, cols]
        high = weights.astype(BF16)
        low = (weights - high.astype(F32)).astype(BF16)
        both = dot(spectrum, jnp.concatenate([high, low, high], axis=0))
        return both[:rows], both[rows:]

    def load(slot, mask_taps):
        for copy in copies(slot):
            copy.wait()
        weights = cand_dw_buf[:, 0] if slot == 2 else dw_buf[:, slot]
        if mask_taps:
            side = int(round(taps**0.5))
            index = lax.broadcasted_iota(jnp.int32, weights.shape, 0)
            row = sum((index >= side * n).astype(jnp.int32) for n in range(1, side))
            ring = jnp.maximum(jnp.abs(row - side // 2), jnp.abs(index - side * row - side // 2))
            unit = lax.broadcasted_iota(jnp.int32, weights.shape, 1)
            keep = (ring <= radius_ref[0]) & (unit < half_ref[0] * (hid // 2))
            weights = jnp.where(keep, weights, 0.0)
        dw_pad[:taps, :hid] = weights
        if tail:
            up_tail[:, :tail] = up_buf[slot, :, main:]
            down_pad[:, main:hid] = down_buf[slot, :, main:]

    def forward(slot, keep):
        def tile(cols, weights_up):
            pre = dot(x_now[...], weights_up)
            half = 0.5 * pre
            bend = jnp.tanh(half)
            units = (half + half * bend).astype(BF16)
            if keep:
                slope_e[:, cols] = (0.5 * ((1.0 + bend) + half * (1.0 - bend * bend))).astype(BF16)
            tap_re, tap_im = tap_spectrum(cols)
            for m in range(maps):
                here = slice(m * cells, (m + 1) * cells)
                both = dot(analysis, units[here])
                re, im = both[:rows], both[rows:]
                if keep:
                    spec[m, :, cols] = both.astype(BF16)
                mixed = synthesis(re * tap_re - im * tap_im, re * tap_im + im * tap_re)
                half_k = 0.5 * mixed
                bend_k = jnp.tanh(half_k)
                act[here, cols] = (half_k + half_k * bend_k).astype(BF16)
                if keep:
                    slope_k[here, cols] = (0.5 * ((1.0 + bend_k) + half_k * (1.0 - bend_k * bend_k))).astype(BF16)

        def step(n, _):
            cols = pl.ds(pl.multiple_of(n * TILE, TILE), TILE)
            tile(cols, up_buf[slot, :, cols])
            return 0

        lax.fori_loop(0, main // TILE, step, 0)
        if tail:
            tile(pl.ds(main, padded - main), up_tail[...])
        out = dot_nt(act[:, :main], down_buf[slot, :, :main])
        if tail:
            out += dot_nt(act[:, main:], down_pad[:, main:])
        return out

    whole_turn = (
        lax.broadcasted_iota(jnp.int32, (half_cells, half_cells), 0)
        + lax.broadcasted_iota(jnp.int32, (half_cells, half_cells), 1)
    ) == half_cells - 1
    turn_half = whole_turn.astype(F32).astype(BF16)
    for x_ref, offset in zip(x_refs, offsets):
        if offset is None:
            x_first[...] = x_ref[...]
            continue
        block = x_ref.shape[1]
        for n, distance in enumerate(offset):
            source = place_ref[0] ^ distance
            source = (source & (parts - 1)) * (cells // block) + (source >> (parts.bit_length() - 1))
            at = pl.multiple_of(source * block, block)
            x_first[pl.ds(at, block), :] = x_ref[n]
    for m in range(maps):
        second = slice(m * cells + half_cells, (m + 1) * cells)
        x_first[second] = dot(turn_half, x_first[second]).astype(BF16)
    x_now[...] = x_first[...]
    load(0, False)
    target[...] = forward(0, False)

    @pl.when(layer_ref[0] != 0)
    def _():
        x_now[...] = (x_first[...].astype(F32) + target[...]).astype(BF16)
        load(1, False)
        target[...] = forward(1, False)

    load(2, True)
    down_pad[:, :main] = down_buf[2, :, :main]
    err = (forward(2, True) - target[...]) * scale
    err_now[...] = err.astype(BF16)
    err_turned[...] = jnp.transpose(err).astype(BF16)
    x_turned[...] = jnp.transpose(x_now[...].astype(F32)).astype(BF16)

    start = place_ref[1] * own
    base = jnp.minimum(start // LANES * LANES, padded - window)

    def back(at, width):
        cols = pl.ds(pl.multiple_of(base + at, LANES), width)
        here = pl.ds(pl.multiple_of(at, LANES), width)
        grad_act = dot(err_now[...], down_pad[:, cols])
        grad_k = (grad_act * slope_k[:, cols].astype(F32)).astype(BF16)
        tap_re, tap_im = tap_spectrum(cols)
        sum_re = jnp.zeros((rows, width), F32)
        sum_im = jnp.zeros((rows, width), F32)
        grad_pre = []
        for m in range(maps):
            rows_here = slice(m * cells, (m + 1) * cells)
            both = dot(analysis, grad_k[rows_here])
            re, im = both[:rows], both[rows:]
            kept = spec[m, :, cols].astype(F32)
            e_re, e_im = kept[:rows], kept[rows:]
            sum_re += re * e_re + im * e_im
            sum_im += re * e_im - im * e_re
            grad_e = synthesis(re * tap_re + im * tap_im, im * tap_re - re * tap_im)
            grad_pre.append((grad_e * slope_e[rows_here, cols].astype(F32)).astype(BF16))
        wide_up[:, here] = dot(x_turned[...], jnp.concatenate(grad_pre, axis=0))
        wide_down[:, here] = dot(err_turned[...], act[:, cols])
        sums = jnp.concatenate([sum_re, sum_im], axis=0).astype(BF16)
        wide_dw[:, here] = dot(gather_ref[...], sums)

    def back_step(n, _):
        back(n * TILE, TILE)
        return 0

    lax.fori_loop(0, window // TILE, back_step, 0)
    if window % TILE:
        back(window // TILE * TILE, window % TILE)

    offset = start - base
    turn = lax.rem(window - offset, window)
    grad_up[0] = pltpu.roll(wide_up[...], turn, 1)[:, :own]
    grad_down[0] = pltpu.roll(wide_down[...], turn, 1)[:, :own]
    rolled = pltpu.roll(wide_dw[...], turn, 1)[:taps, :own]
    side = int(round(taps**0.5))
    index = lax.broadcasted_iota(jnp.int32, rolled.shape, 0)
    row = sum((index >= side * n).astype(jnp.int32) for n in range(1, side))
    ring = jnp.maximum(jnp.abs(row - side // 2), jnp.abs(index - side * row - side // 2))
    unit = lax.broadcasted_iota(jnp.int32, rolled.shape, 1) + start
    keep = (ring <= radius_ref[0]) & (unit < half_ref[0] * (hid // 2))
    grad_dw[:, 0] = jnp.where(keep, rolled, 0.0)


def local_grads(pieces, offsets, maps, layer, half, radius, place, parts, images, weights):
    teach_up, teach_dw, teach_down, cand_up, cand_dw, cand_down = weights
    weights = (teach_up, teach_dw.transpose(1, 0, 2), teach_down, cand_up, cand_dw.transpose(1, 0, 2), cand_down)
    channels, hid = teach_up.shape[1:]
    taps = teach_dw.shape[1]
    count = sum(piece.size for piece in pieces) // channels
    cells = count // maps
    side = int(round(cells**0.5))
    rows, constants = dft_matrices(side, taps)
    padded = round_up(hid, LANES)
    own = hid // parts
    spare = max((p * own) % LANES for p in range(parts))
    window = min(round_up(own + spare, LANES), padded)
    tap_rows = round_up(taps, 16)
    main = hid // TILE * TILE
    dims = (maps, cells, channels, hid, taps, rows, parts, 1.0 / images)
    smem = pl.BlockSpec(memory_space=pltpu.SMEM)
    vmem = pl.BlockSpec(memory_space=pltpu.VMEM)
    anywhere = pl.BlockSpec(memory_space=pl.ANY)
    grad_up, grad_dw, grad_down = pl.pallas_call(
        functools.partial(grads_kernel, dims, offsets),
        out_shape=(
            jax.ShapeDtypeStruct((1, channels, own), F32),
            jax.ShapeDtypeStruct((taps, 1, own), F32),
            jax.ShapeDtypeStruct((1, channels, own), F32),
        ),
        in_specs=[smem] * 4 + [vmem] * (len(pieces) + 5) + [anywhere] * 6,
        out_specs=(vmem, vmem, vmem),
        scratch_shapes=[
            pltpu.VMEM((3, channels, hid), BF16),
            pltpu.VMEM(weights[1].shape, F32),
            pltpu.VMEM(weights[4].shape, F32),
            pltpu.VMEM((3, channels, hid), BF16),
            pltpu.VMEM((channels, max(padded - main, LANES)), BF16),
            pltpu.VMEM((tap_rows, padded), F32),
            pltpu.VMEM((channels, padded), BF16),
            pltpu.VMEM((count, padded), BF16),
            pltpu.VMEM((maps, 2 * rows, padded), BF16),
            pltpu.VMEM((count, padded), BF16),
            pltpu.VMEM((count, padded), BF16),
            pltpu.VMEM((count, channels), BF16),
            pltpu.VMEM((count, channels), BF16),
            pltpu.VMEM((channels, count), BF16),
            pltpu.VMEM((count, channels), BF16),
            pltpu.VMEM((channels, count), BF16),
            pltpu.VMEM((count, channels), F32),
            pltpu.VMEM((channels, window), F32),
            pltpu.VMEM((tap_rows, window), F32),
            pltpu.VMEM((channels, window), F32),
            pltpu.SemaphoreType.DMA((3, 3)),
        ],
        compiler_params=pltpu.CompilerParams(vmem_limit_bytes=60 * 2**20),
        cost_estimate=pl.CostEstimate(
            flops=20 * count * channels * hid, bytes_accessed=12 * channels * hid, transcendentals=6 * count * hid
        ),
    )(layer, half, radius, place, *pieces, *constants, *weights)
    return grad_up, grad_dw.transpose(1, 0, 2), grad_down


def exchange(block, masks, axes, devices):
    offset = [0]
    for mask in masks:
        distances = [d for d in range(1, devices) if d & ~mask == 0]
        parts = [block] + [
            lax.ppermute(block, axes, [(source, source ^ d) for source in range(devices)]) for d in distances
        ]
        pieces = [[o ^ d for o in offset] for d in [0] + distances]
        offset = sum(pieces, [])
        if mask != masks[-1]:
            block = jnp.concatenate(parts, axis=0)
    return parts, pieces


def body(
    first_maps,
    layer_of,
    expand_half,
    radius,
    teach_up,
    teach_dw,
    teach_down,
    cand_up,
    cand_dw,
    cand_down,
):
    parts = lax.axis_size("img")
    cands = lax.axis_size("cand")
    devices = parts * cands
    batch, own_cells, channels = first_maps.shape
    images = parts * batch
    part = lax.axis_index("img")
    place = jnp.stack([lax.axis_index("cand") * parts + part, part])
    weights = (teach_up, teach_dw, teach_down, cand_up, cand_dw, cand_down)
    scalars = (layer_of, expand_half, radius, place, parts, images, weights)
    mine = first_maps.astype(BF16)
    if batch == 1 and images == 2 and own_cells % 16 == 0 and devices & (devices - 1) == 0:
        low = min(2, cands) - 1
        low, near = low * parts, (parts - 1) | (low * parts * 2)
        masks = [(devices - 1) & ~near & ~low, near, low]
        pieces, offsets = exchange(mine, masks, ("cand", "img"), devices)
        return local_grads(pieces, offsets, images, *scalars)
    whole = lax.all_gather(mine, ("img", "cand")).reshape(parts, cands, batch, own_cells, channels)
    whole = whole.transpose(0, 2, 1, 3, 4).reshape(images, -1, channels)
    group = 2 if images % 2 == 0 else 1
    total = None
    for first in range(0, images, group):
        pieces = [whole[first : first + group].reshape(-1, channels)]
        grads = local_grads(pieces, [None], group, *scalars)
        total = grads if total is None else tuple(a + b for a, b in zip(total, grads))
    return total


def solution(mesh):
    placed = (
        P("img", "cand", None),
        P("cand"),
        P("cand"),
        P("cand"),
        P(),
        P(),
        P(),
        P("cand", None, None),
        P("cand", None, None),
        P("cand", None, None),
    )
    return jax.shard_map(
        body,
        mesh=mesh,
        in_specs=placed,
        out_specs=(P("cand", None, "img"), P("cand", None, "img"), P("cand", None, "img")),
        check_vma=False,
    )
```

profile of v0, /device:TPU:1, one launch (start us, length us, event | category | flops | bytes accessed | tf_op | source)
XLA Modules:
  0.0 53.8 jit_solution(5156723753307474838)
XLA Ops:
  0.6 0.7 %constant_dynamic-update-slice_fusion.6 = (bf16[16,16,344]{2,1,0:T(8,128)(2,1)S(1)}, bf16[1,16,344]{2,1,0:T(8,128)(2,1)S(1)}) fusion(f32[1,16,344]{2,1,0:T(8,128)} %param.15), kind=kLoop, calls=%fused_computation.7 | loop fusion | flops 5503 | bytes 46592
  1.4 4.2 %collective-permute-start.2 = (bf16[1,16,344]{2,1,0:T(8,128)(2,1)S(1)}, bf16[1,16,344]{2,1,0:T(8,128)(2,1)S(1)}, u32[]{:S(2)}, u32[]{:S(2)}) collective-permute-start(bf16[1,16,344]{2,1,0:T(8,128)(2,1)S(1)} %get-tuple-element.10), channel_id=1, source_target_pairs={{0,24},{1,25},{2,26},{3,27},{4,28},{5,29},{6,30},{7,31},{8,16},{9,... | collective-permute-start | bytes 33032 | tf_op jit(solution)/shard_map/ppermute | solution.py:368
  5.5 0.0 collective-permute-start.1
  5.5 0.3 collective-permute-start
  5.8 0.8 %collective-permute-done.2 = bf16[1,16,344]{2,1,0:T(8,128)(2,1)S(1)} collective-permute-done((bf16[1,16,344]{2,1,0:T(8,128)(2,1)S(1)}, bf16[1,16,344]{2,1,0:T(8,128)(2,1)S(1)}, u32[]{:S(2)}, u32[]{:S(2)}) %collective-permute-start.2) | collective-permute-done | bytes 11040 | tf_op jit(solution)/shard_map/ppermute | solution.py:368
  6.6 2.4 %collective-permute-done.1 = bf16[1,16,344]{2,1,0:T(8,128)(2,1)S(1)} collective-permute-done((bf16[1,16,344]{2,1,0:T(8,128)(2,1)S(1)}, bf16[1,16,344]{2,1,0:T(8,128)(2,1)S(1)}, u32[]{:S(2)}, u32[]{:S(2)}) %collective-permute-start.1) | collective-permute-done | bytes 11040 | tf_op jit(solution)/shard_map/ppermute | solution.py:368
  9.0 0.0 collective-permute-done
  9.0 2.2 %collective-permute-start.5 = (bf16[4,16,344]{2,1,0:T(8,128)(2,1)S(1)}, bf16[4,16,344]{2,1,0:T(8,128)(2,1)S(1)}, u32[]{:S(2)}, u32[]{:S(2)}) collective-permute-start(bf16[4,16,344]{2,1,0:T(8,128)(2,1)S(1)} %pad_maximum_fusion), channel_id=1, source_target_pairs={{0,5},{1,4},{2,7},{3,6},{4,1},{5,0},{6,3},{7,2},{8,13},{9,12},{10,... | collective-permute-start | bytes 132104 | tf_op jit(solution)/shard_map/ppermute | solution.py:368
  11.2 0.2 collective-permute-start.4
  11.5 0.3 collective-permute-start.3
  11.7 2.7 %collective-permute-done.3 = bf16[4,16,344]{2,1,0:T(8,128)(2,1)S(1)} collective-permute-done((bf16[4,16,344]{2,1,0:T(8,128)(2,1)S(1)}, bf16[4,16,344]{2,1,0:T(8,128)(2,1)S(1)}, u32[]{:S(2)}, u32[]{:S(2)}) %collective-permute-start.3) | collective-permute-done | bytes 44064 | tf_op jit(solution)/shard_map/ppermute | solution.py:368
  14.4 0.0 collective-permute-done.4
  14.4 0.0 collective-permute-done.5
  14.5 0.0 copy-start
  14.5 3.9 %collective-permute-start.6 = (bf16[16,16,344]{2,1,0:T(8,128)(2,1)S(1)}, bf16[16,16,344]{2,1,0:T(8,128)(2,1)S(1)}, u32[]{:S(2)}, u32[]{:S(2)}) collective-permute-start(bf16[16,16,344]{2,1,0:T(8,128)(2,1)S(1)} %constant_dynamic-update-slice_fusion.refs_0_), channel_id=1, source_target_pairs={{0,2},{1,3},{2,0},{3,1},{4,6},{5,7},{6,4},{7,5},{8,10},{9,11},{10,... | collective-permute-start | bytes 528392 | tf_op jit(solution)/shard_map/ppermute | solution.py:368
  20.3 0.6 %pad_add_fusion.place_ref = s32[2]{0:T(128)} fusion(s32[1]{0:T(128)} %bitcast.1, s32[1]{0:T(128)} %bitcast), kind=kLoop, calls=%fused_computation.8 | loop fusion | flops 2 | bytes 16 | tf_op jit(solution)/shard_map/stack | solution.py:395
  20.9 0.0 collective-permute-done.6.refs_1_
  20.9 0.0 copy-start.1
  20.9 0.0 copy-done
  20.9 0.7 %copy-done.1 = bf16[16,16,344]{2,1,0:T(8,128)(2,1)} copy-done((bf16[16,16,344]{2,1,0:T(8,128)(2,1)}, bf16[16,16,344]{2,1,0:T(8,128)(2,1)S(1)}, u32[]{:S(2)}) %copy-start.1) | copy-done | bytes 176152
  21.6 32.0 %shard_map.166 = (f32[1,344,1032]{2,1,0:T(8,128)}, f32[25,1,1032]{2,1,0:T(1,128)}, f32[1,344,1032]{2,1,0:T(8,128)}) custom-call(s32[1]{0:T(128)S(6)} %copy.24.layer_ref, s32[1]{0:T(128)S(6)} %copy.25.half_ref, s32[1]{0:T(128)S(6)} %copy.26.radius_ref, s32[2]{0:T(128)} %pad_add_fusion.place_ref, bf16[16,16,344]{2,1,0:T(8,128)(2,1)} %copy-done, ...), custom_call_target="tpu_custom_call" | custom-call | flops 7270563840 | bytes 8520192 | tf_op jit(solution)/shard_map/pallas_call | solution.py:323
  (7 shorter events, 0.1 us)
Async XLA Ops:
  1.4 5.2 %collective-permute-start.2 = (bf16[1,16,344]{2,1,0:T(8,128)(2,1)S(1)}, bf16[1,16,344]{2,1,0:T(8,128)(2,1)S(1)}, u32[]{:S(2)}, u32[]{:S(2)}) collective-permute-start(bf16[1,16,344]{2,1,0:T(8,128)(2,1)S(1)} %get-tuple-element.10), channel_id=1, source_target_pairs={{0,24},{1,25},{2,26},{3,27},{4,28},{5,29},{6,30},{7,31},{8,16},{9,... | collective-permute-start | bytes 33032 | tf_op jit(solution)/shard_map/ppermute | solution.py:368
  5.5 3.4 %collective-permute-start.1 = (bf16[1,16,344]{2,1,0:T(8,128)(2,1)S(1)}, bf16[1,16,344]{2,1,0:T(8,128)(2,1)S(1)}, u32[]{:S(2)}, u32[]{:S(2)}) collective-permute-start(bf16[1,16,344]{2,1,0:T(8,128)(2,1)S(1)} %get-tuple-element.10), channel_id=1, source_target_pairs={{0,16},{1,17},{2,18},{3,19},{4,20},{5,21},{6,22},{7,23},{8,24},{9,... | collective-permute-start | bytes 33032 | tf_op jit(solution)/shard_map/ppermute | solution.py:368
  5.5 3.4 %collective-permute-start = (bf16[1,16,344]{2,1,0:T(8,128)(2,1)S(1)}, bf16[1,16,344]{2,1,0:T(8,128)(2,1)S(1)}, u32[]{:S(2)}, u32[]{:S(2)}) collective-permute-start(bf16[1,16,344]{2,1,0:T(8,128)(2,1)S(1)} %get-tuple-element.10), channel_id=1, source_target_pairs={{0,8},{1,9},{2,10},{3,11},{4,12},{5,13},{6,14},{7,15},{8,0},{9,1},... | collective-permute-start | bytes 33032 | tf_op jit(solution)/shard_map/ppermute | solution.py:368
  9.0 5.4 %collective-permute-start.5 = (bf16[4,16,344]{2,1,0:T(8,128)(2,1)S(1)}, bf16[4,16,344]{2,1,0:T(8,128)(2,1)S(1)}, u32[]{:S(2)}, u32[]{:S(2)}) collective-permute-start(bf16[4,16,344]{2,1,0:T(8,128)(2,1)S(1)} %pad_maximum_fusion), channel_id=1, source_target_pairs={{0,5},{1,4},{2,7},{3,6},{4,1},{5,0},{6,3},{7,2},{8,13},{9,12},{10,... | collective-permute-start | bytes 132104 | tf_op jit(solution)/shard_map/ppermute | solution.py:368
  11.2 3.2 %collective-permute-start.4 = (bf16[4,16,344]{2,1,0:T(8,128)(2,1)S(1)}, bf16[4,16,344]{2,1,0:T(8,128)(2,1)S(1)}, u32[]{:S(2)}, u32[]{:S(2)}) collective-permute-start(bf16[4,16,344]{2,1,0:T(8,128)(2,1)S(1)} %pad_maximum_fusion), channel_id=1, source_target_pairs={{0,4},{1,5},{2,6},{3,7},{4,0},{5,1},{6,2},{7,3},{8,12},{9,13},{10,... | collective-permute-start | bytes 132104 | tf_op jit(solution)/shard_map/ppermute | solution.py:368
  11.5 2.9 %collective-permute-start.3 = (bf16[4,16,344]{2,1,0:T(8,128)(2,1)S(1)}, bf16[4,16,344]{2,1,0:T(8,128)(2,1)S(1)}, u32[]{:S(2)}, u32[]{:S(2)}) collective-permute-start(bf16[4,16,344]{2,1,0:T(8,128)(2,1)S(1)} %pad_maximum_fusion), channel_id=1, source_target_pairs={{0,1},{1,0},{2,3},{3,2},{4,5},{5,4},{6,7},{7,6},{8,9},{9,8},{10,11... | collective-permute-start | bytes 132104 | tf_op jit(solution)/shard_map/ppermute | solution.py:368
  14.5 6.5 %copy-start = (bf16[16,16,344]{2,1,0:T(8,128)(2,1)}, bf16[16,16,344]{2,1,0:T(8,128)(2,1)S(1)}, u32[]{:S(2)}) copy-start(bf16[16,16,344]{2,1,0:T(8,128)(2,1)S(1)} %constant_dynamic-update-slice_fusion.refs_0_) | copy-start | bytes 528388
  14.5 6.4 %collective-permute-start.6 = (bf16[16,16,344]{2,1,0:T(8,128)(2,1)S(1)}, bf16[16,16,344]{2,1,0:T(8,128)(2,1)S(1)}, u32[]{:S(2)}, u32[]{:S(2)}) collective-permute-start(bf16[16,16,344]{2,1,0:T(8,128)(2,1)S(1)} %constant_dynamic-update-slice_fusion.refs_0_), channel_id=1, source_target_pairs={{0,2},{1,3},{2,0},{3,1},{4,6},{5,7},{6,4},{7,5},{8,10},{9,11},{10,... | collective-permute-start | bytes 528392 | tf_op jit(solution)/shard_map/ppermute | solution.py:368
  20.9 0.7 %copy-start.1 = (bf16[16,16,344]{2,1,0:T(8,128)(2,1)}, bf16[16,16,344]{2,1,0:T(8,128)(2,1)S(1)}, u32[]{:S(2)}) copy-start(bf16[16,16,344]{2,1,0:T(8,128)(2,1)S(1)} %collective-permute-done.6.refs_1_) | copy-start | bytes 528388
where the time goes:
time: 54 us; the launch traced here: 53.8 us
  Pallas kernels  32 us (59%)
  starting transfers between devices  11 us (20%)
  waiting for transfers between devices  5.83 us (11%)
  between operations  2.79 us (5%)
  other arithmetic  1.38 us (3%)
  local copies, waits for them, and re-layouts  0.74 us (1%)
    pallas_call x1, Pallas kernels, local_grads(): pl.pallas_call(functools.partial(grads_kernel, dims, offsets), out_shape=...  32 us
    ppermute x7, starting transfers between devices, exchange(): lax.ppermute(block, axes, [(source, source ^ d) for source in range(devic...  11 us
    ppermute x7, waiting for transfers between devices, exchange(): lax.ppermute(block, axes, [(source, source ^ d) for source in range(devic...  5.83 us
  transfers between devices with their start and end apart: 7, of which 3 were waited for; matrix products, arithmetic and copies ran while one was open for 1% of the time, Pallas kernels for 0%

commit v1 on v0

--- a/solution.py
+++ b/solution.py
@@ -12,7 +12,10 @@
 F32 = jnp.float32
 BF16 = jnp.bfloat16
 LANES = 128
-TILE = 1024
+UNIT = 512
+BACK_UNIT = 384
+DEPTH = 2
+STAGGER = 5
 
 
 def round_up(value, step):
@@ -66,6 +69,20 @@
 
 def dot_nt(a, b):
     return lax.dot_general(a, b, (((1,), (1,)), ((), ())), preferred_element_type=F32)
+
+
+def interleave(units):
+    waiting, running = list(units), []
+    turn = 0
+    while waiting or running:
+        if waiting and len(running) < DEPTH and turn % STAGGER == 0:
+            running.append(waiting.pop(0))
+        turn += 1
+        for unit in list(running):
+            try:
+                next(unit)
+            except StopIteration:
+                running.remove(unit)
 
 
 def grads_kernel(
@@ -97,7 +114,6 @@
     dw_buf,
     cand_dw_buf,
     down_buf,
-    up_tail,
     dw_pad,
     down_pad,
     act,
@@ -105,6 +121,7 @@
     slope_e,
     slope_k,
     x_first,
+    x_next,
     x_now,
     x_turned,
     err_now,
@@ -116,8 +133,6 @@
     sems,
     ) = refs
     maps, cells, channels, hid, taps, rows, parts, scale = dims
-    main = hid // TILE * TILE
-    tail = hid - main
     padded = round_up(hid, LANES)
     own = hid // parts
     window = wide_up.shape[1]
@@ -136,21 +151,14 @@
             for n, (src, dst) in enumerate(zip(sources, targets))
         ]
 
-    for slot in (0, 2):
+    for slot in (0, 2, 1):
         for copy in copies(slot):
-            copy.start()
-
-    @pl.when(layer_ref[0] != 0)
-    def _():
-        for copy in copies(1):
             copy.start()
 
     analysis = analysis_ref[...]
     even, odd = even_ref[...], odd_ref[...]
     spectrum = spectrum_ref[...]
     dw_pad[...] = jnp.zeros_like(dw_pad)
-    up_tail[...] = jnp.zeros_like(up_tail)
-    down_pad[:, main:] = jnp.zeros((channels, padded - main), BF16)
 
     half_cells = cells // 2
 
@@ -158,8 +166,8 @@
         same, other = dot(even, re.astype(BF16)), dot(odd, im.astype(BF16))
         return jnp.concatenate([same + other, same - other], axis=0)
 
-    def tap_spectrum(cols):
-        weights = dw_pad[:, cols]
+    def tap_spectrum(slot, cols):
+        weights = dw_pad[slot, :, cols]
         high = weights.astype(BF16)
         low = (weights - high.astype(F32)).astype(BF16)
         both = dot(spectrum, jnp.concatenate([high, low, high], axis=0))
@@ -177,45 +185,42 @@
             unit = lax.broadcasted_iota(jnp.int32, weights.shape, 1)
             keep = (ring <= radius_ref[0]) & (unit < half_ref[0] * (hid // 2))
             weights = jnp.where(keep, weights, 0.0)
-        dw_pad[:taps, :hid] = weights
-        if tail:
-            up_tail[:, :tail] = up_buf[slot, :, main:]
-            down_pad[:, main:hid] = down_buf[slot, :, main:]
-
-    def forward(slot, keep):
-        def tile(cols, weights_up):
-            pre = dot(x_now[...], weights_up)
-            half = 0.5 * pre
-            bend = jnp.tanh(half)
-            units = (half + half * bend).astype(BF16)
+        dw_pad[slot, :taps, :hid] = weights
+
+    def forward(slot, lhs, keep, lo, hi, results):
+        cols = slice(lo, hi)
+        pre = dot(lhs[...], up_buf[slot, :, cols])
+        yield
+        half = 0.5 * pre
+        bend = jnp.tanh(half)
+        units = (half + half * bend).astype(BF16)
+        if keep:
+            slope_e[:, cols] = (0.5 * ((1.0 + bend) + half * (1.0 - bend * bend))).astype(BF16)
+        yield
+        tap_re, tap_im = tap_spectrum(slot, cols)
+        acts = []
+        for m in range(maps):
+            here = slice(m * cells, (m + 1) * cells)
+            both = dot(analysis, units[here])
+            yield
+            re, im = both[:rows], both[rows:]
             if keep:
-                slope_e[:, cols] = (0.5 * ((1.0 + bend) + half * (1.0 - bend * bend))).astype(BF16)
-            tap_re, tap_im = tap_spectrum(cols)
-            for m in range(maps):
-                here = slice(m * cells, (m + 1) * cells)
-                both = dot(analysis, units[here])
-                re, im = both[:rows], both[rows:]
-                if keep:
-                    spec[m, :, cols] = both.astype(BF16)
-                mixed = synthesis(re * tap_re - im * tap_im, re * tap_im + im * tap_re)
-                half_k = 0.5 * mixed
-                bend_k = jnp.tanh(half_k)
-                act[here, cols] = (half_k + half_k * bend_k).astype(BF16)
-                if keep:
-                    slope_k[here, cols] = (0.5 * ((1.0 + bend_k) + half_k * (1.0 - bend_k * bend_k))).astype(BF16)
-
-        def step(n, _):
-            cols = pl.ds(pl.multiple_of(n * TILE, TILE), TILE)
-            tile(cols, up_buf[slot, :, cols])
-            return 0
-
-        lax.fori_loop(0, main // TILE, step, 0)
-        if tail:
-            tile(pl.ds(main, padded - main), up_tail[...])
-        out = dot_nt(act[:, :main], down_buf[slot, :, :main])
-        if tail:
-            out += dot_nt(act[:, main:], down_pad[:, main:])
-        return out
+                spec[m, :, cols] = both.astype(BF16)
+            mixed_re, mixed_im = re * tap_re - im * tap_im, re * tap_im + im * tap_re
+            yield
+            mixed = synthesis(mixed_re, mixed_im)
+            yield
+            half_k = 0.5 * mixed
+            bend_k = jnp.tanh(half_k)
+            acts.append((half_k + half_k * bend_k).astype(BF16))
+            if keep:
+                act[here, cols] = acts[-1]
+                slope_k[here, cols] = (0.5 * ((1.0 + bend_k) + half_k * (1.0 - bend_k * bend_k))).astype(BF16)
+        yield
+        results.append(dot_nt(jnp.concatenate(acts, axis=0), down_buf[slot, :, cols]))
+
+    bounds = list(range(0, max(hid - UNIT // 2, 1), UNIT)) + [hid]
+    spans = list(zip(bounds, bounds[1:]))
 
     whole_turn = (
         lax.broadcasted_iota(jnp.int32, (half_cells, half_cells), 0)
@@ -235,19 +240,23 @@
     for m in range(maps):
         second = slice(m * cells + half_cells, (m + 1) * cells)
         x_first[second] = dot(turn_half, x_first[second]).astype(BF16)
-    x_now[...] = x_first[...]
     load(0, False)
-    target[...] = forward(0, False)
-
-    @pl.when(layer_ref[0] != 0)
-    def _():
-        x_now[...] = (x_first[...].astype(F32) + target[...]).astype(BF16)
-        load(1, False)
-        target[...] = forward(1, False)
-
+    first = []
+    interleave([forward(0, x_first, False, lo, hi, first) for lo, hi in spans])
+    branch = sum(first)
+    x_next[...] = (x_first[...].astype(F32) + branch).astype(BF16)
+    x_now[...] = jnp.where(layer_ref[0] == 0, x_first[...], x_next[...])
+    target[...] = branch
     load(2, True)
-    down_pad[:, :main] = down_buf[2, :, :main]
-    err = (forward(2, True) - target[...]) * scale
+    load(1, False)
+    second, third = [], []
+    units = []
+    for lo, hi in spans:
+        units.append(forward(1, x_next, False, lo, hi, second))
+        units.append(forward(2, x_now, True, lo, hi, third))
+    interleave(units)
+    down_pad[:, :hid] = down_buf[2]
+    err = (sum(third) - jnp.where(layer_ref[0] == 0, target[...], sum(second))) * scale
     err_now[...] = err.astype(BF16)
     err_turned[...] = jnp.transpose(err).astype(BF16)
     x_turned[...] = jnp.transpose(x_now[...].astype(F32)).astype(BF16)
@@ -257,35 +266,35 @@
 
     def back(at, width):
         cols = pl.ds(pl.multiple_of(base + at, LANES), width)
-        here = pl.ds(pl.multiple_of(at, LANES), width)
+        here = slice(at, at + width)
         grad_act = dot(err_now[...], down_pad[:, cols])
+        wide_down[:, here] = dot(err_turned[...], act[:, cols])
+        yield
         grad_k = (grad_act * slope_k[:, cols].astype(F32)).astype(BF16)
-        tap_re, tap_im = tap_spectrum(cols)
-        sum_re = jnp.zeros((rows, width), F32)
-        sum_im = jnp.zeros((rows, width), F32)
+        yield
+        tap_re, tap_im = tap_spectrum(2, cols)
+        sum_re = sum_im = 0.0
         grad_pre = []
         for m in range(maps):
             rows_here = slice(m * cells, (m + 1) * cells)
             both = dot(analysis, grad_k[rows_here])
+            yield
             re, im = both[:rows], both[rows:]
             kept = spec[m, :, cols].astype(F32)
             e_re, e_im = kept[:rows], kept[rows:]
             sum_re += re * e_re + im * e_im
             sum_im += re * e_im - im * e_re
-            grad_e = synthesis(re * tap_re + im * tap_im, im * tap_re - re * tap_im)
+            mixed_re, mixed_im = re * tap_re + im * tap_im, im * tap_re - re * tap_im
+            yield
+            grad_e = synthesis(mixed_re, mixed_im)
+            yield
             grad_pre.append((grad_e * slope_e[rows_here, cols].astype(F32)).astype(BF16))
+        yield
         wide_up[:, here] = dot(x_turned[...], jnp.concatenate(grad_pre, axis=0))
-        wide_down[:, here] = dot(err_turned[...], act[:, cols])
         sums = jnp.concatenate([sum_re, sum_im], axis=0).astype(BF16)
         wide_dw[:, here] = dot(gather_ref[...], sums)
 
-    def back_step(n, _):
-        back(n * TILE, TILE)
-        return 0
-
-    lax.fori_loop(0, window // TILE, back_step, 0)
-    if window % TILE:
-        back(window // TILE * TILE, window % TILE)
+    interleave([back(at, min(BACK_UNIT, window - at)) for at in range(0, window, BACK_UNIT)])
 
     offset = start - base
     turn = lax.rem(window - offset, window)
@@ -315,7 +324,6 @@
     spare = max((p * own) % LANES for p in range(parts))
     window = min(round_up(own + spare, LANES), padded)
     tap_rows = round_up(taps, 16)
-    main = hid // TILE * TILE
     dims = (maps, cells, channels, hid, taps, rows, parts, 1.0 / images)
     smem = pl.BlockSpec(memory_space=pltpu.SMEM)
     vmem = pl.BlockSpec(memory_space=pltpu.VMEM)
@@ -334,13 +342,13 @@
             pltpu.VMEM(weights[1].shape, F32),
             pltpu.VMEM(weights[4].shape, F32),
             pltpu.VMEM((3, channels, hid), BF16),
-            pltpu.VMEM((channels, max(padded - main, LANES)), BF16),
-            pltpu.VMEM((tap_rows, padded), F32),
+            pltpu.VMEM((3, tap_rows, padded), F32),
             pltpu.VMEM((channels, padded), BF16),
             pltpu.VMEM((count, padded), BF16),
             pltpu.VMEM((maps, 2 * rows, padded), BF16),
             pltpu.VMEM((count, padded), BF16),
             pltpu.VMEM((count, padded), BF16),
+            pltpu.VMEM((count, channels), BF16),
             pltpu.VMEM((count, channels), BF16),
             pltpu.VMEM((count, channels), BF16),
             pltpu.VMEM((channels, count), BF16),

time: 54 us -> 49.5 us (0.917)
  Pallas kernels: 32 us -> 27.5 us
    pallas_call x1, Pallas kernels: 32 us -> 27.5 us  [local_grads(): pl.pallas_call(functools.partial(grads_kernel, dims, offsets), out_shape=...]
where the time goes in v1:
time: 49.5 us; the launch traced here: 49.3 us
  Pallas kernels  27.5 us (56%)
  starting transfers between devices  11 us (22%)
  waiting for transfers between devices  5.83 us (12%)
  between operations  2.79 us (6%)
  other arithmetic  1.38 us (3%)
  local copies, waits for them, and re-layouts  0.74 us (1%)
    pallas_call x1, Pallas kernels, local_grads(): pl.pallas_call(functools.partial(grads_kernel, dims, offsets), out_shape=...  27.5 us
    ppermute x7, starting transfers between devices, exchange(): lax.ppermute(block, axes, [(source, source ^ d) for source in range(devic...  11 us
    ppermute x7, waiting for transfers between devices, exchange(): lax.ppermute(block, axes, [(source, source ^ d) for source in range(devic...  5.83 us
  transfers between devices with their start and end apart: 7, of which 3 were waited for; matrix products, arithmetic and copies ran while one was open for 1% of the time, Pallas kernels for 0%

profile of v1, /device:TPU:1, one launch (start us, length us, event | category | flops | bytes accessed | tf_op | source)
XLA Modules:
  0.0 49.3 jit_solution(476417897333051196)
XLA Ops:
  0.6 0.7 %constant_dynamic-update-slice_fusion.6 = (bf16[16,16,344]{2,1,0:T(8,128)(2,1)S(1)}, bf16[1,16,344]{2,1,0:T(8,128)(2,1)S(1)}) fusion(f32[1,16,344]{2,1,0:T(8,128)} %param.15), kind=kLoop, calls=%fused_computation.7 | loop fusion | flops 5503 | bytes 46592
  1.4 4.2 %collective-permute-start.2 = (bf16[1,16,344]{2,1,0:T(8,128)(2,1)S(1)}, bf16[1,16,344]{2,1,0:T(8,128)(2,1)S(1)}, u32[]{:S(2)}, u32[]{:S(2)}) collective-permute-start(bf16[1,16,344]{2,1,0:T(8,128)(2,1)S(1)} %get-tuple-element.10), channel_id=1, source_target_pairs={{0,24},{1,25},{2,26},{3,27},{4,28},{5,29},{6,30},{7,31},{8,16},{9,... | collective-permute-start | bytes 33032 | tf_op jit(solution)/shard_map/ppermute | solution.py:376
  5.5 0.0 collective-permute-start.1
  5.5 0.3 collective-permute-start
  5.8 0.8 %collective-permute-done.2 = bf16[1,16,344]{2,1,0:T(8,128)(2,1)S(1)} collective-permute-done((bf16[1,16,344]{2,1,0:T(8,128)(2,1)S(1)}, bf16[1,16,344]{2,1,0:T(8,128)(2,1)S(1)}, u32[]{:S(2)}, u32[]{:S(2)}) %collective-permute-start.2) | collective-permute-done | bytes 11040 | tf_op jit(solution)/shard_map/ppermute | solution.py:376
  6.6 2.4 %collective-permute-done.1 = bf16[1,16,344]{2,1,0:T(8,128)(2,1)S(1)} collective-permute-done((bf16[1,16,344]{2,1,0:T(8,128)(2,1)S(1)}, bf16[1,16,344]{2,1,0:T(8,128)(2,1)S(1)}, u32[]{:S(2)}, u32[]{:S(2)}) %collective-permute-start.1) | collective-permute-done | bytes 11040 | tf_op jit(solution)/shard_map/ppermute | solution.py:376
  9.0 0.0 collective-permute-done
  9.0 2.2 %collective-permute-start.5 = (bf16[4,16,344]{2,1,0:T(8,128)(2,1)S(1)}, bf16[4,16,344]{2,1,0:T(8,128)(2,1)S(1)}, u32[]{:S(2)}, u32[]{:S(2)}) collective-permute-start(bf16[4,16,344]{2,1,0:T(8,128)(2,1)S(1)} %pad_maximum_fusion), channel_id=1, source_target_pairs={{0,5},{1,4},{2,7},{3,6},{4,1},{5,0},{6,3},{7,2},{8,13},{9,12},{10,... | collective-permute-start | bytes 132104 | tf_op jit(solution)/shard_map/ppermute | solution.py:376
  11.2 0.2 collective-permute-start.4
  11.5 0.3 collective-permute-start.3
  11.7 2.7 %collective-permute-done.3 = bf16[4,16,344]{2,1,0:T(8,128)(2,1)S(1)} collective-permute-done((bf16[4,16,344]{2,1,0:T(8,128)(2,1)S(1)}, bf16[4,16,344]{2,1,0:T(8,128)(2,1)S(1)}, u32[]{:S(2)}, u32[]{:S(2)}) %collective-permute-start.3) | collective-permute-done | bytes 44064 | tf_op jit(solution)/shard_map/ppermute | solution.py:376
  14.4 0.0 collective-permute-done.4
  14.4 0.0 collective-permute-done.5
  14.5 0.0 copy-start
  14.5 3.9 %collective-permute-start.6 = (bf16[16,16,344]{2,1,0:T(8,128)(2,1)S(1)}, bf16[16,16,344]{2,1,0:T(8,128)(2,1)S(1)}, u32[]{:S(2)}, u32[]{:S(2)}) collective-permute-start(bf16[16,16,344]{2,1,0:T(8,128)(2,1)S(1)} %constant_dynamic-update-slice_fusion.refs_0_), channel_id=1, source_target_pairs={{0,2},{1,3},{2,0},{3,1},{4,6},{5,7},{6,4},{7,5},{8,10},{9,11},{10,... | collective-permute-start | bytes 528392 | tf_op jit(solution)/shard_map/ppermute | solution.py:376
  20.3 0.6 %pad_add_fusion.place_ref = s32[2]{0:T(128)} fusion(s32[1]{0:T(128)} %bitcast.1, s32[1]{0:T(128)} %bitcast), kind=kLoop, calls=%fused_computation.8 | loop fusion | flops 2 | bytes 16 | tf_op jit(solution)/shard_map/stack | solution.py:403
  20.9 0.0 collective-permute-done.6.refs_1_
  20.9 0.0 copy-start.1
  20.9 0.0 copy-done
  20.9 0.7 %copy-done.1 = bf16[16,16,344]{2,1,0:T(8,128)(2,1)} copy-done((bf16[16,16,344]{2,1,0:T(8,128)(2,1)}, bf16[16,16,344]{2,1,0:T(8,128)(2,1)S(1)}, u32[]{:S(2)}) %copy-start.1) | copy-done | bytes 176152
  21.6 27.5 %shard_map.166 = (f32[1,344,1032]{2,1,0:T(8,128)}, f32[25,1,1032]{2,1,0:T(1,128)}, f32[1,344,1032]{2,1,0:T(8,128)}) custom-call(s32[1]{0:T(128)S(6)} %copy.24.layer_ref, s32[1]{0:T(128)S(6)} %copy.25.half_ref, s32[1]{0:T(128)S(6)} %copy.26.radius_ref, s32[2]{0:T(128)} %pad_add_fusion.place_ref, bf16[16,16,344]{2,1,0:T(8,128)(2,1)} %copy-done, ...), custom_call_target="tpu_custom_call" | custom-call | flops 7270563840 | bytes 8520192 | tf_op jit(solution)/shard_map/pallas_call | solution.py:331
  (7 shorter events, 0.1 us)
Async XLA Ops:
  1.4 5.2 %collective-permute-start.2 = (bf16[1,16,344]{2,1,0:T(8,128)(2,1)S(1)}, bf16[1,16,344]{2,1,0:T(8,128)(2,1)S(1)}, u32[]{:S(2)}, u32[]{:S(2)}) collective-permute-start(bf16[1,16,344]{2,1,0:T(8,128)(2,1)S(1)} %get-tuple-element.10), channel_id=1, source_target_pairs={{0,24},{1,25},{2,26},{3,27},{4,28},{5,29},{6,30},{7,31},{8,16},{9,... | collective-permute-start | bytes 33032 | tf_op jit(solution)/shard_map/ppermute | solution.py:376
  5.5 3.4 %collective-permute-start.1 = (bf16[1,16,344]{2,1,0:T(8,128)(2,1)S(1)}, bf16[1,16,344]{2,1,0:T(8,128)(2,1)S(1)}, u32[]{:S(2)}, u32[]{:S(2)}) collective-permute-start(bf16[1,16,344]{2,1,0:T(8,128)(2,1)S(1)} %get-tuple-element.10), channel_id=1, source_target_pairs={{0,16},{1,17},{2,18},{3,19},{4,20},{5,21},{6,22},{7,23},{8,24},{9,... | collective-permute-start | bytes 33032 | tf_op jit(solution)/shard_map/ppermute | solution.py:376
  5.5 3.4 %collective-permute-start = (bf16[1,16,344]{2,1,0:T(8,128)(2,1)S(1)}, bf16[1,16,344]{2,1,0:T(8,128)(2,1)S(1)}, u32[]{:S(2)}, u32[]{:S(2)}) collective-permute-start(bf16[1,16,344]{2,1,0:T(8,128)(2,1)S(1)} %get-tuple-element.10), channel_id=1, source_target_pairs={{0,8},{1,9},{2,10},{3,11},{4,12},{5,13},{6,14},{7,15},{8,0},{9,1},... | collective-permute-start | bytes 33032 | tf_op jit(solution)/shard_map/ppermute | solution.py:376
  9.0 5.4 %collective-permute-start.5 = (bf16[4,16,344]{2,1,0:T(8,128)(2,1)S(1)}, bf16[4,16,344]{2,1,0:T(8,128)(2,1)S(1)}, u32[]{:S(2)}, u32[]{:S(2)}) collective-permute-start(bf16[4,16,344]{2,1,0:T(8,128)(2,1)S(1)} %pad_maximum_fusion), channel_id=1, source_target_pairs={{0,5},{1,4},{2,7},{3,6},{4,1},{5,0},{6,3},{7,2},{8,13},{9,12},{10,... | collective-permute-start | bytes 132104 | tf_op jit(solution)/shard_map/ppermute | solution.py:376
  11.2 3.2 %collective-permute-start.4 = (bf16[4,16,344]{2,1,0:T(8,128)(2,1)S(1)}, bf16[4,16,344]{2,1,0:T(8,128)(2,1)S(1)}, u32[]{:S(2)}, u32[]{:S(2)}) collective-permute-start(bf16[4,16,344]{2,1,0:T(8,128)(2,1)S(1)} %pad_maximum_fusion), channel_id=1, source_target_pairs={{0,4},{1,5},{2,6},{3,7},{4,0},{5,1},{6,2},{7,3},{8,12},{9,13},{10,... | collective-permute-start | bytes 132104 | tf_op jit(solution)/shard_map/ppermute | solution.py:376
  11.5 2.9 %collective-permute-start.3 = (bf16[4,16,344]{2,1,0:T(8,128)(2,1)S(1)}, bf16[4,16,344]{2,1,0:T(8,128)(2,1)S(1)}, u32[]{:S(2)}, u32[]{:S(2)}) collective-permute-start(bf16[4,16,344]{2,1,0:T(8,128)(2,1)S(1)} %pad_maximum_fusion), channel_id=1, source_target_pairs={{0,1},{1,0},{2,3},{3,2},{4,5},{5,4},{6,7},{7,6},{8,9},{9,8},{10,11... | collective-permute-start | bytes 132104 | tf_op jit(solution)/shard_map/ppermute | solution.py:376
  14.5 6.5 %copy-start = (bf16[16,16,344]{2,1,0:T(8,128)(2,1)}, bf16[16,16,344]{2,1,0:T(8,128)(2,1)S(1)}, u32[]{:S(2)}) copy-start(bf16[16,16,344]{2,1,0:T(8,128)(2,1)S(1)} %constant_dynamic-update-slice_fusion.refs_0_) | copy-start | bytes 528388
  14.5 6.4 %collective-permute-start.6 = (bf16[16,16,344]{2,1,0:T(8,128)(2,1)S(1)}, bf16[16,16,344]{2,1,0:T(8,128)(2,1)S(1)}, u32[]{:S(2)}, u32[]{:S(2)}) collective-permute-start(bf16[16,16,344]{2,1,0:T(8,128)(2,1)S(1)} %constant_dynamic-update-slice_fusion.refs_0_), channel_id=1, source_target_pairs={{0,2},{1,3},{2,0},{3,1},{4,6},{5,7},{6,4},{7,5},{8,10},{9,11},{10,... | collective-permute-start | bytes 528392 | tf_op jit(solution)/shard_map/ppermute | solution.py:376
  20.9 0.7 %copy-start.1 = (bf16[16,16,344]{2,1,0:T(8,128)(2,1)}, bf16[16,16,344]{2,1,0:T(8,128)(2,1)S(1)}, u32[]{:S(2)}) copy-start(bf16[16,16,344]{2,1,0:T(8,128)(2,1)S(1)} %collective-permute-done.6.refs_1_) | copy-start | bytes 528388

commit v2 on v1

--- a/solution.py
+++ b/solution.py
@@ -1,4 +1,5 @@
 import functools
+import itertools
 
 import jax
 import jax.numpy as jnp
@@ -115,6 +116,7 @@
     cand_dw_buf,
     down_buf,
     dw_pad,
+    up_pad,
     down_pad,
     act,
     spec,
@@ -161,6 +163,9 @@
     dw_pad[...] = jnp.zeros_like(dw_pad)
 
     half_cells = cells // 2
+    bases = [min(p * own // LANES * LANES, padded - window) for p in range(parts)]
+    start = place_ref[1] * own
+    base = jnp.minimum(start // LANES * LANES, padded - window)
 
     def synthesis(re, im):
         same, other = dot(even, re.astype(BF16)), dot(odd, im.astype(BF16))
@@ -187,15 +192,17 @@
             weights = jnp.where(keep, weights, 0.0)
         dw_pad[slot, :taps, :hid] = weights
 
-    def forward(slot, lhs, keep, lo, hi, results):
-        cols = slice(lo, hi)
-        pre = dot(lhs[...], up_buf[slot, :, cols])
+    def forward(slot, lhs, up, down, cols, save, results):
+        keep = save is not None
+        pre = dot(lhs[...], up[:, cols])
         yield
         half = 0.5 * pre
         bend = jnp.tanh(half)
-        units = (half + half * bend).astype(BF16)
+        more = 1.0 + bend
+        wide = half * more
+        units = wide.astype(BF16)
         if keep:
-            slope_e[:, cols] = (0.5 * ((1.0 + bend) + half * (1.0 - bend * bend))).astype(BF16)
+            slope_e[:, save] = (more + wide - wide * bend).astype(BF16)
         yield
         tap_re, tap_im = tap_spectrum(slot, cols)
         acts = []
@@ -205,22 +212,43 @@
             yield
             re, im = both[:rows], both[rows:]
             if keep:
-                spec[m, :, cols] = both.astype(BF16)
+                spec[m, :, save] = both.astype(BF16)
             mixed_re, mixed_im = re * tap_re - im * tap_im, re * tap_im + im * tap_re
             yield
             mixed = synthesis(mixed_re, mixed_im)
             yield
             half_k = 0.5 * mixed
             bend_k = jnp.tanh(half_k)
-            acts.append((half_k + half_k * bend_k).astype(BF16))
+            more_k = 1.0 + bend_k
+            wide_k = half_k * more_k
+            acts.append(wide_k.astype(BF16))
             if keep:
-                act[here, cols] = acts[-1]
-                slope_k[here, cols] = (0.5 * ((1.0 + bend_k) + half_k * (1.0 - bend_k * bend_k))).astype(BF16)
-        yield
-        results.append(dot_nt(jnp.concatenate(acts, axis=0), down_buf[slot, :, cols]))
-
-    bounds = list(range(0, max(hid - UNIT // 2, 1), UNIT)) + [hid]
-    spans = list(zip(bounds, bounds[1:]))
+                act[here, save] = acts[-1]
+                slope_k[here, save] = (more_k + wide_k - wide_k * bend_k).astype(BF16)
+        yield
+        results.append(dot_nt(jnp.concatenate(acts, axis=0), down[:, cols]))
+
+    def teacher(slot, lhs, results):
+        bounds = list(range(0, max(hid - UNIT // 2, 1), UNIT)) + [hid]
+        return [
+            forward(slot, lhs, up_buf.at[slot], down_buf.at[slot], slice(lo, hi), None, results)
+            for lo, hi in zip(bounds, bounds[1:])
+        ]
+
+    def aligned(at, width):
+        return pl.ds(pl.multiple_of(at, LANES), width)
+
+    def candidate(lhs, results):
+        units = []
+        for at in range(0, window, BACK_UNIT):
+            width = min(BACK_UNIT, window - at)
+            cols = aligned(base + at, width)
+            units.append(forward(2, lhs, up_pad, down_pad, cols, slice(at, at + width), results))
+        step = max(w for w in (LANES, 2 * LANES, UNIT) if all(b % w == 0 for b in bases))
+        for at in range(0, padded - window, step):
+            cols = aligned(jnp.where(at < base, at, at + window), min(step, padded - window - at))
+            units.append(forward(2, lhs, up_pad, down_pad, cols, None, results))
+        return units
 
     whole_turn = (
         lax.broadcasted_iota(jnp.int32, (half_cells, half_cells), 0)
@@ -232,8 +260,8 @@
             x_first[...] = x_ref[...]
             continue
         block = x_ref.shape[1]
-        for n, distance in enumerate(offset):
-            source = place_ref[0] ^ distance
+        for n, (mask, distance) in enumerate(offset):
+            source = (place_ref[0] & mask) ^ distance
             source = (source & (parts - 1)) * (cells // block) + (source >> (parts.bit_length() - 1))
             at = pl.multiple_of(source * block, block)
             x_first[pl.ds(at, block), :] = x_ref[n]
@@ -242,35 +270,31 @@
         x_first[second] = dot(turn_half, x_first[second]).astype(BF16)
     load(0, False)
     first = []
-    interleave([forward(0, x_first, False, lo, hi, first) for lo, hi in spans])
+    interleave(teacher(0, x_first, first))
     branch = sum(first)
     x_next[...] = (x_first[...].astype(F32) + branch).astype(BF16)
     x_now[...] = jnp.where(layer_ref[0] == 0, x_first[...], x_next[...])
     target[...] = branch
     load(2, True)
     load(1, False)
+    for pad, buf in ((up_pad, up_buf), (down_pad, down_buf)):
+        pad[:, hid // LANES * LANES :] = jnp.zeros((channels, padded - hid // LANES * LANES), BF16)
+        pad[:, :hid] = buf[2]
     second, third = [], []
-    units = []
-    for lo, hi in spans:
-        units.append(forward(1, x_next, False, lo, hi, second))
-        units.append(forward(2, x_now, True, lo, hi, third))
-    interleave(units)
-    down_pad[:, :hid] = down_buf[2]
+    units = [teacher(1, x_next, second), candidate(x_now, third)]
+    interleave([unit for pair in itertools.zip_longest(*units) for unit in pair if unit is not None])
     err = (sum(third) - jnp.where(layer_ref[0] == 0, target[...], sum(second))) * scale
-    err_now[...] = err.astype(BF16)
+    err_now[...] = (0.5 * err).astype(BF16)
     err_turned[...] = jnp.transpose(err).astype(BF16)
-    x_turned[...] = jnp.transpose(x_now[...].astype(F32)).astype(BF16)
-
-    start = place_ref[1] * own
-    base = jnp.minimum(start // LANES * LANES, padded - window)
+    x_turned[...] = jnp.transpose(0.5 * x_now[...].astype(F32)).astype(BF16)
 
     def back(at, width):
-        cols = pl.ds(pl.multiple_of(base + at, LANES), width)
+        cols = aligned(base + at, width)
         here = slice(at, at + width)
         grad_act = dot(err_now[...], down_pad[:, cols])
-        wide_down[:, here] = dot(err_turned[...], act[:, cols])
-        yield
-        grad_k = (grad_act * slope_k[:, cols].astype(F32)).astype(BF16)
+        wide_down[:, here] = dot(err_turned[...], act[:, here])
+        yield
+        grad_k = (grad_act * slope_k[:, here].astype(F32)).astype(BF16)
         yield
         tap_re, tap_im = tap_spectrum(2, cols)
         sum_re = sum_im = 0.0
@@ -280,7 +304,7 @@
             both = dot(analysis, grad_k[rows_here])
             yield
             re, im = both[:rows], both[rows:]
-            kept = spec[m, :, cols].astype(F32)
+            kept = spec[m, :, here].astype(F32)
             e_re, e_im = kept[:rows], kept[rows:]
             sum_re += re * e_re + im * e_im
             sum_im += re * e_im - im * e_re
@@ -288,7 +312,7 @@
             yield
             grad_e = synthesis(mixed_re, mixed_im)
             yield
-            grad_pre.append((grad_e * slope_e[rows_here, cols].astype(F32)).astype(BF16))
+            grad_pre.append((grad_e * slope_e[rows_here, here].astype(F32)).astype(BF16))
         yield
         wide_up[:, here] = dot(x_turned[...], jnp.concatenate(grad_pre, axis=0))
         sums = jnp.concatenate([sum_re, sum_im], axis=0).astype(BF16)
@@ -344,10 +368,11 @@
             pltpu.VMEM((3, channels, hid), BF16),
             pltpu.VMEM((3, tap_rows, padded), F32),
             pltpu.VMEM((channels, padded), BF16),
-            pltpu.VMEM((count, padded), BF16),
-            pltpu.VMEM((maps, 2 * rows, padded), BF16),
-            pltpu.VMEM((count, padded), BF16),
-            pltpu.VMEM((count, padded), BF16),
+            pltpu.VMEM((channels, padded), BF16),
+            pltpu.VMEM((count, window), BF16),
+            pltpu.VMEM((maps, 2 * rows, window), BF16),
+            pltpu.VMEM((count, window), BF16),
+            pltpu.VMEM((count, window), BF16),
             pltpu.VMEM((count, channels), BF16),
             pltpu.VMEM((count, channels), BF16),
             pltpu.VMEM((count, channels), BF16),
@@ -360,7 +385,7 @@
             pltpu.VMEM((channels, window), F32),
             pltpu.SemaphoreType.DMA((3, 3)),
         ],
-        compiler_params=pltpu.CompilerParams(vmem_limit_bytes=60 * 2**20),
+        compiler_params=pltpu.CompilerParams(vmem_limit_bytes=40 * 2**20),
         cost_estimate=pl.CostEstimate(
             flops=20 * count * channels * hid, bytes_accessed=12 * channels * hid, transcendentals=6 * count * hid
         ),
@@ -368,18 +393,14 @@
     return grad_up, grad_dw.transpose(1, 0, 2), grad_down
 
 
-def exchange(block, masks, axes, devices):
-    offset = [0]
-    for mask in masks:
-        distances = [d for d in range(1, devices) if d & ~mask == 0]
-        parts = [block] + [
-            lax.ppermute(block, axes, [(source, source ^ d) for source in range(devices)]) for d in distances
-        ]
-        pieces = [[o ^ d for o in offset] for d in [0] + distances]
-        offset = sum(pieces, [])
-        if mask != masks[-1]:
-            block = jnp.concatenate(parts, axis=0)
-    return parts, pieces
+def spread(block, cands, parts):
+    sent = jnp.broadcast_to(block, (cands, *block.shape[1:]))
+    image = lax.all_to_all(sent, "cand", split_axis=0, concat_axis=0, tiled=True)
+    pieces, offsets = [image], [[(parts - 1, c * parts) for c in range(cands)]]
+    for d in range(1, parts):
+        pieces.append(lax.ppermute(image, "img", [(source, source ^ d) for source in range(parts)]))
+        offsets.append([(parts - 1, c * parts + d) for c in range(cands)])
+    return pieces, offsets
 
 
 def body(
@@ -405,10 +426,7 @@
     scalars = (layer_of, expand_half, radius, place, parts, images, weights)
     mine = first_maps.astype(BF16)
     if batch == 1 and images == 2 and own_cells % 16 == 0 and devices & (devices - 1) == 0:
-        low = min(2, cands) - 1
-        low, near = low * parts, (parts - 1) | (low * parts * 2)
-        masks = [(devices - 1) & ~near & ~low, near, low]
-        pieces, offsets = exchange(mine, masks, ("cand", "img"), devices)
+        pieces, offsets = spread(mine, cands, parts)
         return local_grads(pieces, offsets, images, *scalars)
     whole = lax.all_gather(mine, ("img", "cand")).reshape(parts, cands, batch, own_cells, channels)
     whole = whole.transpose(0, 2, 1, 3, 4).reshape(images, -1, channels)

time: 49.5 us -> 64.1 us (1.29)
  the two profiles are of different devices: /device:TPU:1 before, /device:TPU:0 now
where the time goes in v2:
time: 64.1 us; the launch traced here: 63.5 us
  Pallas kernels  26.6 us (41%)
  blocking collectives  16.2 us (25%)
  local copies, waits for them, and re-layouts  12.6 us (20%)
  waiting for transfers between devices  3.03 us (5%)
  between operations  2.75 us (4%)
  starting transfers between devices  1.49 us (2%)
  other arithmetic  0.82 us (1%)
    pallas_call x1, Pallas kernels, local_grads(): pl.pallas_call(functools.partial(grads_kernel, dims, offsets), out_shape=...  26.6 us
    all_to_all x1, blocking collectives, spread(): lax.all_to_all(sent, 'cand', split_axis=0, concat_axis=0, tiled=True)  16.2 us
    unnamed x22, local copies, waits for them, and re-layouts  12.6 us
    ppermute x1, waiting for transfers between devices, spread(): lax.ppermute(image, 'img', [(source, source ^ d) for source in range(part...  3.03 us
    ppermute x1, starting transfers between devices, spread(): lax.ppermute(image, 'img', [(source, source ^ d) for source in range(part...  1.49 us
  transfers between devices with their start and end apart: 1, of which 1 were waited for; matrix products, arithmetic and copies ran while one was open for 0% of the time, Pallas kernels for 0%

profile of v2, /device:TPU:0, one launch (start us, length us, event | category | flops | bytes accessed | tf_op | source)
XLA Modules:
  0.0 63.5 jit_solution(15680494197082021932)
XLA Ops:
  0.6 0.7 %convert_bitcast_fusion = bf16[16,344]{1,0:T(8,128)(2,1)S(1)} fusion(f32[1,16,344]{2,1,0:T(8,128)} %param.15), kind=kLoop, calls=%fused_computation | loop fusion | flops 5504 | bytes 33024 | tf_op jit(solution)/shard_map/broadcast_in_dim | solution.py:397
  1.4 16.2 %all_to_all.5.refs_0_ = bf16[16,16,344]{2,1,0:T(8,128)(2,1)S(1)} all-to-all(bf16[16,16,344]{2,1,0:T(8,128)(2,1)S(1)} %broadcast_in_dim.8), channel_id=1, replica_groups=mesh['cand'=16,'img'=2] {'cand'}, dimensions={0} | all-to-all | bytes 352256 | tf_op jit(solution)/shard_map/all_to_all | solution.py:398
  17.6 1.5 %collective-permute-start = (bf16[16,16,344]{2,1,0:T(8,128)(2,1)S(1)}, bf16[16,16,344]{2,1,0:T(8,128)(2,1)S(1)}, u32[]{:S(2)}, u32[]{:S(2)}) collective-permute-start(bf16[16,16,344]{2,1,0:T(8,128)(2,1)S(1)} %all_to_all.5.refs_0_), channel_id=1, source_target_pairs={{0,1},{1,0},{2,3},{3,2},{4,5},{5,4},{6,7},{7,6},{8,9},{9,8},{10,11... | collective-permute-start | bytes 528392 | tf_op jit(solution)/shard_map/ppermute | solution.py:401
  21.0 0.1 pad_add_fusion.place_ref
  21.1 3.0 %collective-permute-done.refs_1_ = bf16[16,16,344]{2,1,0:T(8,128)(2,1)S(1)} collective-permute-done((bf16[16,16,344]{2,1,0:T(8,128)(2,1)S(1)}, bf16[16,16,344]{2,1,0:T(8,128)(2,1)S(1)}, u32[]{:S(2)}, u32[]{:S(2)}) %collective-permute-start) | collective-permute-done | bytes 176160 | tf_op jit(solution)/shard_map/ppermute | solution.py:401
  24.1 0.0 copy-start
  24.1 1.8 %copy-done = bf16[2,344,2064]{2,1,0:T(8,128)(2,1)S(1)} copy-done((bf16[2,344,2064]{2,1,0:T(8,128)(2,1)S(1)}, bf16[2,344,2064]{2,1,0:T(8,128)(2,1)}, u32[]{:S(2)}) %copy-start) | copy-done | bytes 2840088
  26.0 0.0 copy-start.1
  26.0 1.8 %copy-done.1 = bf16[2,344,2064]{2,1,0:T(8,128)(2,1)S(1)} copy-done((bf16[2,344,2064]{2,1,0:T(8,128)(2,1)S(1)}, bf16[2,344,2064]{2,1,0:T(8,128)(2,1)}, u32[]{:S(2)}) %copy-start.1) | copy-done | bytes 2840088
  27.8 0.0 copy-start.2
  27.8 1.4 %copy-done.2 = bf16[1,344,2064]{2,1,0:T(8,128)(2,1)S(1)} copy-done((bf16[1,344,2064]{2,1,0:T(8,128)(2,1)S(1)}, bf16[1,344,2064]{2,1,0:T(8,128)(2,1)}, u32[]{:S(2)}) %copy-start.2) | copy-done | bytes 1420056
  29.2 0.0 copy-start.3
  29.2 1.4 %copy-done.3 = bf16[1,344,2064]{2,1,0:T(8,128)(2,1)S(1)} copy-done((bf16[1,344,2064]{2,1,0:T(8,128)(2,1)S(1)}, bf16[1,344,2064]{2,1,0:T(8,128)(2,1)}, u32[]{:S(2)}) %copy-start.3) | copy-done | bytes 1420056
  30.6 0.0 copy-start.4
  30.6 1.0 %copy-done.4 = f32[2,25,2064]{2,0,1:T(2,128)S(1)} copy-done((f32[2,25,2064]{2,0,1:T(2,128)S(1)}, f32[2,25,2064]{2,0,1:T(2,128)}, u32[]{:S(2)}) %copy-start.4) | copy-done | bytes 412824
  31.6 0.0 copy-start.5
  31.6 0.9 %copy-done.5 = f32[1,25,2064]{2,0,1:T(1,128)S(1)} copy-done((f32[1,25,2064]{2,0,1:T(1,128)S(1)}, f32[1,25,2064]{2,0,1:T(1,128)}, u32[]{:S(2)}) %copy-start.5) | copy-done | bytes 206424
  32.5 0.0 copy-start.6
  32.5 0.9 %copy-done.6 = bf16[336,256]{1,0:T(8,128)(2,1)S(1)} copy-done((bf16[336,256]{1,0:T(8,128)(2,1)S(1)}, bf16[336,256]{1,0:T(8,128)(2,1)}, u32[]{:S(2)}) %copy-start.6) | copy-done | bytes 172056
  33.4 0.0 copy-start.7
  33.4 0.9 %copy-done.7 = bf16[336,96]{1,0:T(8,128)(2,1)S(1)} copy-done((bf16[336,96]{1,0:T(8,128)(2,1)S(1)}, bf16[336,96]{1,0:T(8,128)(2,1)}, u32[]{:S(2)}) %copy-start.7) | copy-done | bytes 64536
  34.3 0.0 copy-start.8
  34.3 0.8 %copy-done.8 = bf16[128,168]{1,0:T(8,128)(2,1)S(1)} copy-done((bf16[128,168]{1,0:T(8,128)(2,1)S(1)}, bf16[128,168]{1,0:T(8,128)(2,1)}, u32[]{:S(2)}) %copy-start.8) | copy-done | bytes 43032
  35.2 0.0 copy-start.9
  35.2 0.8 %copy-done.9 = bf16[128,168]{1,0:T(8,128)(2,1)S(1)} copy-done((bf16[128,168]{1,0:T(8,128)(2,1)S(1)}, bf16[128,168]{1,0:T(8,128)(2,1)}, u32[]{:S(2)}) %copy-start.9) | copy-done | bytes 43032
  36.0 0.0 copy-start.10
  36.0 0.7 %copy-done.10 = bf16[32,336]{1,0:T(8,128)(2,1)S(1)} copy-done((bf16[32,336]{1,0:T(8,128)(2,1)S(1)}, bf16[32,336]{1,0:T(8,128)(2,1)}, u32[]{:S(2)}) %copy-start.10) | copy-done | bytes 21528
  36.7 26.6 %shard_map.166 = (f32[1,344,1032]{2,1,0:T(8,128)}, f32[25,1,1032]{2,1,0:T(1,128)}, f32[1,344,1032]{2,1,0:T(8,128)}) custom-call(s32[1]{0:T(128)S(6)} %copy.18.layer_ref, s32[1]{0:T(128)S(6)} %copy.19.half_ref, s32[1]{0:T(128)S(6)} %copy.20.radius_ref, s32[2]{0:T(128)S(1)} %pad_add_fusion.place_ref, bf16[16,16,344]{2,1,0:T(8,128)(2,1)S(1)} %all_to_all.5.refs_0_, ...), custom_call_target="tpu_custom_call" | custom-call | flops 7270563840 | bytes 8520192 | tf_op jit(solution)/shard_map/pallas_call | solution.py:355
  (1 shorter events, 0.0 us)
Async XLA Ops:
  17.6 6.5 %collective-permute-start = (bf16[16,16,344]{2,1,0:T(8,128)(2,1)S(1)}, bf16[16,16,344]{2,1,0:T(8,128)(2,1)S(1)}, u32[]{:S(2)}, u32[]{:S(2)}) collective-permute-start(bf16[16,16,344]{2,1,0:T(8,128)(2,1)S(1)} %all_to_all.5.refs_0_), channel_id=1, source_target_pairs={{0,1},{1,0},{2,3},{3,2},{4,5},{5,4},{6,7},{7,6},{8,9},{9,8},{10,11... | collective-permute-start | bytes 528392 | tf_op jit(solution)/shard_map/ppermute | solution.py:401
  24.1 1.8 %copy-start = (bf16[2,344,2064]{2,1,0:T(8,128)(2,1)S(1)}, bf16[2,344,2064]{2,1,0:T(8,128)(2,1)}, u32[]{:S(2)}) copy-start(bf16[2,344,2064]{2,1,0:T(8,128)(2,1)} %refs_7_.1) | copy-start | bytes 8520196
  26.0 1.8 %copy-start.1 = (bf16[2,344,2064]{2,1,0:T(8,128)(2,1)S(1)}, bf16[2,344,2064]{2,1,0:T(8,128)(2,1)}, u32[]{:S(2)}) copy-start(bf16[2,344,2064]{2,1,0:T(8,128)(2,1)} %refs_9_.1) | copy-start | bytes 8520196
  27.8 1.4 %copy-start.2 = (bf16[1,344,2064]{2,1,0:T(8,128)(2,1)S(1)}, bf16[1,344,2064]{2,1,0:T(8,128)(2,1)}, u32[]{:S(2)}) copy-start(bf16[1,344,2064]{2,1,0:T(8,128)(2,1)} %refs_10_.1) | copy-start | bytes 4260100
  29.2 1.4 %copy-start.3 = (bf16[1,344,2064]{2,1,0:T(8,128)(2,1)S(1)}, bf16[1,344,2064]{2,1,0:T(8,128)(2,1)}, u32[]{:S(2)}) copy-start(bf16[1,344,2064]{2,1,0:T(8,128)(2,1)} %refs_12_.1) | copy-start | bytes 4260100
  30.6 1.0 %copy-start.4 = (f32[2,25,2064]{2,0,1:T(2,128)S(1)}, f32[2,25,2064]{2,0,1:T(2,128)}, u32[]{:S(2)}) copy-start(f32[2,25,2064]{2,0,1:T(2,128)} %param.20) | copy-start | bytes 1238404
  31.6 0.9 %copy-start.5 = (f32[1,25,2064]{2,0,1:T(1,128)S(1)}, f32[1,25,2064]{2,0,1:T(1,128)}, u32[]{:S(2)}) copy-start(f32[1,25,2064]{2,0,1:T(1,128)} %param.23) | copy-start | bytes 619204
  32.5 0.9 %copy-start.6 = (bf16[336,256]{1,0:T(8,128)(2,1)S(1)}, bf16[336,256]{1,0:T(8,128)(2,1)}, u32[]{:S(2)}) copy-start(bf16[336,256]{1,0:T(8,128)(2,1)} %constant.20.clone.refs_2_) | copy-start | bytes 516100
  33.4 0.9 %copy-start.7 = (bf16[336,96]{1,0:T(8,128)(2,1)S(1)}, bf16[336,96]{1,0:T(8,128)(2,1)}, u32[]{:S(2)}) copy-start(bf16[336,96]{1,0:T(8,128)(2,1)} %constant.23.clone.refs_5_) | copy-start | bytes 193540
  34.3 0.8 %copy-start.8 = (bf16[128,168]{1,0:T(8,128)(2,1)S(1)}, bf16[128,168]{1,0:T(8,128)(2,1)}, u32[]{:S(2)}) copy-start(bf16[128,168]{1,0:T(8,128)(2,1)} %constant.22.clone.refs_4_) | copy-start | bytes 129028
  35.2 0.8 %copy-start.9 = (bf16[128,168]{1,0:T(8,128)(2,1)S(1)}, bf16[128,168]{1,0:T(8,128)(2,1)}, u32[]{:S(2)}) copy-start(bf16[128,168]{1,0:T(8,128)(2,1)} %constant.21.clone.refs_3_) | copy-start | bytes 129028
  36.0 0.7 %copy-start.10 = (bf16[32,336]{1,0:T(8,128)(2,1)S(1)}, bf16[32,336]{1,0:T(8,128)(2,1)}, u32[]{:S(2)}) copy-start(bf16[32,336]{1,0:T(8,128)(2,1)} %constant.24.clone.refs_6_) | copy-start | bytes 64516

commit v3 on v2

--- a/solution.py
+++ b/solution.py
@@ -95,13 +95,9 @@
     place_ref,
     *refs,
 ):
-    x_refs, refs = refs[: len(offsets)], refs[len(offsets) :]
+    pieces = len(offsets)
+    in_hbm, refs, in_vmem = refs[: pieces + 5], refs[pieces + 5 : -pieces - 5], refs[-pieces - 5 :]
     (
-    analysis_ref,
-    even_ref,
-    odd_ref,
-    spectrum_ref,
-    gather_ref,
     teach_up,
     teach_dw,
     teach_down,
@@ -122,6 +118,9 @@
     spec,
     slope_e,
     slope_k,
+    out_up,
+    out_dw,
+    out_down,
     x_first,
     x_next,
     x_now,
@@ -131,8 +130,9 @@
     target,
     wide_up,
     wide_dw,
-    wide_down,
     sems,
+    in_sems,
+    out_sems,
     ) = refs
     maps, cells, channels, hid, taps, rows, parts, scale = dims
     padded = round_up(hid, LANES)
@@ -153,13 +153,14 @@
             for n, (src, dst) in enumerate(zip(sources, targets))
         ]
 
-    for slot in (0, 2, 1):
-        for copy in copies(slot):
-            copy.start()
-
-    analysis = analysis_ref[...]
-    even, odd = even_ref[...], odd_ref[...]
-    spectrum = spectrum_ref[...]
+    staged = [
+        pltpu.make_async_copy(src, dst, in_sems.at[n]) for n, (src, dst) in enumerate(zip(in_hbm, in_vmem))
+    ]
+    x_refs, (analysis_ref, even_ref, odd_ref, spectrum_ref, gather_ref) = in_vmem[:pieces], in_vmem[pieces:]
+    first_copies = copies(0)
+    for copy in [first_copies[1], *staged, first_copies[0], first_copies[2], *copies(2), *copies(1)]:
+        copy.start()
+
     dw_pad[...] = jnp.zeros_like(dw_pad)
 
     half_cells = cells // 2
@@ -179,8 +180,8 @@
         return both[:rows], both[rows:]
 
     def load(slot, mask_taps):
-        for copy in copies(slot):
-            copy.wait()
+        if slot != 1:
+            copies(slot)[1].wait()
         weights = cand_dw_buf[:, 0] if slot == 2 else dw_buf[:, slot]
         if mask_taps:
             side = int(round(taps**0.5))
@@ -250,6 +251,12 @@
             units.append(forward(2, lhs, up_pad, down_pad, cols, None, results))
         return units
 
+    load(0, False)
+    for copy in staged:
+        copy.wait()
+    analysis = analysis_ref[...]
+    even, odd = even_ref[...], odd_ref[...]
+    spectrum = spectrum_ref[...]
     whole_turn = (
         lax.broadcasted_iota(jnp.int32, (half_cells, half_cells), 0)
         + lax.broadcasted_iota(jnp.int32, (half_cells, half_cells), 1)
@@ -260,15 +267,16 @@
             x_first[...] = x_ref[...]
             continue
         block = x_ref.shape[1]
-        for n, (mask, distance) in enumerate(offset):
-            source = (place_ref[0] & mask) ^ distance
+        for n, distance in enumerate(offset):
+            source = place_ref[0] ^ distance
             source = (source & (parts - 1)) * (cells // block) + (source >> (parts.bit_length() - 1))
             at = pl.multiple_of(source * block, block)
             x_first[pl.ds(at, block), :] = x_ref[n]
     for m in range(maps):
         second = slice(m * cells + half_cells, (m + 1) * cells)
         x_first[second] = dot(turn_half, x_first[second]).astype(BF16)
-    load(0, False)
+    for copy in copies(0)[::2]:
+        copy.wait()
     first = []
     interleave(teacher(0, x_first, first))
     branch = sum(first)
@@ -277,6 +285,8 @@
     target[...] = branch
     load(2, True)
     load(1, False)
+    for copy in copies(2)[::2] + copies(1):
+        copy.wait()
     for pad, buf in ((up_pad, up_buf), (down_pad, down_buf)):
         pad[:, hid // LANES * LANES :] = jnp.zeros((channels, padded - hid // LANES * LANES), BF16)
         pad[:, :hid] = buf[2]
@@ -288,11 +298,23 @@
     err_turned[...] = jnp.transpose(err).astype(BF16)
     x_turned[...] = jnp.transpose(0.5 * x_now[...].astype(F32)).astype(BF16)
 
+    offset = start - base
+    shifts = sorted({p * own - at for p, at in enumerate(bases)})
+
+    def leave(wide, out, n, grad):
+        for shift in shifts:
+            @pl.when(offset == shift)
+            def _():
+                out[...] = wide[:, shift : shift + own]
+        pltpu.make_async_copy(out, grad.at[0], out_sems.at[n]).start()
+
+    wide_up[...] = dot(err_turned[...], act[...])
+    leave(wide_up, out_down, 0, grad_down)
+
     def back(at, width):
         cols = aligned(base + at, width)
         here = slice(at, at + width)
         grad_act = dot(err_now[...], down_pad[:, cols])
-        wide_down[:, here] = dot(err_turned[...], act[:, here])
         yield
         grad_k = (grad_act * slope_k[:, here].astype(F32)).astype(BF16)
         yield
@@ -320,18 +342,22 @@
 
     interleave([back(at, min(BACK_UNIT, window - at)) for at in range(0, window, BACK_UNIT)])
 
-    offset = start - base
-    turn = lax.rem(window - offset, window)
-    grad_up[0] = pltpu.roll(wide_up[...], turn, 1)[:, :own]
-    grad_down[0] = pltpu.roll(wide_down[...], turn, 1)[:, :own]
-    rolled = pltpu.roll(wide_dw[...], turn, 1)[:taps, :own]
-    side = int(round(taps**0.5))
-    index = lax.broadcasted_iota(jnp.int32, rolled.shape, 0)
-    row = sum((index >= side * n).astype(jnp.int32) for n in range(1, side))
-    ring = jnp.maximum(jnp.abs(row - side // 2), jnp.abs(index - side * row - side // 2))
-    unit = lax.broadcasted_iota(jnp.int32, rolled.shape, 1) + start
-    keep = (ring <= radius_ref[0]) & (unit < half_ref[0] * (hid // 2))
-    grad_dw[:, 0] = jnp.where(keep, rolled, 0.0)
+    leave(wide_up, out_up, 1, grad_up)
+    for shift in shifts:
+        @pl.when(offset == shift)
+        def _():
+            own_dw = wide_dw[:taps, shift : shift + own]
+            side = int(round(taps**0.5))
+            index = lax.broadcasted_iota(jnp.int32, own_dw.shape, 0)
+            row = sum((index >= side * n).astype(jnp.int32) for n in range(1, side))
+            ring = jnp.maximum(jnp.abs(row - side // 2), jnp.abs(index - side * row - side // 2))
+            unit = lax.broadcasted_iota(jnp.int32, own_dw.shape, 1) + start
+            keep = (ring <= radius_ref[0]) & (unit < half_ref[0] * (hid // 2))
+            out_dw[:, 0] = jnp.where(keep, own_dw, 0.0)
+    pltpu.make_async_copy(out_dw, grad_dw, out_sems.at[2]).start()
+    pltpu.make_async_copy(out_down, grad_down.at[0], out_sems.at[0]).wait()
+    pltpu.make_async_copy(out_up, grad_up.at[0], out_sems.at[1]).wait()
+    pltpu.make_async_copy(out_dw, grad_dw, out_sems.at[2]).wait()
 
 
 def local_grads(pieces, offsets, maps, layer, half, radius, place, parts, images, weights):
@@ -350,7 +376,6 @@
     tap_rows = round_up(taps, 16)
     dims = (maps, cells, channels, hid, taps, rows, parts, 1.0 / images)
     smem = pl.BlockSpec(memory_space=pltpu.SMEM)
-    vmem = pl.BlockSpec(memory_space=pltpu.VMEM)
     anywhere = pl.BlockSpec(memory_space=pl.ANY)
     grad_up, grad_dw, grad_down = pl.pallas_call(
         functools.partial(grads_kernel, dims, offsets),
@@ -359,8 +384,8 @@
             jax.ShapeDtypeStruct((taps, 1, own), F32),
             jax.ShapeDtypeStruct((1, channels, own), F32),
         ),
-        in_specs=[smem] * 4 + [vmem] * (len(pieces) + 5) + [anywhere] * 6,
-        out_specs=(vmem, vmem, vmem),
+        in_specs=[smem] * 4 + [anywhere] * (len(pieces) + 11),
+        out_specs=(anywhere, anywhere, anywhere),
         scratch_shapes=[
             pltpu.VMEM((3, channels, hid), BF16),
             pltpu.VMEM(weights[1].shape, F32),
@@ -373,6 +398,9 @@
             pltpu.VMEM((maps, 2 * rows, window), BF16),
             pltpu.VMEM((count, window), BF16),
             pltpu.VMEM((count, window), BF16),
+            pltpu.VMEM((channels, own), F32),
+            pltpu.VMEM((taps, 1, own), F32),
+            pltpu.VMEM((channels, own), F32),
             pltpu.VMEM((count, channels), BF16),
             pltpu.VMEM((count, channels), BF16),
             pltpu.VMEM((count, channels), BF16),
@@ -382,10 +410,12 @@
             pltpu.VMEM((count, channels), F32),
             pltpu.VMEM((channels, window), F32),
             pltpu.VMEM((tap_rows, window), F32),
-            pltpu.VMEM((channels, window), F32),
             pltpu.SemaphoreType.DMA((3, 3)),
+            pltpu.SemaphoreType.DMA((len(pieces) + len(constants),)),
+            pltpu.SemaphoreType.DMA((3,)),
+            *[pltpu.VMEM(array.shape, BF16) for array in (*pieces, *constants)],
         ],
-        compiler_params=pltpu.CompilerParams(vmem_limit_bytes=40 * 2**20),
+        compiler_params=pltpu.CompilerParams(vmem_limit_bytes=60 * 2**20),
         cost_estimate=pl.CostEstimate(
             flops=20 * count * channels * hid, bytes_accessed=12 * channels * hid, transcendentals=6 * count * hid
         ),
@@ -393,14 +423,19 @@
     return grad_up, grad_dw.transpose(1, 0, 2), grad_down
 
 
-def spread(block, cands, parts):
-    sent = jnp.broadcast_to(block, (cands, *block.shape[1:]))
-    image = lax.all_to_all(sent, "cand", split_axis=0, concat_axis=0, tiled=True)
-    pieces, offsets = [image], [[(parts - 1, c * parts) for c in range(cands)]]
-    for d in range(1, parts):
-        pieces.append(lax.ppermute(image, "img", [(source, source ^ d) for source in range(parts)]))
-        offsets.append([(parts - 1, c * parts + d) for c in range(cands)])
-    return pieces, offsets
+def exchange(block, masks, devices):
+    offset = [0]
+    for mask in masks:
+        distances = [d for d in range(1, devices) if d & ~mask == 0]
+        parts = [block] + [
+            lax.ppermute(block, ("cand", "img"), [(source, source ^ d) for source in range(devices)])
+            for d in distances
+        ]
+        pieces = [[o ^ d for o in offset] for d in [0] + distances]
+        offset = sum(pieces, [])
+        if mask != masks[-1]:
+            block = jnp.concatenate(parts, axis=0)
+    return parts, pieces
 
 
 def body(
@@ -426,7 +461,8 @@
     scalars = (layer_of, expand_half, radius, place, parts, images, weights)
     mine = first_maps.astype(BF16)
     if batch == 1 and images == 2 and own_cells % 16 == 0 and devices & (devices - 1) == 0:
-        pieces, offsets = spread(mine, cands, parts)
+        near = parts * min(2, cands) - 1
+        pieces, offsets = exchange(mine, [(devices - 1) & ~near, near], devices)
         return local_grads(pieces, offsets, images, *scalars)
     whole = lax.all_gather(mine, ("img", "cand")).reshape(parts, cands, batch, own_cells, channels)
     whole = whole.transpose(0, 2, 1, 3, 4).reshape(images, -1, channels)

time: 64.1 us -> 58.1 us (0.906)
  the two profiles are of different devices: /device:TPU:0 before, /device:TPU:1 now
where the time goes in v3:
time: 58.1 us; the launch traced here: 57.4 us
  Pallas kernels  27.3 us (47%)
  starting transfers between devices  16.9 us (29%)
  waiting for transfers between devices  8.33 us (14%)
  between operations  2.8 us (5%)
  other arithmetic  1.34 us (2%)
  local copies, waits for them, and re-layouts  0.7 us (1%)
    pallas_call x1, Pallas kernels, local_grads(): pl.pallas_call(functools.partial(grads_kernel, dims, offsets), out_shape=...  27.3 us
    ppermute x10, starting transfers between devices, exchange(): lax.ppermute(block, ('cand', 'img'), [(source, source ^ d) for source in...  16.9 us
    ppermute x10, waiting for transfers between devices, exchange(): lax.ppermute(block, ('cand', 'img'), [(source, source ^ d) for source in...  8.33 us
  transfers between devices with their start and end apart: 10, of which 4 were waited for; matrix products, arithmetic and copies ran while one was open for 1% of the time, Pallas kernels for 0%

profile of v3, /device:TPU:1, one launch (start us, length us, event | category | flops | bytes accessed | tf_op | source)
XLA Modules:
  0.0 57.4 jit_solution(10460556444339785637)
XLA Ops:
  0.6 0.7 %constant_dynamic-update-slice_fusion.7 = (bf16[8,16,344]{2,1,0:T(8,128)(2,1)S(1)}, bf16[1,16,344]{2,1,0:T(8,128)(2,1)S(1)}) fusion(f32[1,16,344]{2,1,0:T(8,128)} %param.15), kind=kLoop, calls=%fused_computation.7 | loop fusion | flops 5503 | bytes 46592
  1.4 2.1 %collective-permute-start = (bf16[1,16,344]{2,1,0:T(8,128)(2,1)S(1)}, bf16[1,16,344]{2,1,0:T(8,128)(2,1)S(1)}, u32[]{:S(2)}, u32[]{:S(2)}) collective-permute-start(bf16[1,16,344]{2,1,0:T(8,128)(2,1)S(1)} %get-tuple-element.10), channel_id=1, source_target_pairs={{0,4},{1,5},{2,6},{3,7},{4,0},{5,1},{6,2},{7,3},{8,12},{9,13},{10,... | collective-permute-start | bytes 33032 | tf_op jit(solution)/shard_map/ppermute | solution.py:431
  3.4 3.3 %collective-permute-start.6 = (bf16[1,16,344]{2,1,0:T(8,128)(2,1)S(1)}, bf16[1,16,344]{2,1,0:T(8,128)(2,1)S(1)}, u32[]{:S(2)}, u32[]{:S(2)}) collective-permute-start(bf16[1,16,344]{2,1,0:T(8,128)(2,1)S(1)} %get-tuple-element.10), channel_id=1, source_target_pairs={{0,28},{1,29},{2,30},{3,31},{4,24},{5,25},{6,26},{7,27},{8,20},{9,... | collective-permute-start | bytes 33032 | tf_op jit(solution)/shard_map/ppermute | solution.py:431
  6.7 0.1 collective-permute-start.5
  6.8 1.3 %collective-permute-start.4 = (bf16[1,16,344]{2,1,0:T(8,128)(2,1)S(1)}, bf16[1,16,344]{2,1,0:T(8,128)(2,1)S(1)}, u32[]{:S(2)}, u32[]{:S(2)}) collective-permute-start(bf16[1,16,344]{2,1,0:T(8,128)(2,1)S(1)} %get-tuple-element.10), channel_id=1, source_target_pairs={{0,20},{1,21},{2,22},{3,23},{4,16},{5,17},{6,18},{7,19},{8,28},{9,... | collective-permute-start | bytes 33032 | tf_op jit(solution)/shard_map/ppermute | solution.py:431
  8.1 1.9 %collective-permute-start.3 = (bf16[1,16,344]{2,1,0:T(8,128)(2,1)S(1)}, bf16[1,16,344]{2,1,0:T(8,128)(2,1)S(1)}, u32[]{:S(2)}, u32[]{:S(2)}) collective-permute-start(bf16[1,16,344]{2,1,0:T(8,128)(2,1)S(1)} %get-tuple-element.10), channel_id=1, source_target_pairs={{0,16},{1,17},{2,18},{3,19},{4,20},{5,21},{6,22},{7,23},{8,24},{9,... | collective-permute-start | bytes 33032 | tf_op jit(solution)/shard_map/ppermute | solution.py:431
  12.0 0.0 collective-permute-done
  12.0 1.2 %collective-permute-start.1 = (bf16[1,16,344]{2,1,0:T(8,128)(2,1)S(1)}, bf16[1,16,344]{2,1,0:T(8,128)(2,1)S(1)}, u32[]{:S(2)}, u32[]{:S(2)}) collective-permute-start(bf16[1,16,344]{2,1,0:T(8,128)(2,1)S(1)} %get-tuple-element.10), channel_id=1, source_target_pairs={{0,8},{1,9},{2,10},{3,11},{4,12},{5,13},{6,14},{7,15},{8,0},{9,1},... | collective-permute-start | bytes 33032 | tf_op jit(solution)/shard_map/ppermute | solution.py:431
  13.2 1.4 %collective-permute-done.1 = bf16[1,16,344]{2,1,0:T(8,128)(2,1)S(1)} collective-permute-done((bf16[1,16,344]{2,1,0:T(8,128)(2,1)S(1)}, bf16[1,16,344]{2,1,0:T(8,128)(2,1)S(1)}, u32[]{:S(2)}, u32[]{:S(2)}) %collective-permute-start.1) | collective-permute-done | bytes 11040 | tf_op jit(solution)/shard_map/ppermute | solution.py:431
  14.6 1.2 %collective-permute-start.2 = (bf16[1,16,344]{2,1,0:T(8,128)(2,1)S(1)}, bf16[1,16,344]{2,1,0:T(8,128)(2,1)S(1)}, u32[]{:S(2)}, u32[]{:S(2)}) collective-permute-start(bf16[1,16,344]{2,1,0:T(8,128)(2,1)S(1)} %get-tuple-element.10), channel_id=1, source_target_pairs={{0,12},{1,13},{2,14},{3,15},{4,8},{5,9},{6,10},{7,11},{8,4},{9,5},... | collective-permute-start | bytes 33032 | tf_op jit(solution)/shard_map/ppermute | solution.py:431
  15.8 2.3 %collective-permute-done.2 = bf16[1,16,344]{2,1,0:T(8,128)(2,1)S(1)} collective-permute-done((bf16[1,16,344]{2,1,0:T(8,128)(2,1)S(1)}, bf16[1,16,344]{2,1,0:T(8,128)(2,1)S(1)}, u32[]{:S(2)}, u32[]{:S(2)}) %collective-permute-start.2) | collective-permute-done | bytes 11040 | tf_op jit(solution)/shard_map/ppermute | solution.py:431
  18.1 0.0 collective-permute-done.3
  18.1 0.0 collective-permute-done.4
  18.1 0.0 collective-permute-done.5
  18.1 0.0 collective-permute-done.6
  18.1 0.0 copy-start
  18.1 5.5 %collective-permute-start.9 = (bf16[8,16,344]{2,1,0:T(8,128)(2,1)S(1)}, bf16[8,16,344]{2,1,0:T(8,128)(2,1)S(1)}, u32[]{:S(2)}, u32[]{:S(2)}) collective-permute-start(bf16[8,16,344]{2,1,0:T(8,128)(2,1)S(1)} %constant_dynamic-update-slice_fusion.refs_0_), channel_id=1, source_target_pairs={{0,3},{1,2},{2,1},{3,0},{4,7},{5,6},{6,5},{7,4},{8,11},{9,10},{10,... | collective-permute-start | bytes 264200 | tf_op jit(solution)/shard_map/ppermute | solution.py:431
  23.7 0.0 collective-permute-start.8
  23.7 0.3 collective-permute-start.7
  23.9 0.6 %pad_add_fusion.place_ref = s32[2]{0:T(128)} fusion(s32[1]{0:T(128)} %bitcast.1, s32[1]{0:T(128)} %bitcast), kind=kLoop, calls=%fused_computation.8 | loop fusion | flops 2 | bytes 16 | tf_op jit(solution)/shard_map/stack | solution.py:459
  24.5 2.7 %collective-permute-done.9.refs_3_ = bf16[8,16,344]{2,1,0:T(8,128)(2,1)S(1)} collective-permute-done((bf16[8,16,344]{2,1,0:T(8,128)(2,1)S(1)}, bf16[8,16,344]{2,1,0:T(8,128)(2,1)S(1)}, u32[]{:S(2)}, u32[]{:S(2)}) %collective-permute-start.9) | collective-permute-done | bytes 88096 | tf_op jit(solution)/shard_map/ppermute | solution.py:431
  27.2 0.0 copy-start.1
  27.2 0.0 collective-permute-done.8.refs_2_
  27.2 0.0 copy-start.2
  27.2 2.0 %collective-permute-done.7.refs_1_ = bf16[8,16,344]{2,1,0:T(8,128)(2,1)S(1)} collective-permute-done((bf16[8,16,344]{2,1,0:T(8,128)(2,1)S(1)}, bf16[8,16,344]{2,1,0:T(8,128)(2,1)S(1)}, u32[]{:S(2)}, u32[]{:S(2)}) %collective-permute-start.7) | collective-permute-done | bytes 88096 | tf_op jit(solution)/shard_map/ppermute | solution.py:431
  29.2 0.0 copy-start.3
  29.2 0.0 copy-done
  29.2 0.0 copy-done.1
  29.2 0.0 copy-done.2
  29.3 0.6 %copy-done.3 = bf16[8,16,344]{2,1,0:T(8,128)(2,1)} copy-done((bf16[8,16,344]{2,1,0:T(8,128)(2,1)}, bf16[8,16,344]{2,1,0:T(8,128)(2,1)S(1)}, u32[]{:S(2)}) %copy-start.3) | copy-done | bytes 88088
  29.9 27.3 %shard_map.166 = (f32[1,344,1032]{2,1,0:T(8,128)}, f32[25,1,1032]{2,1,0:T(1,128)}, f32[1,344,1032]{2,1,0:T(8,128)}) custom-call(s32[1]{0:T(128)S(6)} %copy.25.layer_ref, s32[1]{0:T(128)S(6)} %copy.26.half_ref, s32[1]{0:T(128)S(6)} %copy.27.radius_ref, s32[2]{0:T(128)} %pad_add_fusion.place_ref, bf16[8,16,344]{2,1,0:T(8,128)(2,1)} %copy-done, ...), custom_call_target="tpu_custom_call" | custom-call | flops 7270563840 | bytes 8520192 | tf_op jit(solution)/shard_map/pallas_call | solution.py:380
  (7 shorter events, 0.1 us)
Async XLA Ops:
  1.4 10.6 %collective-permute-start = (bf16[1,16,344]{2,1,0:T(8,128)(2,1)S(1)}, bf16[1,16,344]{2,1,0:T(8,128)(2,1)S(1)}, u32[]{:S(2)}, u32[]{:S(2)}) collective-permute-start(bf16[1,16,344]{2,1,0:T(8,128)(2,1)S(1)} %get-tuple-element.10), channel_id=1, source_target_pairs={{0,4},{1,5},{2,6},{3,7},{4,0},{5,1},{6,2},{7,3},{8,12},{9,13},{10,... | collective-permute-start | bytes 33032 | tf_op jit(solution)/shard_map/ppermute | solution.py:431
  3.4 14.7 %collective-permute-start.6 = (bf16[1,16,344]{2,1,0:T(8,128)(2,1)S(1)}, bf16[1,16,344]{2,1,0:T(8,128)(2,1)S(1)}, u32[]{:S(2)}, u32[]{:S(2)}) collective-permute-start(bf16[1,16,344]{2,1,0:T(8,128)(2,1)S(1)} %get-tuple-element.10), channel_id=1, source_target_pairs={{0,28},{1,29},{2,30},{3,31},{4,24},{5,25},{6,26},{7,27},{8,20},{9,... | collective-permute-start | bytes 33032 | tf_op jit(solution)/shard_map/ppermute | solution.py:431
  6.7 11.4 %collective-permute-start.5 = (bf16[1,16,344]{2,1,0:T(8,128)(2,1)S(1)}, bf16[1,16,344]{2,1,0:T(8,128)(2,1)S(1)}, u32[]{:S(2)}, u32[]{:S(2)}) collective-permute-start(bf16[1,16,344]{2,1,0:T(8,128)(2,1)S(1)} %get-tuple-element.10), channel_id=1, source_target_pairs={{0,24},{1,25},{2,26},{3,27},{4,28},{5,29},{6,30},{7,31},{8,16},{9,... | collective-permute-start | bytes 33032 | tf_op jit(solution)/shard_map/ppermute | solution.py:431
  6.8 11.3 %collective-permute-start.4 = (bf16[1,16,344]{2,1,0:T(8,128)(2,1)S(1)}, bf16[1,16,344]{2,1,0:T(8,128)(2,1)S(1)}, u32[]{:S(2)}, u32[]{:S(2)}) collective-permute-start(bf16[1,16,344]{2,1,0:T(8,128)(2,1)S(1)} %get-tuple-element.10), channel_id=1, source_target_pairs={{0,20},{1,21},{2,22},{3,23},{4,16},{5,17},{6,18},{7,19},{8,28},{9,... | collective-permute-start | bytes 33032 | tf_op jit(solution)/shard_map/ppermute | solution.py:431
  8.1 9.9 %collective-permute-start.3 = (bf16[1,16,344]{2,1,0:T(8,128)(2,1)S(1)}, bf16[1,16,344]{2,1,0:T(8,128)(2,1)S(1)}, u32[]{:S(2)}, u32[]{:S(2)}) collective-permute-start(bf16[1,16,344]{2,1,0:T(8,128)(2,1)S(1)} %get-tuple-element.10), channel_id=1, source_target_pairs={{0,16},{1,17},{2,18},{3,19},{4,20},{5,21},{6,22},{7,23},{8,24},{9,... | collective-permute-start | bytes 33032 | tf_op jit(solution)/shard_map/ppermute | solution.py:431
  12.0 2.6 %collective-permute-start.1 = (bf16[1,16,344]{2,1,0:T(8,128)(2,1)S(1)}, bf16[1,16,344]{2,1,0:T(8,128)(2,1)S(1)}, u32[]{:S(2)}, u32[]{:S(2)}) collective-permute-start(bf16[1,16,344]{2,1,0:T(8,128)(2,1)S(1)} %get-tuple-element.10), channel_id=1, source_target_pairs={{0,8},{1,9},{2,10},{3,11},{4,12},{5,13},{6,14},{7,15},{8,0},{9,1},... | collective-permute-start | bytes 33032 | tf_op jit(solution)/shard_map/ppermute | solution.py:431
  14.6 3.4 %collective-permute-start.2 = (bf16[1,16,344]{2,1,0:T(8,128)(2,1)S(1)}, bf16[1,16,344]{2,1,0:T(8,128)(2,1)S(1)}, u32[]{:S(2)}, u32[]{:S(2)}) collective-permute-start(bf16[1,16,344]{2,1,0:T(8,128)(2,1)S(1)} %get-tuple-element.10), channel_id=1, source_target_pairs={{0,12},{1,13},{2,14},{3,15},{4,8},{5,9},{6,10},{7,11},{8,4},{9,5},... | collective-permute-start | bytes 33032 | tf_op jit(solution)/shard_map/ppermute | solution.py:431
  18.1 11.1 %copy-start = (bf16[8,16,344]{2,1,0:T(8,128)(2,1)}, bf16[8,16,344]{2,1,0:T(8,128)(2,1)S(1)}, u32[]{:S(2)}) copy-start(bf16[8,16,344]{2,1,0:T(8,128)(2,1)S(1)} %constant_dynamic-update-slice_fusion.refs_0_) | copy-start | bytes 264196
  18.1 9.1 %collective-permute-start.9 = (bf16[8,16,344]{2,1,0:T(8,128)(2,1)S(1)}, bf16[8,16,344]{2,1,0:T(8,128)(2,1)S(1)}, u32[]{:S(2)}, u32[]{:S(2)}) collective-permute-start(bf16[8,16,344]{2,1,0:T(8,128)(2,1)S(1)} %constant_dynamic-update-slice_fusion.refs_0_), channel_id=1, source_target_pairs={{0,3},{1,2},{2,1},{3,0},{4,7},{5,6},{6,5},{7,4},{8,11},{9,10},{10,... | collective-permute-start | bytes 264200 | tf_op jit(solution)/shard_map/ppermute | solution.py:431
  23.7 3.6 %collective-permute-start.8 = (bf16[8,16,344]{2,1,0:T(8,128)(2,1)S(1)}, bf16[8,16,344]{2,1,0:T(8,128)(2,1)S(1)}, u32[]{:S(2)}, u32[]{:S(2)}) collective-permute-start(bf16[8,16,344]{2,1,0:T(8,128)(2,1)S(1)} %constant_dynamic-update-slice_fusion.refs_0_), channel_id=1, source_target_pairs={{0,2},{1,3},{2,0},{3,1},{4,6},{5,7},{6,4},{7,5},{8,10},{9,11},{10,... | collective-permute-start | bytes 264200 | tf_op jit(solution)/shard_map/ppermute | solution.py:431
  23.7 5.6 %collective-permute-start.7 = (bf16[8,16,344]{2,1,0:T(8,128)(2,1)S(1)}, bf16[8,16,344]{2,1,0:T(8,128)(2,1)S(1)}, u32[]{:S(2)}, u32[]{:S(2)}) collective-permute-start(bf16[8,16,344]{2,1,0:T(8,128)(2,1)S(1)} %constant_dynamic-update-slice_fusion.refs_0_), channel_id=1, source_target_pairs={{0,1},{1,0},{2,3},{3,2},{4,5},{5,4},{6,7},{7,6},{8,9},{9,8},{10,11... | collective-permute-start | bytes 264200 | tf_op jit(solution)/shard_map/ppermute | solution.py:431
  27.2 2.0 %copy-start.1 = (bf16[8,16,344]{2,1,0:T(8,128)(2,1)}, bf16[8,16,344]{2,1,0:T(8,128)(2,1)S(1)}, u32[]{:S(2)}) copy-start(bf16[8,16,344]{2,1,0:T(8,128)(2,1)S(1)} %collective-permute-done.9.refs_3_) | copy-start | bytes 264196
  27.2 2.0 %copy-start.2 = (bf16[8,16,344]{2,1,0:T(8,128)(2,1)}, bf16[8,16,344]{2,1,0:T(8,128)(2,1)S(1)}, u32[]{:S(2)}) copy-start(bf16[8,16,344]{2,1,0:T(8,128)(2,1)S(1)} %collective-permute-done.8.refs_2_) | copy-start | bytes 264196
  29.2 0.6 %copy-start.3 = (bf16[8,16,344]{2,1,0:T(8,128)(2,1)}, bf16[8,16,344]{2,1,0:T(8,128)(2,1)S(1)}, u32[]{:S(2)}) copy-start(bf16[8,16,344]{2,1,0:T(8,128)(2,1)S(1)} %collective-permute-done.7.refs_1_) | copy-start | bytes 264196

commit v4 on v3

--- a/solution.py
+++ b/solution.py
@@ -55,13 +55,14 @@
     spectrum = np.zeros((2 * rows, tap_rows))
     spectrum[:count, :taps] = np.cos(tap_angle)
     spectrum[rows : rows + count, :taps] = np.sin(tap_angle)
-    gather = np.zeros((tap_rows, 2 * rows))
-    gather[:taps, :count] = (weight[:, None] * np.cos(tap_angle)).T
-    gather[:taps, rows : rows + count] = -(weight[:, None] * np.sin(tap_angle)).T
+    gather_re, gather_im = np.zeros((tap_rows, rows)), np.zeros((tap_rows, rows))
+    gather_re[:taps, :count] = (weight[:, None] * np.cos(tap_angle)).T
+    gather_im[:taps, :count] = -(weight[:, None] * np.sin(tap_angle)).T
 
     coarse = spectrum.astype(ml_dtypes.bfloat16).astype(np.float64)
     spectrum = np.concatenate([coarse, coarse, spectrum - coarse], axis=1)
-    return rows, [jnp.asarray(m.astype(ml_dtypes.bfloat16)) for m in (analysis, even, odd, spectrum, gather)]
+    matrices = (analysis, even, odd, spectrum, gather_re, gather_im)
+    return rows, [jnp.asarray(m.astype(ml_dtypes.bfloat16)) for m in matrices]
 
 
 def dot(a, b):
@@ -96,7 +97,7 @@
     *refs,
 ):
     pieces = len(offsets)
-    in_hbm, refs, in_vmem = refs[: pieces + 5], refs[pieces + 5 : -pieces - 5], refs[-pieces - 5 :]
+    in_hbm, refs, in_vmem = refs[: pieces + 6], refs[pieces + 6 : -pieces - 6], refs[-pieces - 6 :]
     (
     teach_up,
     teach_dw,
@@ -156,7 +157,7 @@
     staged = [
         pltpu.make_async_copy(src, dst, in_sems.at[n]) for n, (src, dst) in enumerate(zip(in_hbm, in_vmem))
     ]
-    x_refs, (analysis_ref, even_ref, odd_ref, spectrum_ref, gather_ref) = in_vmem[:pieces], in_vmem[pieces:]
+    x_refs, constants = in_vmem[:pieces], in_vmem[pieces:]
     first_copies = copies(0)
     for copy in [first_copies[1], *staged, first_copies[0], first_copies[2], *copies(2), *copies(1)]:
         copy.start()
@@ -168,16 +169,18 @@
     start = place_ref[1] * own
     base = jnp.minimum(start // LANES * LANES, padded - window)
 
+    def split(both):
+        return both[:rows].astype(BF16), both[rows:].astype(BF16)
+
     def synthesis(re, im):
-        same, other = dot(even, re.astype(BF16)), dot(odd, im.astype(BF16))
+        same, other = dot(even, re), dot(odd, im)
         return jnp.concatenate([same + other, same - other], axis=0)
 
     def tap_spectrum(slot, cols):
         weights = dw_pad[slot, :, cols]
         high = weights.astype(BF16)
         low = (weights - high.astype(F32)).astype(BF16)
-        both = dot(spectrum, jnp.concatenate([high, low, high], axis=0))
-        return both[:rows], both[rows:]
+        return split(dot(spectrum, jnp.concatenate([high, low, high], axis=0)))
 
     def load(slot, mask_taps):
         if slot != 1:
@@ -211,9 +214,9 @@
             here = slice(m * cells, (m + 1) * cells)
             both = dot(analysis, units[here])
             yield
-            re, im = both[:rows], both[rows:]
+            re, im = split(both)
             if keep:
-                spec[m, :, save] = both.astype(BF16)
+                spec[m, 0, :, save], spec[m, 1, :, save] = re, im
             mixed_re, mixed_im = re * tap_re - im * tap_im, re * tap_im + im * tap_re
             yield
             mixed = synthesis(mixed_re, mixed_im)
@@ -254,9 +257,7 @@
     load(0, False)
     for copy in staged:
         copy.wait()
-    analysis = analysis_ref[...]
-    even, odd = even_ref[...], odd_ref[...]
-    spectrum = spectrum_ref[...]
+    analysis, even, odd, spectrum, gather_re, gather_im = (ref[...] for ref in constants)
     whole_turn = (
         lax.broadcasted_iota(jnp.int32, (half_cells, half_cells), 0)
         + lax.broadcasted_iota(jnp.int32, (half_cells, half_cells), 1)
@@ -316,29 +317,27 @@
         here = slice(at, at + width)
         grad_act = dot(err_now[...], down_pad[:, cols])
         yield
-        grad_k = (grad_act * slope_k[:, here].astype(F32)).astype(BF16)
+        grad_k = grad_act.astype(BF16) * slope_k[:, here]
         yield
         tap_re, tap_im = tap_spectrum(2, cols)
-        sum_re = sum_im = 0.0
+        sum_re, sum_im = [], []
         grad_pre = []
         for m in range(maps):
             rows_here = slice(m * cells, (m + 1) * cells)
             both = dot(analysis, grad_k[rows_here])
             yield
-            re, im = both[:rows], both[rows:]
-            kept = spec[m, :, here].astype(F32)
-            e_re, e_im = kept[:rows], kept[rows:]
-            sum_re += re * e_re + im * e_im
-            sum_im += re * e_im - im * e_re
+            re, im = split(both)
+            e_re, e_im = spec[m, 0, :, here], spec[m, 1, :, here]
+            sum_re.append(re * e_re + im * e_im)
+            sum_im.append(re * e_im - im * e_re)
             mixed_re, mixed_im = re * tap_re + im * tap_im, im * tap_re - re * tap_im
             yield
             grad_e = synthesis(mixed_re, mixed_im)
             yield
-            grad_pre.append((grad_e * slope_e[rows_here, here].astype(F32)).astype(BF16))
+            grad_pre.append(grad_e.astype(BF16) * slope_e[rows_here, here])
         yield
         wide_up[:, here] = dot(x_turned[...], jnp.concatenate(grad_pre, axis=0))
-        sums = jnp.concatenate([sum_re, sum_im], axis=0).astype(BF16)
-        wide_dw[:, here] = dot(gather_ref[...], sums)
+        wide_dw[:, here] = dot(gather_re, sum(sum_re[1:], sum_re[0])) + dot(gather_im, sum(sum_im[1:], sum_im[0]))
 
     interleave([back(at, min(BACK_UNIT, window - at)) for at in range(0, window, BACK_UNIT)])
 
@@ -384,7 +383,7 @@
             jax.ShapeDtypeStruct((taps, 1, own), F32),
             jax.ShapeDtypeStruct((1, channels, own), F32),
         ),
-        in_specs=[smem] * 4 + [anywhere] * (len(pieces) + 11),
+        in_specs=[smem] * 4 + [anywhere] * (len(pieces) + 12),
         out_specs=(anywhere, anywhere, anywhere),
         scratch_shapes=[
             pltpu.VMEM((3, channels, hid), BF16),
@@ -395,7 +394,7 @@
             pltpu.VMEM((channels, padded), BF16),
             pltpu.VMEM((channels, padded), BF16),
             pltpu.VMEM((count, window), BF16),
-            pltpu.VMEM((maps, 2 * rows, window), BF16),
+            pltpu.VMEM((maps, 2, rows, window), BF16),
             pltpu.VMEM((count, window), BF16),
             pltpu.VMEM((count, window), BF16),
             pltpu.VMEM((channels, own), F32),
@@ -461,8 +460,9 @@
     scalars = (layer_of, expand_half, radius, place, parts, images, weights)
     mine = first_maps.astype(BF16)
     if batch == 1 and images == 2 and own_cells % 16 == 0 and devices & (devices - 1) == 0:
-        near = parts * min(2, cands) - 1
-        pieces, offsets = exchange(mine, [(devices - 1) & ~near, near], devices)
+        core = parts if cands > 1 else 0
+        bits = [1 << n for n in reversed(range(devices.bit_length() - 1))]
+        pieces, offsets = exchange(mine, [b for b in bits if b != core] + [core] * (core > 0), devices)
         return local_grads(pieces, offsets, images, *scalars)
     whole = lax.all_gather(mine, ("img", "cand")).reshape(parts, cands, batch, own_cells, channels)
     whole = whole.transpose(0, 2, 1, 3, 4).reshape(images, -1, channels)

time: 58.1 us -> 50.1 us (0.86)
  starting transfers between devices: 16.9 us -> 12.3 us
  waiting for transfers between devices: 8.33 us -> 6.23 us
  Pallas kernels: 27.3 us -> 26.2 us
    ppermute x10 -> x5, starting transfers between devices: 16.9 us -> 12.3 us  [exchange(): lax.ppermute(block, ('cand', 'img'), [(source, source ^ d) for source in...]
    ppermute x10 -> x5, waiting for transfers between devices: 8.33 us -> 6.23 us  [exchange(): lax.ppermute(block, ('cand', 'img'), [(source, source ^ d) for source in...]
    pallas_call x1, Pallas kernels: 27.3 us -> 26.2 us  [local_grads(): pl.pallas_call(functools.partial(grads_kernel, dims, offsets), out_shape=...]
  transfers between devices with their start and end apart: 10 -> 5, of which waited for: 4 -> 4; matrix products, arithmetic and copies ran while one was open for 1% -> 1% of each run, Pallas kernels for 0% -> 0%
where the time goes in v4:
time: 50.1 us; the launch traced here: 49.5 us
  Pallas kernels  26.2 us (52%)
  starting transfers between devices  12.3 us (25%)
  waiting for transfers between devices  6.23 us (12%)
  between operations  2.76 us (6%)
  other arithmetic  1.37 us (3%)
  local copies, waits for them, and re-layouts  0.72 us (1%)
    pallas_call x1, Pallas kernels, local_grads(): pl.pallas_call(functools.partial(grads_kernel, dims, offsets), out_shape=...  26.2 us
    ppermute x5, starting transfers between devices, exchange(): lax.ppermute(block, ('cand', 'img'), [(source, source ^ d) for source in...  12.3 us
    ppermute x5, waiting for transfers between devices, exchange(): lax.ppermute(block, ('cand', 'img'), [(source, source ^ d) for source in...  6.23 us
  transfers between devices with their start and end apart: 5, of which 4 were waited for; matrix products, arithmetic and copies ran while one was open for 1% of the time, Pallas kernels for 0%

profile of v4, /device:TPU:1, one launch (start us, length us, event | category | flops | bytes accessed | tf_op | source)
XLA Modules:
  0.0 49.5 jit_solution(1483387023549981571)
XLA Ops:
  0.6 0.7 %constant_dynamic-update-slice_fusion.4 = (bf16[16,16,344]{2,1,0:T(8,128)(2,1)S(1)}, bf16[1,16,344]{2,1,0:T(8,128)(2,1)S(1)}) fusion(f32[1,16,344]{2,1,0:T(8,128)} %param.16), kind=kLoop, calls=%fused_computation.7 | loop fusion | flops 5503 | bytes 46592
  1.4 3.1 %collective-permute-start = (bf16[1,16,344]{2,1,0:T(8,128)(2,1)S(1)}, bf16[1,16,344]{2,1,0:T(8,128)(2,1)S(1)}, u32[]{:S(2)}, u32[]{:S(2)}) collective-permute-start(bf16[1,16,344]{2,1,0:T(8,128)(2,1)S(1)} %get-tuple-element.10), channel_id=1, source_target_pairs={{0,16},{1,17},{2,18},{3,19},{4,20},{5,21},{6,22},{7,23},{8,24},{9,... | collective-permute-start | bytes 33032 | tf_op jit(solution)/shard_map/ppermute | solution.py:430
  4.5 1.1 %collective-permute-done = bf16[1,16,344]{2,1,0:T(8,128)(2,1)S(1)} collective-permute-done((bf16[1,16,344]{2,1,0:T(8,128)(2,1)S(1)}, bf16[1,16,344]{2,1,0:T(8,128)(2,1)S(1)}, u32[]{:S(2)}, u32[]{:S(2)}) %collective-permute-start) | collective-permute-done | bytes 11040 | tf_op jit(solution)/shard_map/ppermute | solution.py:430
  5.6 1.4 %collective-permute-start.1 = (bf16[2,16,344]{2,1,0:T(8,128)(2,1)S(1)}, bf16[2,16,344]{2,1,0:T(8,128)(2,1)S(1)}, u32[]{:S(2)}, u32[]{:S(2)}) collective-permute-start(bf16[2,16,344]{2,1,0:T(8,128)(2,1)S(1)} %pad_maximum_fusion.2), channel_id=1, source_target_pairs={{0,8},{1,9},{2,10},{3,11},{4,12},{5,13},{6,14},{7,15},{8,0},{9,1},... | collective-permute-start | bytes 66056 | tf_op jit(solution)/shard_map/ppermute | solution.py:430
  7.0 1.3 %collective-permute-done.1 = bf16[2,16,344]{2,1,0:T(8,128)(2,1)S(1)} collective-permute-done((bf16[2,16,344]{2,1,0:T(8,128)(2,1)S(1)}, bf16[2,16,344]{2,1,0:T(8,128)(2,1)S(1)}, u32[]{:S(2)}, u32[]{:S(2)}) %collective-permute-start.1) | collective-permute-done | bytes 22048 | tf_op jit(solution)/shard_map/ppermute | solution.py:430
  8.4 1.4 %collective-permute-start.2 = (bf16[4,16,344]{2,1,0:T(8,128)(2,1)S(1)}, bf16[4,16,344]{2,1,0:T(8,128)(2,1)S(1)}, u32[]{:S(2)}, u32[]{:S(2)}) collective-permute-start(bf16[4,16,344]{2,1,0:T(8,128)(2,1)S(1)} %pad_maximum_fusion.1), channel_id=1, source_target_pairs={{0,4},{1,5},{2,6},{3,7},{4,0},{5,1},{6,2},{7,3},{8,12},{9,13},{10,... | collective-permute-start | bytes 132104 | tf_op jit(solution)/shard_map/ppermute | solution.py:430
  9.7 1.6 %collective-permute-done.2 = bf16[4,16,344]{2,1,0:T(8,128)(2,1)S(1)} collective-permute-done((bf16[4,16,344]{2,1,0:T(8,128)(2,1)S(1)}, bf16[4,16,344]{2,1,0:T(8,128)(2,1)S(1)}, u32[]{:S(2)}, u32[]{:S(2)}) %collective-permute-start.2) | collective-permute-done | bytes 44064 | tf_op jit(solution)/shard_map/ppermute | solution.py:430
  11.4 1.3 %collective-permute-start.3 = (bf16[8,16,344]{2,1,0:T(8,128)(2,1)S(1)}, bf16[8,16,344]{2,1,0:T(8,128)(2,1)S(1)}, u32[]{:S(2)}, u32[]{:S(2)}) collective-permute-start(bf16[8,16,344]{2,1,0:T(8,128)(2,1)S(1)} %pad_maximum_fusion), channel_id=1, source_target_pairs={{0,1},{1,0},{2,3},{3,2},{4,5},{5,4},{6,7},{7,6},{8,9},{9,8},{10,11... | collective-permute-start | bytes 264200 | tf_op jit(solution)/shard_map/ppermute | solution.py:430
  12.7 2.2 %collective-permute-done.3 = bf16[8,16,344]{2,1,0:T(8,128)(2,1)S(1)} collective-permute-done((bf16[8,16,344]{2,1,0:T(8,128)(2,1)S(1)}, bf16[8,16,344]{2,1,0:T(8,128)(2,1)S(1)}, u32[]{:S(2)}, u32[]{:S(2)}) %collective-permute-start.3) | collective-permute-done | bytes 88096 | tf_op jit(solution)/shard_map/ppermute | solution.py:430
  15.0 0.0 copy-start
  15.0 5.1 %collective-permute-start.4 = (bf16[16,16,344]{2,1,0:T(8,128)(2,1)S(1)}, bf16[16,16,344]{2,1,0:T(8,128)(2,1)S(1)}, u32[]{:S(2)}, u32[]{:S(2)}) collective-permute-start(bf16[16,16,344]{2,1,0:T(8,128)(2,1)S(1)} %constant_dynamic-update-slice_fusion.refs_0_), channel_id=1, source_target_pairs={{0,2},{1,3},{2,0},{3,1},{4,6},{5,7},{6,4},{7,5},{8,10},{9,11},{10,... | collective-permute-start | bytes 528392 | tf_op jit(solution)/shard_map/ppermute | solution.py:430
  22.0 0.6 %pad_add_fusion.place_ref = s32[2]{0:T(128)} fusion(s32[1]{0:T(128)} %bitcast.1, s32[1]{0:T(128)} %bitcast), kind=kLoop, calls=%fused_computation.8 | loop fusion | flops 2 | bytes 16 | tf_op jit(solution)/shard_map/stack | solution.py:458
  22.5 0.0 collective-permute-done.4.refs_1_
  22.6 0.0 copy-start.1
  22.6 0.0 copy-done
  22.6 0.7 %copy-done.1 = bf16[16,16,344]{2,1,0:T(8,128)(2,1)} copy-done((bf16[16,16,344]{2,1,0:T(8,128)(2,1)}, bf16[16,16,344]{2,1,0:T(8,128)(2,1)S(1)}, u32[]{:S(2)}) %copy-start.1) | copy-done | bytes 176152
  23.2 26.2 %shard_map.175 = (f32[1,344,1032]{2,1,0:T(8,128)}, f32[25,1,1032]{2,1,0:T(1,128)}, f32[1,344,1032]{2,1,0:T(8,128)}) custom-call(s32[1]{0:T(128)S(6)} %copy.23.layer_ref, s32[1]{0:T(128)S(6)} %copy.24.half_ref, s32[1]{0:T(128)S(6)} %copy.25.radius_ref, s32[2]{0:T(128)} %pad_add_fusion.place_ref, bf16[16,16,344]{2,1,0:T(8,128)(2,1)} %copy-done, ...), custom_call_target="tpu_custom_call" | custom-call | flops 7270563840 | bytes 8520192 | tf_op jit(solution)/shard_map/pallas_call | solution.py:379
  (7 shorter events, 0.1 us)
Async XLA Ops:
  1.4 4.2 %collective-permute-start = (bf16[1,16,344]{2,1,0:T(8,128)(2,1)S(1)}, bf16[1,16,344]{2,1,0:T(8,128)(2,1)S(1)}, u32[]{:S(2)}, u32[]{:S(2)}) collective-permute-start(bf16[1,16,344]{2,1,0:T(8,128)(2,1)S(1)} %get-tuple-element.10), channel_id=1, source_target_pairs={{0,16},{1,17},{2,18},{3,19},{4,20},{5,21},{6,22},{7,23},{8,24},{9,... | collective-permute-start | bytes 33032 | tf_op jit(solution)/shard_map/ppermute | solution.py:430
  5.6 2.7 %collective-permute-start.1 = (bf16[2,16,344]{2,1,0:T(8,128)(2,1)S(1)}, bf16[2,16,344]{2,1,0:T(8,128)(2,1)S(1)}, u32[]{:S(2)}, u32[]{:S(2)}) collective-permute-start(bf16[2,16,344]{2,1,0:T(8,128)(2,1)S(1)} %pad_maximum_fusion.2), channel_id=1, source_target_pairs={{0,8},{1,9},{2,10},{3,11},{4,12},{5,13},{6,14},{7,15},{8,0},{9,1},... | collective-permute-start | bytes 66056 | tf_op jit(solution)/shard_map/ppermute | solution.py:430
  8.4 3.0 %collective-permute-start.2 = (bf16[4,16,344]{2,1,0:T(8,128)(2,1)S(1)}, bf16[4,16,344]{2,1,0:T(8,128)(2,1)S(1)}, u32[]{:S(2)}, u32[]{:S(2)}) collective-permute-start(bf16[4,16,344]{2,1,0:T(8,128)(2,1)S(1)} %pad_maximum_fusion.1), channel_id=1, source_target_pairs={{0,4},{1,5},{2,6},{3,7},{4,0},{5,1},{6,2},{7,3},{8,12},{9,13},{10,... | collective-permute-start | bytes 132104 | tf_op jit(solution)/shard_map/ppermute | solution.py:430
  11.4 3.5 %collective-permute-start.3 = (bf16[8,16,344]{2,1,0:T(8,128)(2,1)S(1)}, bf16[8,16,344]{2,1,0:T(8,128)(2,1)S(1)}, u32[]{:S(2)}, u32[]{:S(2)}) collective-permute-start(bf16[8,16,344]{2,1,0:T(8,128)(2,1)S(1)} %pad_maximum_fusion), channel_id=1, source_target_pairs={{0,1},{1,0},{2,3},{3,2},{4,5},{5,4},{6,7},{7,6},{8,9},{9,8},{10,11... | collective-permute-start | bytes 264200 | tf_op jit(solution)/shard_map/ppermute | solution.py:430
  15.0 7.6 %copy-start = (bf16[16,16,344]{2,1,0:T(8,128)(2,1)}, bf16[16,16,344]{2,1,0:T(8,128)(2,1)S(1)}, u32[]{:S(2)}) copy-start(bf16[16,16,344]{2,1,0:T(8,128)(2,1)S(1)} %constant_dynamic-update-slice_fusion.refs_0_) | copy-start | bytes 528388
  15.0 7.6 %collective-permute-start.4 = (bf16[16,16,344]{2,1,0:T(8,128)(2,1)S(1)}, bf16[16,16,344]{2,1,0:T(8,128)(2,1)S(1)}, u32[]{:S(2)}, u32[]{:S(2)}) collective-permute-start(bf16[16,16,344]{2,1,0:T(8,128)(2,1)S(1)} %constant_dynamic-update-slice_fusion.refs_0_), channel_id=1, source_target_pairs={{0,2},{1,3},{2,0},{3,1},{4,6},{5,7},{6,4},{7,5},{8,10},{9,11},{10,... | collective-permute-start | bytes 528392 | tf_op jit(solution)/shard_map/ppermute | solution.py:430
  22.6 0.7 %copy-start.1 = (bf16[16,16,344]{2,1,0:T(8,128)(2,1)}, bf16[16,16,344]{2,1,0:T(8,128)(2,1)S(1)}, u32[]{:S(2)}) copy-start(bf16[16,16,344]{2,1,0:T(8,128)(2,1)S(1)} %collective-permute-done.4.refs_1_) | copy-start | bytes 528388

commit v5 on v4

--- a/solution.py
+++ b/solution.py
@@ -97,7 +97,7 @@
     *refs,
 ):
     pieces = len(offsets)
-    in_hbm, refs, in_vmem = refs[: pieces + 6], refs[pieces + 6 : -pieces - 6], refs[-pieces - 6 :]
+    x_refs, in_hbm, refs, constants = refs[:pieces], refs[pieces : pieces + 6], refs[pieces + 6 : -6], refs[-6:]
     (
     teach_up,
     teach_dw,
@@ -155,9 +155,8 @@
         ]
 
     staged = [
-        pltpu.make_async_copy(src, dst, in_sems.at[n]) for n, (src, dst) in enumerate(zip(in_hbm, in_vmem))
+        pltpu.make_async_copy(src, dst, in_sems.at[n]) for n, (src, dst) in enumerate(zip(in_hbm, constants))
     ]
-    x_refs, constants = in_vmem[:pieces], in_vmem[pieces:]
     first_copies = copies(0)
     for copy in [first_copies[1], *staged, first_copies[0], first_copies[2], *copies(2), *copies(1)]:
         copy.start()
@@ -230,7 +229,7 @@
                 act[here, save] = acts[-1]
                 slope_k[here, save] = (more_k + wide_k - wide_k * bend_k).astype(BF16)
         yield
-        results.append(dot_nt(jnp.concatenate(acts, axis=0), down[:, cols]))
+        results.append(dot_nt(down[:, cols], jnp.concatenate(acts, axis=0)))
 
     def teacher(slot, lhs, results):
         bounds = list(range(0, max(hid - UNIT // 2, 1), UNIT)) + [hid]
@@ -281,7 +280,7 @@
     first = []
     interleave(teacher(0, x_first, first))
     branch = sum(first)
-    x_next[...] = (x_first[...].astype(F32) + branch).astype(BF16)
+    x_next[...] = (x_first[...].astype(F32) + jnp.transpose(branch)).astype(BF16)
     x_now[...] = jnp.where(layer_ref[0] == 0, x_first[...], x_next[...])
     target[...] = branch
     load(2, True)
@@ -295,8 +294,8 @@
     units = [teacher(1, x_next, second), candidate(x_now, third)]
     interleave([unit for pair in itertools.zip_longest(*units) for unit in pair if unit is not None])
     err = (sum(third) - jnp.where(layer_ref[0] == 0, target[...], sum(second))) * scale
-    err_now[...] = (0.5 * err).astype(BF16)
-    err_turned[...] = jnp.transpose(err).astype(BF16)
+    err_now[...] = jnp.transpose(0.5 * err).astype(BF16)
+    err_turned[...] = err.astype(BF16)
     x_turned[...] = jnp.transpose(0.5 * x_now[...].astype(F32)).astype(BF16)
 
     offset = start - base
@@ -375,6 +374,7 @@
     tap_rows = round_up(taps, 16)
     dims = (maps, cells, channels, hid, taps, rows, parts, 1.0 / images)
     smem = pl.BlockSpec(memory_space=pltpu.SMEM)
+    vmem = pl.BlockSpec(memory_space=pltpu.VMEM)
     anywhere = pl.BlockSpec(memory_space=pl.ANY)
     grad_up, grad_dw, grad_down = pl.pallas_call(
         functools.partial(grads_kernel, dims, offsets),
@@ -383,7 +383,7 @@
             jax.ShapeDtypeStruct((taps, 1, own), F32),
             jax.ShapeDtypeStruct((1, channels, own), F32),
         ),
-        in_specs=[smem] * 4 + [anywhere] * (len(pieces) + 12),
+        in_specs=[smem] * 4 + [vmem] * len(pieces) + [anywhere] * 12,
         out_specs=(anywhere, anywhere, anywhere),
         scratch_shapes=[
             pltpu.VMEM((3, channels, hid), BF16),
@@ -406,13 +406,13 @@
             pltpu.VMEM((channels, count), BF16),
             pltpu.VMEM((count, channels), BF16),
             pltpu.VMEM((channels, count), BF16),
-            pltpu.VMEM((count, channels), F32),
+            pltpu.VMEM((channels, count), F32),
             pltpu.VMEM((channels, window), F32),
             pltpu.VMEM((tap_rows, window), F32),
             pltpu.SemaphoreType.DMA((3, 3)),
-            pltpu.SemaphoreType.DMA((len(pieces) + len(constants),)),
+            pltpu.SemaphoreType.DMA((len(constants),)),
             pltpu.SemaphoreType.DMA((3,)),
-            *[pltpu.VMEM(array.shape, BF16) for array in (*pieces, *constants)],
+            *[pltpu.VMEM(array.shape, BF16) for array in constants],
         ],
         compiler_params=pltpu.CompilerParams(vmem_limit_bytes=60 * 2**20),
         cost_estimate=pl.CostEstimate(
@@ -433,7 +433,7 @@
         pieces = [[o ^ d for o in offset] for d in [0] + distances]
         offset = sum(pieces, [])
         if mask != masks[-1]:
-            block = jnp.concatenate(parts, axis=0)
+            block = jnp.concatenate(parts, axis=0).astype(BF16)
     return parts, pieces
 
 
@@ -458,13 +458,13 @@
     place = jnp.stack([lax.axis_index("cand") * parts + part, part])
     weights = (teach_up, teach_dw, teach_down, cand_up, cand_dw, cand_down)
     scalars = (layer_of, expand_half, radius, place, parts, images, weights)
-    mine = first_maps.astype(BF16)
     if batch == 1 and images == 2 and own_cells % 16 == 0 and devices & (devices - 1) == 0:
-        core = parts if cands > 1 else 0
-        bits = [1 << n for n in reversed(range(devices.bit_length() - 1))]
-        pieces, offsets = exchange(mine, [b for b in bits if b != core] + [core] * (core > 0), devices)
+        core = parts * (cands > 1)
+        near = (parts - 1) | (2 * core)
+        masks = [(devices - 1) & ~near & ~core, near, core]
+        pieces, offsets = exchange(first_maps, masks, devices)
         return local_grads(pieces, offsets, images, *scalars)
-    whole = lax.all_gather(mine, ("img", "cand")).reshape(parts, cands, batch, own_cells, channels)
+    whole = lax.all_gather(first_maps.astype(BF16), ("img", "cand")).reshape(parts, cands, batch, own_cells, channels)
     whole = whole.transpose(0, 2, 1, 3, 4).reshape(images, -1, channels)
     group = 2 if images % 2 == 0 else 1
     total = None

time: 50.1 us -> 49.4 us (0.986)
  starting transfers between devices: 12.3 us -> 11.3 us
  other arithmetic: 1.37 us -> 2.12 us
    ppermute x5 -> x7, starting transfers between devices: 12.3 us -> 11.3 us  [exchange(): lax.ppermute(block, ('cand', 'img'), [(source, source ^ d) for source in...]
    unnamed x1 -> x2, other arithmetic: 0.74 us -> 1.48 us
    ppermute x5 -> x7, waiting for transfers between devices: 6.23 us -> 6.26 us  [exchange(): lax.ppermute(block, ('cand', 'img'), [(source, source ^ d) for source in...]
  transfers between devices with their start and end apart: 5 -> 7, of which waited for: 4 -> 3; matrix products, arithmetic and copies ran while one was open for 1% -> 3% of each run, Pallas kernels for 0% -> 0%
where the time goes in v5:
time: 49.4 us; the launch traced here: 49.1 us
  Pallas kernels  25.9 us (52%)
  starting transfers between devices  11.3 us (23%)
  waiting for transfers between devices  6.26 us (13%)
  between operations  2.79 us (6%)
  other arithmetic  2.12 us (4%)
  local copies, waits for them, and re-layouts  0.74 us (1%)
    pallas_call x1, Pallas kernels, local_grads(): pl.pallas_call(functools.partial(grads_kernel, dims, offsets), out_shape=...  25.9 us
    ppermute x7, starting transfers between devices, exchange(): lax.ppermute(block, ('cand', 'img'), [(source, source ^ d) for source in...  11.3 us
    ppermute x7, waiting for transfers between devices, exchange(): lax.ppermute(block, ('cand', 'img'), [(source, source ^ d) for source in...  6.26 us
    unnamed x2, other arithmetic  1.48 us
  transfers between devices with their start and end apart: 7, of which 3 were waited for; matrix products, arithmetic and copies ran while one was open for 3% of the time, Pallas kernels for 0%

profile of v5, /device:TPU:1, one launch (start us, length us, event | category | flops | bytes accessed | tf_op | source)
XLA Modules:
  0.0 49.1 jit_solution(16320049241161522336)
XLA Ops:
  0.6 0.7 %convert.23 = bf16[1,16,344]{2,1,0:T(8,128)(2,1)S(1)} convert(f32[1,16,344]{2,1,0:T(8,128)} %param.16) | non-fusion elementwise | flops 5504 | bytes 33024
  1.4 3.1 %collective-permute-start.1 = (bf16[1,16,344]{2,1,0:T(8,128)(2,1)S(1)}, bf16[1,16,344]{2,1,0:T(8,128)(2,1)S(1)}, u32[]{:S(2)}, u32[]{:S(2)}) collective-permute-start(bf16[1,16,344]{2,1,0:T(8,128)(2,1)S(1)} %convert.23), channel_id=1, source_target_pairs={{0,16},{1,17},{2,18},{3,19},{4,20},{5,21},{6,22},{7,23},{8,24},{9,... | collective-permute-start | bytes 33032 | tf_op jit(solution)/shard_map/ppermute | solution.py:430
  4.5 1.3 %collective-permute-start = (bf16[1,16,344]{2,1,0:T(8,128)(2,1)S(1)}, bf16[1,16,344]{2,1,0:T(8,128)(2,1)S(1)}, u32[]{:S(2)}, u32[]{:S(2)}) collective-permute-start(bf16[1,16,344]{2,1,0:T(8,128)(2,1)S(1)} %convert.23), channel_id=1, source_target_pairs={{0,8},{1,9},{2,10},{3,11},{4,12},{5,13},{6,14},{7,15},{8,0},{9,1},... | collective-permute-start | bytes 33032 | tf_op jit(solution)/shard_map/ppermute | solution.py:430
  5.8 0.0 collective-permute-start.2
  5.8 0.7 %constant_dynamic-update-slice_fusion.6 = (bf16[16,16,344]{2,1,0:T(8,128)(2,1)S(1)}, bf16[1,16,344]{2,1,0:T(8,128)(2,1)S(1)}) fusion(f32[1,16,344]{2,1,0:T(8,128)} %param.16), kind=kLoop, calls=%fused_computation.7 | loop fusion | flops 5503 | bytes 46592
  6.6 0.0 collective-permute-done.1
  6.6 0.5 %collective-permute-done = bf16[1,16,344]{2,1,0:T(8,128)(2,1)S(1)} collective-permute-done((bf16[1,16,344]{2,1,0:T(8,128)(2,1)S(1)}, bf16[1,16,344]{2,1,0:T(8,128)(2,1)S(1)}, u32[]{:S(2)}, u32[]{:S(2)}) %collective-permute-start) | collective-permute-done | bytes 11040 | tf_op jit(solution)/shard_map/ppermute | solution.py:430
  7.1 3.1 %collective-permute-done.2 = bf16[1,16,344]{2,1,0:T(8,128)(2,1)S(1)} collective-permute-done((bf16[1,16,344]{2,1,0:T(8,128)(2,1)S(1)}, bf16[1,16,344]{2,1,0:T(8,128)(2,1)S(1)}, u32[]{:S(2)}, u32[]{:S(2)}) %collective-permute-start.2) | collective-permute-done | bytes 11040 | tf_op jit(solution)/shard_map/ppermute | solution.py:430
  10.2 2.2 %collective-permute-start.5 = (bf16[4,16,344]{2,1,0:T(8,128)(2,1)S(1)}, bf16[4,16,344]{2,1,0:T(8,128)(2,1)S(1)}, u32[]{:S(2)}, u32[]{:S(2)}) collective-permute-start(bf16[4,16,344]{2,1,0:T(8,128)(2,1)S(1)} %pad_maximum_fusion), channel_id=1, source_target_pairs={{0,5},{1,4},{2,7},{3,6},{4,1},{5,0},{6,3},{7,2},{8,13},{9,12},{10,... | collective-permute-start | bytes 132104 | tf_op jit(solution)/shard_map/ppermute | solution.py:430
  12.4 0.2 collective-permute-start.4
  12.6 0.3 collective-permute-start.3
  12.9 2.7 %collective-permute-done.3 = bf16[4,16,344]{2,1,0:T(8,128)(2,1)S(1)} collective-permute-done((bf16[4,16,344]{2,1,0:T(8,128)(2,1)S(1)}, bf16[4,16,344]{2,1,0:T(8,128)(2,1)S(1)}, u32[]{:S(2)}, u32[]{:S(2)}) %collective-permute-start.3) | collective-permute-done | bytes 44064 | tf_op jit(solution)/shard_map/ppermute | solution.py:430
  15.6 0.0 collective-permute-done.4
  15.6 0.0 collective-permute-done.5
  15.6 0.0 copy-start
  15.7 4.2 %collective-permute-start.6 = (bf16[16,16,344]{2,1,0:T(8,128)(2,1)S(1)}, bf16[16,16,344]{2,1,0:T(8,128)(2,1)S(1)}, u32[]{:S(2)}, u32[]{:S(2)}) collective-permute-start(bf16[16,16,344]{2,1,0:T(8,128)(2,1)S(1)} %constant_dynamic-update-slice_fusion.refs_0_), channel_id=1, source_target_pairs={{0,2},{1,3},{2,0},{3,1},{4,6},{5,7},{6,4},{7,5},{8,10},{9,11},{10,... | collective-permute-start | bytes 528392 | tf_op jit(solution)/shard_map/ppermute | solution.py:430
  21.8 0.6 %pad_add_fusion.place_ref = s32[2]{0:T(128)} fusion(s32[1]{0:T(128)} %bitcast.1, s32[1]{0:T(128)} %bitcast), kind=kLoop, calls=%fused_computation.8 | loop fusion | flops 2 | bytes 16 | tf_op jit(solution)/shard_map/stack | solution.py:458
  22.4 0.0 collective-permute-done.6.refs_1_
  22.4 0.0 copy-start.1
  22.4 0.0 copy-done
  22.4 0.7 %copy-done.1 = bf16[16,16,344]{2,1,0:T(8,128)(2,1)} copy-done((bf16[16,16,344]{2,1,0:T(8,128)(2,1)}, bf16[16,16,344]{2,1,0:T(8,128)(2,1)S(1)}, u32[]{:S(2)}) %copy-start.1) | copy-done | bytes 176152
  23.1 25.9 %shard_map.175 = (f32[1,344,1032]{2,1,0:T(8,128)}, f32[25,1,1032]{2,1,0:T(1,128)}, f32[1,344,1032]{2,1,0:T(8,128)}) custom-call(s32[1]{0:T(128)S(6)} %copy.25.layer_ref, s32[1]{0:T(128)S(6)} %copy.26.half_ref, s32[1]{0:T(128)S(6)} %copy.27.radius_ref, s32[2]{0:T(128)} %pad_add_fusion.place_ref, bf16[16,16,344]{2,1,0:T(8,128)(2,1)} %copy-done, ...), custom_call_target="tpu_custom_call" | custom-call | flops 7270563840 | bytes 8520192 | tf_op jit(solution)/shard_map/pallas_call | solution.py:379
  (7 shorter events, 0.1 us)
Async XLA Ops:
  1.4 5.2 %collective-permute-start.1 = (bf16[1,16,344]{2,1,0:T(8,128)(2,1)S(1)}, bf16[1,16,344]{2,1,0:T(8,128)(2,1)S(1)}, u32[]{:S(2)}, u32[]{:S(2)}) collective-permute-start(bf16[1,16,344]{2,1,0:T(8,128)(2,1)S(1)} %convert.23), channel_id=1, source_target_pairs={{0,16},{1,17},{2,18},{3,19},{4,20},{5,21},{6,22},{7,23},{8,24},{9,... | collective-permute-start | bytes 33032 | tf_op jit(solution)/shard_map/ppermute | solution.py:430
  4.5 2.5 %collective-permute-start = (bf16[1,16,344]{2,1,0:T(8,128)(2,1)S(1)}, bf16[1,16,344]{2,1,0:T(8,128)(2,1)S(1)}, u32[]{:S(2)}, u32[]{:S(2)}) collective-permute-start(bf16[1,16,344]{2,1,0:T(8,128)(2,1)S(1)} %convert.23), channel_id=1, source_target_pairs={{0,8},{1,9},{2,10},{3,11},{4,12},{5,13},{6,14},{7,15},{8,0},{9,1},... | collective-permute-start | bytes 33032 | tf_op jit(solution)/shard_map/ppermute | solution.py:430
  5.8 4.3 %collective-permute-start.2 = (bf16[1,16,344]{2,1,0:T(8,128)(2,1)S(1)}, bf16[1,16,344]{2,1,0:T(8,128)(2,1)S(1)}, u32[]{:S(2)}, u32[]{:S(2)}) collective-permute-start(bf16[1,16,344]{2,1,0:T(8,128)(2,1)S(1)} %convert.23), channel_id=1, source_target_pairs={{0,24},{1,25},{2,26},{3,27},{4,28},{5,29},{6,30},{7,31},{8,16},{9,... | collective-permute-start | bytes 33032 | tf_op jit(solution)/shard_map/ppermute | solution.py:430
  10.2 5.4 %collective-permute-start.5 = (bf16[4,16,344]{2,1,0:T(8,128)(2,1)S(1)}, bf16[4,16,344]{2,1,0:T(8,128)(2,1)S(1)}, u32[]{:S(2)}, u32[]{:S(2)}) collective-permute-start(bf16[4,16,344]{2,1,0:T(8,128)(2,1)S(1)} %pad_maximum_fusion), channel_id=1, source_target_pairs={{0,5},{1,4},{2,7},{3,6},{4,1},{5,0},{6,3},{7,2},{8,13},{9,12},{10,... | collective-permute-start | bytes 132104 | tf_op jit(solution)/shard_map/ppermute | solution.py:430
  12.4 3.2 %collective-permute-start.4 = (bf16[4,16,344]{2,1,0:T(8,128)(2,1)S(1)}, bf16[4,16,344]{2,1,0:T(8,128)(2,1)S(1)}, u32[]{:S(2)}, u32[]{:S(2)}) collective-permute-start(bf16[4,16,344]{2,1,0:T(8,128)(2,1)S(1)} %pad_maximum_fusion), channel_id=1, source_target_pairs={{0,4},{1,5},{2,6},{3,7},{4,0},{5,1},{6,2},{7,3},{8,12},{9,13},{10,... | collective-permute-start | bytes 132104 | tf_op jit(solution)/shard_map/ppermute | solution.py:430
  12.6 2.9 %collective-permute-start.3 = (bf16[4,16,344]{2,1,0:T(8,128)(2,1)S(1)}, bf16[4,16,344]{2,1,0:T(8,128)(2,1)S(1)}, u32[]{:S(2)}, u32[]{:S(2)}) collective-permute-start(bf16[4,16,344]{2,1,0:T(8,128)(2,1)S(1)} %pad_maximum_fusion), channel_id=1, source_target_pairs={{0,1},{1,0},{2,3},{3,2},{4,5},{5,4},{6,7},{7,6},{8,9},{9,8},{10,11... | collective-permute-start | bytes 132104 | tf_op jit(solution)/shard_map/ppermute | solution.py:430
  15.6 6.7 %copy-start = (bf16[16,16,344]{2,1,0:T(8,128)(2,1)}, bf16[16,16,344]{2,1,0:T(8,128)(2,1)S(1)}, u32[]{:S(2)}) copy-start(bf16[16,16,344]{2,1,0:T(8,128)(2,1)S(1)} %constant_dynamic-update-slice_fusion.refs_0_) | copy-start | bytes 528388
  15.7 6.7 %collective-permute-start.6 = (bf16[16,16,344]{2,1,0:T(8,128)(2,1)S(1)}, bf16[16,16,344]{2,1,0:T(8,128)(2,1)S(1)}, u32[]{:S(2)}, u32[]{:S(2)}) collective-permute-start(bf16[16,16,344]{2,1,0:T(8,128)(2,1)S(1)} %constant_dynamic-update-slice_fusion.refs_0_), channel_id=1, source_target_pairs={{0,2},{1,3},{2,0},{3,1},{4,6},{5,7},{6,4},{7,5},{8,10},{9,11},{10,... | collective-permute-start | bytes 528392 | tf_op jit(solution)/shard_map/ppermute | solution.py:430
  22.4 0.7 %copy-start.1 = (bf16[16,16,344]{2,1,0:T(8,128)(2,1)}, bf16[16,16,344]{2,1,0:T(8,128)(2,1)S(1)}, u32[]{:S(2)}) copy-start(bf16[16,16,344]{2,1,0:T(8,128)(2,1)S(1)} %collective-permute-done.6.refs_1_) | copy-start | bytes 528388

commit v6 on v5

--- a/solution.py
+++ b/solution.py
@@ -267,11 +267,9 @@
             x_first[...] = x_ref[...]
             continue
         block = x_ref.shape[1]
-        for n, distance in enumerate(offset):
-            source = place_ref[0] ^ distance
-            source = (source & (parts - 1)) * (cells // block) + (source >> (parts.bit_length() - 1))
-            at = pl.multiple_of(source * block, block)
-            x_first[pl.ds(at, block), :] = x_ref[n]
+        for n, owner in enumerate(offset):
+            at = owner % parts * cells + owner // parts * block
+            x_first[at : at + block] = x_ref[n]
     for m in range(maps):
         second = slice(m * cells + half_cells, (m + 1) * cells)
         x_first[second] = dot(turn_half, x_first[second]).astype(BF16)
@@ -422,19 +420,17 @@
     return grad_up, grad_dw.transpose(1, 0, 2), grad_down
 
 
-def exchange(block, masks, devices):
-    offset = [0]
-    for mask in masks:
-        distances = [d for d in range(1, devices) if d & ~mask == 0]
-        parts = [block] + [
-            lax.ppermute(block, ("cand", "img"), [(source, source ^ d) for source in range(devices)])
-            for d in distances
-        ]
-        pieces = [[o ^ d for o in offset] for d in [0] + distances]
-        offset = sum(pieces, [])
-        if mask != masks[-1]:
-            block = jnp.concatenate(parts, axis=0).astype(BF16)
-    return parts, pieces
+def spread(block, cands, parts):
+    stages = [("cand", 4, cands // 4), ("cand", 2, 2), ("img", 1, parts), ("cand", 1, 2)]
+    owners = [0]
+    for axis, stride, size in stages:
+        count = parts if axis == "img" else cands
+        starts = [n for n in range(count) if n // stride % size == 0]
+        groups = [[n + stride * j for j in range(size)] for n in starts]
+        block = lax.all_gather(block, axis, axis_index_groups=groups, axis=0, tiled=True)
+        weight = stride * (parts if axis == "cand" else 1)
+        owners = [owner + weight * j for j in range(size) for owner in owners]
+    return [block], [owners]
 
 
 def body(
@@ -458,12 +454,9 @@
     place = jnp.stack([lax.axis_index("cand") * parts + part, part])
     weights = (teach_up, teach_dw, teach_down, cand_up, cand_dw, cand_down)
     scalars = (layer_of, expand_half, radius, place, parts, images, weights)
-    if batch == 1 and images == 2 and own_cells % 16 == 0 and devices & (devices - 1) == 0:
-        core = parts * (cands > 1)
-        near = (parts - 1) | (2 * core)
-        masks = [(devices - 1) & ~near & ~core, near, core]
-        pieces, offsets = exchange(first_maps, masks, devices)
-        return local_grads(pieces, offsets, images, *scalars)
+    if batch == 1 and images == 2 and own_cells % 16 == 0 and devices & (devices - 1) == 0 and cands >= 4:
+        pieces, owners = spread(first_maps.astype(BF16), cands, parts)
+        return local_grads(pieces, owners, images, *scalars)
     whole = lax.all_gather(first_maps.astype(BF16), ("img", "cand")).reshape(parts, cands, batch, own_cells, channels)
     whole = whole.transpose(0, 2, 1, 3, 4).reshape(images, -1, channels)
     group = 2 if images % 2 == 0 else 1

time: 49.4 us -> 57.1 us (1.16)
  blocking collectives: 0 us -> 26.7 us
  starting transfers between devices: 11.3 us -> 0 us
  waiting for transfers between devices: 6.26 us -> 0 us
  other arithmetic: 2.12 us -> 1.34 us
  local copies, waits for them, and re-layouts: 0.74 us -> 0 us
    all_gather x0 -> x4, blocking collectives: none -> 26.7 us  [spread(): lax.all_gather(block, axis, axis_index_groups=groups, axis=0, tiled=True)]
    ppermute x7 -> x0, starting transfers between devices: 11.3 us -> none  [exchange(): lax.ppermute(block, ('cand', 'img'), [(source, source ^ d) for source in...]
    ppermute x7 -> x0, waiting for transfers between devices: 6.26 us -> none  [exchange(): lax.ppermute(block, ('cand', 'img'), [(source, source ^ d) for source in...]
    unnamed x2 -> x0, other arithmetic: 1.48 us -> none
    convert_element_type x0 -> x1, other arithmetic: none -> 0.74 us  [body(): pieces, owners = spread(first_maps.astype(BF16), cands, parts)]
    unnamed x9 -> x0, local copies, waits for them, and re-layouts: 0.72 us -> none
  transfers between devices with their start and end apart: 7 -> 0, of which waited for: 3 -> 0; matrix products, arithmetic and copies ran while one was open for 3% -> 0% of each run, Pallas kernels for 0% -> 0%
where the time goes in v6:
time: 57.1 us; the launch traced here: 56.5 us
  blocking collectives  26.7 us (47%)
  Pallas kernels  25.8 us (45%)
  between operations  2.74 us (5%)
  other arithmetic  1.34 us (2%)
    all_gather x4, blocking collectives, spread(): lax.all_gather(block, axis, axis_index_groups=groups, axis=0, tiled=True)  26.7 us
    pallas_call x1, Pallas kernels, local_grads(): pl.pallas_call(functools.partial(grads_kernel, dims, offsets), out_shape=...  25.8 us

profile of v6, /device:TPU:1, one launch (start us, length us, event | category | flops | bytes accessed | tf_op | source)
XLA Modules:
  0.0 56.5 jit_solution(9893391662376082118)
XLA Ops:
  2.6 0.6 %pad_add_fusion.place_ref = s32[2]{0:T(128)} fusion(s32[1]{0:T(128)} %bitcast.1, s32[1]{0:T(128)} %bitcast), kind=kLoop, calls=%fused_computation | loop fusion | flops 2 | bytes 16 | tf_op jit(solution)/shard_map/stack | solution.py:454
  3.2 0.7 %convert_element_type.3 = bf16[1,16,344]{2,1,0:T(8,128)(2,1)S(1)} convert(f32[1,16,344]{2,1,0:T(8,128)} %param.16) | non-fusion elementwise | flops 5504 | bytes 33024 | tf_op jit(solution)/shard_map/convert_element_type | solution.py:458
  3.9 11.6 %all_gather.12 = bf16[4,16,344]{2,1,0:T(8,128)(2,1)S(1)} all-gather(bf16[1,16,344]{2,1,0:T(8,128)(2,1)S(1)} %convert_element_type.3), channel_id=1, replica_groups={{0,8,16,24},{2,10,18,26},{4,12,20,28},{6,14,22,30},{1,9,17,25},{3,11,19..., dimensions={0}, use_global_device_ids=true | all-gather | bytes 55040 | tf_op jit(solution)/shard_map/all_gather | solution.py:430
  15.6 3.6 %all_gather.13 = bf16[8,16,344]{2,1,0:T(8,128)(2,1)S(1)} all-gather(bf16[4,16,344]{2,1,0:T(8,128)(2,1)S(1)} %all_gather.12), channel_id=1, replica_groups={{0,4},{2,6},{8,12},{10,14},{16,20},{18,22},{24,28},{26,30},{1,5},{3,7},..., dimensions={0}, use_global_device_ids=true | all-gather | bytes 132096 | tf_op jit(solution)/shard_map/all_gather | solution.py:430
  19.2 4.1 %all_gather.14 = bf16[16,16,344]{2,1,0:T(8,128)(2,1)S(1)} all-gather(bf16[8,16,344]{2,1,0:T(8,128)(2,1)S(1)} %all_gather.13), channel_id=1, replica_groups={{0,1},{2,3},{4,5},{6,7},{8,9},{10,11},{12,13},{14,15},{16,17},{18,19},{..., dimensions={0}, use_global_device_ids=true | all-gather | bytes 264192 | tf_op jit(solution)/shard_map/all_gather | solution.py:430
  23.3 7.3 %all_gather.15.refs_0_ = bf16[32,16,344]{2,1,0:T(8,128)(2,1)} all-gather(bf16[16,16,344]{2,1,0:T(8,128)(2,1)S(1)} %all_gather.14), channel_id=1, replica_groups={{0,2},{4,6},{8,10},{12,14},{16,18},{20,22},{24,26},{28,30},{1,3},{5,7},..., dimensions={0}, use_global_device_ids=true | all-gather | bytes 528384 | tf_op jit(solution)/shard_map/all_gather | solution.py:430
  30.6 25.8 %shard_map.175 = (f32[1,344,1032]{2,1,0:T(8,128)}, f32[25,1,1032]{2,1,0:T(1,128)}, f32[1,344,1032]{2,1,0:T(8,128)}) custom-call(s32[1]{0:T(128)S(6)} %copy.19.layer_ref, s32[1]{0:T(128)S(6)} %copy.20.half_ref, s32[1]{0:T(128)S(6)} %copy.21.radius_ref, s32[2]{0:T(128)} %pad_add_fusion.place_ref, bf16[32,16,344]{2,1,0:T(8,128)(2,1)} %all_gather.15.refs_0_, ...), custom_call_target="tpu_custom_call" | custom-call | flops 7270563840 | bytes 8520192 | tf_op jit(solution)/shard_map/pallas_call | solution.py:377

commit v7 on v5

--- a/solution.py
+++ b/solution.py
@@ -90,13 +90,11 @@
 def grads_kernel(
     dims,
     offsets,
-    layer_ref,
-    half_ref,
-    radius_ref,
-    place_ref,
     *refs,
 ):
     pieces = len(offsets)
+    flags, refs = refs[0], refs[1:]
+    layer, half_units, radius = flags[:, 0:1], flags[:, 1:2], flags[:, 2:3]
     x_refs, in_hbm, refs, constants = refs[:pieces], refs[pieces : pieces + 6], refs[pieces + 6 : -6], refs[-6:]
     (
     teach_up,
@@ -165,7 +163,9 @@
 
     half_cells = cells // 2
     bases = [min(p * own // LANES * LANES, padded - window) for p in range(parts)]
-    start = place_ref[1] * own
+    part = lax.axis_index("img")
+    place = lax.axis_index("cand") * parts + part
+    start = part * own
     base = jnp.minimum(start // LANES * LANES, padded - window)
 
     def split(both):
@@ -191,7 +191,7 @@
             row = sum((index >= side * n).astype(jnp.int32) for n in range(1, side))
             ring = jnp.maximum(jnp.abs(row - side // 2), jnp.abs(index - side * row - side // 2))
             unit = lax.broadcasted_iota(jnp.int32, weights.shape, 1)
-            keep = (ring <= radius_ref[0]) & (unit < half_ref[0] * (hid // 2))
+            keep = (ring <= radius) & (unit < half_units * (hid // 2))
             weights = jnp.where(keep, weights, 0.0)
         dw_pad[slot, :taps, :hid] = weights
 
@@ -268,7 +268,7 @@
             continue
         block = x_ref.shape[1]
         for n, distance in enumerate(offset):
-            source = place_ref[0] ^ distance
+            source = place ^ distance
             source = (source & (parts - 1)) * (cells // block) + (source >> (parts.bit_length() - 1))
             at = pl.multiple_of(source * block, block)
             x_first[pl.ds(at, block), :] = x_ref[n]
@@ -281,7 +281,7 @@
     interleave(teacher(0, x_first, first))
     branch = sum(first)
     x_next[...] = (x_first[...].astype(F32) + jnp.transpose(branch)).astype(BF16)
-    x_now[...] = jnp.where(layer_ref[0] == 0, x_first[...], x_next[...])
+    x_now[...] = jnp.where(layer == 0, x_first[...], x_next[...])
     target[...] = branch
     load(2, True)
     load(1, False)
@@ -293,7 +293,7 @@
     second, third = [], []
     units = [teacher(1, x_next, second), candidate(x_now, third)]
     interleave([unit for pair in itertools.zip_longest(*units) for unit in pair if unit is not None])
-    err = (sum(third) - jnp.where(layer_ref[0] == 0, target[...], sum(second))) * scale
+    err = (sum(third) - jnp.where(layer == 0, target[...], sum(second))) * scale
     err_now[...] = jnp.transpose(0.5 * err).astype(BF16)
     err_turned[...] = err.astype(BF16)
     x_turned[...] = jnp.transpose(0.5 * x_now[...].astype(F32)).astype(BF16)
@@ -350,7 +350,7 @@
             row = sum((index >= side * n).astype(jnp.int32) for n in range(1, side))
             ring = jnp.maximum(jnp.abs(row - side // 2), jnp.abs(index - side * row - side // 2))
             unit = lax.broadcasted_iota(jnp.int32, own_dw.shape, 1) + start
-            keep = (ring <= radius_ref[0]) & (unit < half_ref[0] * (hid // 2))
+            keep = (ring <= radius) & (unit < half_units * (hid // 2))
             out_dw[:, 0] = jnp.where(keep, own_dw, 0.0)
     pltpu.make_async_copy(out_dw, grad_dw, out_sems.at[2]).start()
     pltpu.make_async_copy(out_down, grad_down.at[0], out_sems.at[0]).wait()
@@ -358,7 +358,7 @@
     pltpu.make_async_copy(out_dw, grad_dw, out_sems.at[2]).wait()
 
 
-def local_grads(pieces, offsets, maps, layer, half, radius, place, parts, images, weights):
+def local_grads(pieces, offsets, maps, flags, parts, images, weights):
     teach_up, teach_dw, teach_down, cand_up, cand_dw, cand_down = weights
     weights = (teach_up, teach_dw.transpose(1, 0, 2), teach_down, cand_up, cand_dw.transpose(1, 0, 2), cand_down)
     channels, hid = teach_up.shape[1:]
@@ -373,7 +373,6 @@
     window = min(round_up(own + spare, LANES), padded)
     tap_rows = round_up(taps, 16)
     dims = (maps, cells, channels, hid, taps, rows, parts, 1.0 / images)
-    smem = pl.BlockSpec(memory_space=pltpu.SMEM)
     vmem = pl.BlockSpec(memory_space=pltpu.VMEM)
     anywhere = pl.BlockSpec(memory_space=pl.ANY)
     grad_up, grad_dw, grad_down = pl.pallas_call(
@@ -383,7 +382,7 @@
             jax.ShapeDtypeStruct((taps, 1, own), F32),
             jax.ShapeDtypeStruct((1, channels, own), F32),
         ),
-        in_specs=[smem] * 4 + [vmem] * len(pieces) + [anywhere] * 12,
+        in_specs=[vmem] * (1 + len(pieces)) + [anywhere] * 12,
         out_specs=(anywhere, anywhere, anywhere),
         scratch_shapes=[
             pltpu.VMEM((3, channels, hid), BF16),
@@ -418,11 +417,11 @@
         cost_estimate=pl.CostEstimate(
             flops=20 * count * channels * hid, bytes_accessed=12 * channels * hid, transcendentals=6 * count * hid
         ),
-    )(layer, half, radius, place, *pieces, *constants, *weights)
+    )(flags, *pieces, *constants, *weights)
     return grad_up, grad_dw.transpose(1, 0, 2), grad_down
 
 
-def exchange(block, masks, devices):
+def exchange(block, masks, devices, flags):
     offset = [0]
     for mask in masks:
         distances = [d for d in range(1, devices) if d & ~mask == 0]
@@ -433,8 +432,8 @@
         pieces = [[o ^ d for o in offset] for d in [0] + distances]
         offset = sum(pieces, [])
         if mask != masks[-1]:
-            block = jnp.concatenate(parts, axis=0).astype(BF16)
-    return parts, pieces
+            block, flags = lax.optimization_barrier((jnp.concatenate(parts, axis=0), flags))
+    return parts, pieces, flags
 
 
 def body(
@@ -454,16 +453,15 @@
     devices = parts * cands
     batch, own_cells, channels = first_maps.shape
     images = parts * batch
-    part = lax.axis_index("img")
-    place = jnp.stack([lax.axis_index("cand") * parts + part, part])
     weights = (teach_up, teach_dw, teach_down, cand_up, cand_dw, cand_down)
-    scalars = (layer_of, expand_half, radius, place, parts, images, weights)
+    flags = jnp.concatenate([layer_of, expand_half, radius]).reshape(1, 3)
+    scalars = (flags, parts, images, weights)
     if batch == 1 and images == 2 and own_cells % 16 == 0 and devices & (devices - 1) == 0:
         core = parts * (cands > 1)
         near = (parts - 1) | (2 * core)
         masks = [(devices - 1) & ~near & ~core, near, core]
-        pieces, offsets = exchange(first_maps, masks, devices)
-        return local_grads(pieces, offsets, images, *scalars)
+        pieces, offsets, flags = exchange(first_maps.astype(BF16), masks, devices, flags)
+        return local_grads(pieces, offsets, images, flags, *scalars[1:])
     whole = lax.all_gather(first_maps.astype(BF16), ("img", "cand")).reshape(parts, cands, batch, own_cells, channels)
     whole = whole.transpose(0, 2, 1, 3, 4).reshape(images, -1, channels)
     group = 2 if images % 2 == 0 else 1

time: 49.4 us -> 46.3 us (0.937)
  waiting for transfers between devices: 6.26 us -> 4.31 us
  other arithmetic: 2.12 us -> 1.46 us
    ppermute x7, waiting for transfers between devices: 6.26 us -> 4.31 us  [exchange(): lax.ppermute(block, ('cand', 'img'), [(source, source ^ d) for source in...]
    unnamed x2 -> x0, other arithmetic: 1.48 us -> none
    convert_element_type x0 -> x1, other arithmetic: none -> 0.74 us  [body(): first_maps.astype(BF16)]
    reshape x0 -> x1, other arithmetic: none -> 0.66 us  [body(): flags = jnp.concatenate([layer_of, expand_half, radius]).reshape(1, 3)]
    another operation x1 -> x0, other arithmetic: 0.62 us -> none  [body(): place = jnp.stack([lax.axis_index('cand') * parts + part, part])]
  transfers between devices with their start and end apart: 7 -> 7, of which waited for: 3 -> 5; matrix products, arithmetic and copies ran while one was open for 3% -> 1% of each run, Pallas kernels for 0% -> 0%
where the time goes in v7:
time: 46.3 us; the launch traced here: 45.7 us
  Pallas kernels  25.5 us (55%)
  starting transfers between devices  11 us (24%)
  waiting for transfers between devices  4.31 us (9%)
  between operations  2.76 us (6%)
  other arithmetic  1.46 us (3%)
  local copies, waits for them, and re-layouts  0.66 us (1%)
    pallas_call x1, Pallas kernels, local_grads(): pl.pallas_call(functools.partial(grads_kernel, dims, offsets), out_shape=...  25.5 us
    ppermute x7, starting transfers between devices, exchange(): lax.ppermute(block, ('cand', 'img'), [(source, source ^ d) for source in...  11 us
    ppermute x7, waiting for transfers between devices, exchange(): lax.ppermute(block, ('cand', 'img'), [(source, source ^ d) for source in...  4.31 us
  transfers between devices with their start and end apart: 7, of which 5 were waited for; matrix products, arithmetic and copies ran while one was open for 1% of the time, Pallas kernels for 0%

profile of v7, /device:TPU:1, one launch (start us, length us, event | category | flops | bytes accessed | tf_op | source)
XLA Modules:
  0.0 45.7 jit_solution(13742933580303447095)
XLA Ops:
  0.6 0.7 %convert_element_type.3 = bf16[1,16,344]{2,1,0:T(8,128)(2,1)S(1)} convert(f32[1,16,344]{2,1,0:T(8,128)} %param.16) | non-fusion elementwise | flops 5504 | bytes 33024 | tf_op jit(solution)/shard_map/convert_element_type | solution.py:463
  1.4 4.2 %collective-permute-start.2 = (bf16[1,16,344]{2,1,0:T(8,128)(2,1)S(1)}, bf16[1,16,344]{2,1,0:T(8,128)(2,1)S(1)}, u32[]{:S(2)}, u32[]{:S(2)}) collective-permute-start(bf16[1,16,344]{2,1,0:T(8,128)(2,1)S(1)} %convert_element_type.3), channel_id=1, source_target_pairs={{0,24},{1,25},{2,26},{3,27},{4,28},{5,29},{6,30},{7,31},{8,16},{9,... | collective-permute-start | bytes 33032 | tf_op jit(solution)/shard_map/ppermute | solution.py:429
  5.5 0.0 collective-permute-start.1
  5.5 0.3 collective-permute-start
  7.8 0.7 %add_bitcast_fusion.refs_0_ = s32[1,3]{1,0:T(1,128)} fusion(s32[1]{0:T(128)S(6)} %copy.21, s32[1]{0:T(128)S(6)} %copy.20, s32[1]{0:T(128)S(6)} %copy.19), kind=kLoop, calls=%fused_computation.2 | loop fusion | flops 6 | bytes 24 | tf_op jit(solution)/shard_map/reshape | solution.py:457
  8.4 0.0 collective-permute-done.2
  8.4 0.6 %collective-permute-done.1 = bf16[1,16,344]{2,1,0:T(8,128)(2,1)S(1)} collective-permute-done((bf16[1,16,344]{2,1,0:T(8,128)(2,1)S(1)}, bf16[1,16,344]{2,1,0:T(8,128)(2,1)S(1)}, u32[]{:S(2)}, u32[]{:S(2)}) %collective-permute-start.1) | collective-permute-done | bytes 11040 | tf_op jit(solution)/shard_map/ppermute | solution.py:429
  9.0 0.0 collective-permute-done
  9.0 2.2 %collective-permute-start.5 = (bf16[4,16,344]{2,1,0:T(8,128)(2,1)S(1)}, bf16[4,16,344]{2,1,0:T(8,128)(2,1)S(1)}, u32[]{:S(2)}, u32[]{:S(2)}) collective-permute-start(bf16[4,16,344]{2,1,0:T(8,128)(2,1)S(1)} %pad_maximum_fusion.1), channel_id=1, source_target_pairs={{0,5},{1,4},{2,7},{3,6},{4,1},{5,0},{6,3},{7,2},{8,13},{9,12},{10,... | collective-permute-start | bytes 132104 | tf_op jit(solution)/shard_map/ppermute | solution.py:429
  11.2 0.2 collective-permute-start.4
  11.5 0.3 collective-permute-start.3
  11.7 1.2 %collective-permute-done.5 = bf16[4,16,344]{2,1,0:T(8,128)(2,1)S(1)} collective-permute-done((bf16[4,16,344]{2,1,0:T(8,128)(2,1)S(1)}, bf16[4,16,344]{2,1,0:T(8,128)(2,1)S(1)}, u32[]{:S(2)}, u32[]{:S(2)}) %collective-permute-start.5) | collective-permute-done | bytes 44064 | tf_op jit(solution)/shard_map/ppermute | solution.py:429
  12.9 1.3 %collective-permute-done.4 = bf16[4,16,344]{2,1,0:T(8,128)(2,1)S(1)} collective-permute-done((bf16[4,16,344]{2,1,0:T(8,128)(2,1)S(1)}, bf16[4,16,344]{2,1,0:T(8,128)(2,1)S(1)}, u32[]{:S(2)}, u32[]{:S(2)}) %collective-permute-start.4) | collective-permute-done | bytes 44064 | tf_op jit(solution)/shard_map/ppermute | solution.py:429
  14.2 0.2 collective-permute-done.3
  14.4 0.0 copy-start
  14.5 3.9 %collective-permute-start.6 = (bf16[16,16,344]{2,1,0:T(8,128)(2,1)S(1)}, bf16[16,16,344]{2,1,0:T(8,128)(2,1)S(1)}, u32[]{:S(2)}, u32[]{:S(2)}) collective-permute-start(bf16[16,16,344]{2,1,0:T(8,128)(2,1)S(1)} %pad_maximum_fusion.refs_1_), channel_id=1, source_target_pairs={{0,2},{1,3},{2,0},{3,1},{4,6},{5,7},{6,4},{7,5},{8,10},{9,11},{10,... | collective-permute-start | bytes 528392 | tf_op jit(solution)/shard_map/ppermute | solution.py:429
  18.3 1.1 %collective-permute-done.6.refs_2_ = bf16[16,16,344]{2,1,0:T(8,128)(2,1)S(1)} collective-permute-done((bf16[16,16,344]{2,1,0:T(8,128)(2,1)S(1)}, bf16[16,16,344]{2,1,0:T(8,128)(2,1)S(1)}, u32[]{:S(2)}, u32[]{:S(2)}) %collective-permute-start.6) | collective-permute-done | bytes 176160 | tf_op jit(solution)/shard_map/ppermute | solution.py:429
  19.4 0.0 copy-start.1
  19.4 0.0 copy-done
  19.4 0.7 %copy-done.1 = bf16[16,16,344]{2,1,0:T(8,128)(2,1)} copy-done((bf16[16,16,344]{2,1,0:T(8,128)(2,1)}, bf16[16,16,344]{2,1,0:T(8,128)(2,1)S(1)}, u32[]{:S(2)}) %copy-start.1) | copy-done | bytes 176152
  20.1 25.5 %shard_map.175 = (f32[1,344,1032]{2,1,0:T(8,128)}, f32[25,1,1032]{2,1,0:T(1,128)}, f32[1,344,1032]{2,1,0:T(8,128)}) custom-call(s32[1,3]{1,0:T(1,128)} %add_bitcast_fusion.refs_0_, bf16[16,16,344]{2,1,0:T(8,128)(2,1)} %copy-done, bf16[16,16,344]{2,1,0:T(8,128)(2,1)} %copy-done.1, bf16[336,256]{1,0:T(8,128)(2,1)} %constant.12.clone.refs_3_, ...), custom_call_target="tpu_custom_call" | custom-call | flops 7270563840 | bytes 8520192 | tf_op jit(solution)/shard_map/pallas_call | solution.py:378
  (2 shorter events, 0.1 us)
Async XLA Ops:
  1.4 7.0 %collective-permute-start.2 = (bf16[1,16,344]{2,1,0:T(8,128)(2,1)S(1)}, bf16[1,16,344]{2,1,0:T(8,128)(2,1)S(1)}, u32[]{:S(2)}, u32[]{:S(2)}) collective-permute-start(bf16[1,16,344]{2,1,0:T(8,128)(2,1)S(1)} %convert_element_type.3), channel_id=1, source_target_pairs={{0,24},{1,25},{2,26},{3,27},{4,28},{5,29},{6,30},{7,31},{8,16},{9,... | collective-permute-start | bytes 33032 | tf_op jit(solution)/shard_map/ppermute | solution.py:429
  5.5 3.4 %collective-permute-start.1 = (bf16[1,16,344]{2,1,0:T(8,128)(2,1)S(1)}, bf16[1,16,344]{2,1,0:T(8,128)(2,1)S(1)}, u32[]{:S(2)}, u32[]{:S(2)}) collective-permute-start(bf16[1,16,344]{2,1,0:T(8,128)(2,1)S(1)} %convert_element_type.3), channel_id=1, source_target_pairs={{0,16},{1,17},{2,18},{3,19},{4,20},{5,21},{6,22},{7,23},{8,24},{9,... | collective-permute-start | bytes 33032 | tf_op jit(solution)/shard_map/ppermute | solution.py:429
  5.5 3.4 %collective-permute-start = (bf16[1,16,344]{2,1,0:T(8,128)(2,1)S(1)}, bf16[1,16,344]{2,1,0:T(8,128)(2,1)S(1)}, u32[]{:S(2)}, u32[]{:S(2)}) collective-permute-start(bf16[1,16,344]{2,1,0:T(8,128)(2,1)S(1)} %convert_element_type.3), channel_id=1, source_target_pairs={{0,8},{1,9},{2,10},{3,11},{4,12},{5,13},{6,14},{7,15},{8,0},{9,1},... | collective-permute-start | bytes 33032 | tf_op jit(solution)/shard_map/ppermute | solution.py:429
  9.0 3.9 %collective-permute-start.5 = (bf16[4,16,344]{2,1,0:T(8,128)(2,1)S(1)}, bf16[4,16,344]{2,1,0:T(8,128)(2,1)S(1)}, u32[]{:S(2)}, u32[]{:S(2)}) collective-permute-start(bf16[4,16,344]{2,1,0:T(8,128)(2,1)S(1)} %pad_maximum_fusion.1), channel_id=1, source_target_pairs={{0,5},{1,4},{2,7},{3,6},{4,1},{5,0},{6,3},{7,2},{8,13},{9,12},{10,... | collective-permute-start | bytes 132104 | tf_op jit(solution)/shard_map/ppermute | solution.py:429
  11.2 2.9 %collective-permute-start.4 = (bf16[4,16,344]{2,1,0:T(8,128)(2,1)S(1)}, bf16[4,16,344]{2,1,0:T(8,128)(2,1)S(1)}, u32[]{:S(2)}, u32[]{:S(2)}) collective-permute-start(bf16[4,16,344]{2,1,0:T(8,128)(2,1)S(1)} %pad_maximum_fusion.1), channel_id=1, source_target_pairs={{0,4},{1,5},{2,6},{3,7},{4,0},{5,1},{6,2},{7,3},{8,12},{9,13},{10,... | collective-permute-start | bytes 132104 | tf_op jit(solution)/shard_map/ppermute | solution.py:429
  11.5 2.9 %collective-permute-start.3 = (bf16[4,16,344]{2,1,0:T(8,128)(2,1)S(1)}, bf16[4,16,344]{2,1,0:T(8,128)(2,1)S(1)}, u32[]{:S(2)}, u32[]{:S(2)}) collective-permute-start(bf16[4,16,344]{2,1,0:T(8,128)(2,1)S(1)} %pad_maximum_fusion.1), channel_id=1, source_target_pairs={{0,1},{1,0},{2,3},{3,2},{4,5},{5,4},{6,7},{7,6},{8,9},{9,8},{10,11... | collective-permute-start | bytes 132104 | tf_op jit(solution)/shard_map/ppermute | solution.py:429
  14.4 5.0 %copy-start = (bf16[16,16,344]{2,1,0:T(8,128)(2,1)}, bf16[16,16,344]{2,1,0:T(8,128)(2,1)S(1)}, u32[]{:S(2)}) copy-start(bf16[16,16,344]{2,1,0:T(8,128)(2,1)S(1)} %pad_maximum_fusion.refs_1_) | copy-start | bytes 528388
  14.5 5.0 %collective-permute-start.6 = (bf16[16,16,344]{2,1,0:T(8,128)(2,1)S(1)}, bf16[16,16,344]{2,1,0:T(8,128)(2,1)S(1)}, u32[]{:S(2)}, u32[]{:S(2)}) collective-permute-start(bf16[16,16,344]{2,1,0:T(8,128)(2,1)S(1)} %pad_maximum_fusion.refs_1_), channel_id=1, source_target_pairs={{0,2},{1,3},{2,0},{3,1},{4,6},{5,7},{6,4},{7,5},{8,10},{9,11},{10,... | collective-permute-start | bytes 528392 | tf_op jit(solution)/shard_map/ppermute | solution.py:429
  19.4 0.7 %copy-start.1 = (bf16[16,16,344]{2,1,0:T(8,128)(2,1)}, bf16[16,16,344]{2,1,0:T(8,128)(2,1)S(1)}, u32[]{:S(2)}) copy-start(bf16[16,16,344]{2,1,0:T(8,128)(2,1)S(1)} %collective-permute-done.6.refs_2_) | copy-start | bytes 528388

commit v8 on v7

--- a/solution.py
+++ b/solution.py
@@ -13,8 +13,8 @@
 F32 = jnp.float32
 BF16 = jnp.bfloat16
 LANES = 128
-UNIT = 512
-BACK_UNIT = 384
+UNIT = 1024
+BACK_UNIT = 640
 DEPTH = 2
 STAGGER = 5
 
@@ -432,7 +432,9 @@
         pieces = [[o ^ d for o in offset] for d in [0] + distances]
         offset = sum(pieces, [])
         if mask != masks[-1]:
-            block, flags = lax.optimization_barrier((jnp.concatenate(parts, axis=0), flags))
+            block = jnp.concatenate(parts, axis=0)
+        if mask == masks[-2]:
+            block, flags = lax.optimization_barrier((block, flags))
     return parts, pieces, flags
 
 

time: 46.3 us -> 45.7 us (0.987)
  Pallas kernels: 25.5 us -> 24.9 us
    unnamed x0 -> x1, other arithmetic: none -> 0.74 us
    convert_element_type x1 -> x0, other arithmetic: 0.74 us -> none  [body(): first_maps.astype(BF16)]
    pallas_call x1, Pallas kernels: 25.5 us -> 24.9 us  [local_grads(): pl.pallas_call(functools.partial(grads_kernel, dims, offsets), out_shape=...]
  transfers between devices with their start and end apart: 7 -> 7, of which waited for: 5 -> 3; matrix products, arithmetic and copies ran while one was open for 1% -> 1% of each run, Pallas kernels for 0% -> 0%
where the time goes in v8:
time: 45.7 us; the launch traced here: 45.2 us
  Pallas kernels  24.9 us (54%)
  starting transfers between devices  11 us (24%)
  waiting for transfers between devices  4.33 us (9%)
  between operations  2.78 us (6%)
  other arithmetic  1.38 us (3%)
  local copies, waits for them, and re-layouts  0.73 us (2%)
    pallas_call x1, Pallas kernels, local_grads(): pl.pallas_call(functools.partial(grads_kernel, dims, offsets), out_shape=...  24.9 us
    ppermute x7, starting transfers between devices, exchange(): lax.ppermute(block, ('cand', 'img'), [(source, source ^ d) for source in...  11 us
    ppermute x7, waiting for transfers between devices, exchange(): lax.ppermute(block, ('cand', 'img'), [(source, source ^ d) for source in...  4.33 us
  transfers between devices with their start and end apart: 7, of which 3 were waited for; matrix products, arithmetic and copies ran while one was open for 1% of the time, Pallas kernels for 0%

profile of v8, /device:TPU:1, one launch (start us, length us, event | category | flops | bytes accessed | tf_op | source)
XLA Modules:
  0.0 45.2 jit_solution(15316876435908833466)
XLA Ops:
  0.6 0.7 %constant_dynamic-update-slice_fusion.6 = (bf16[16,16,344]{2,1,0:T(8,128)(2,1)S(1)}, bf16[1,16,344]{2,1,0:T(8,128)(2,1)S(1)}) fusion(f32[1,16,344]{2,1,0:T(8,128)} %param.16), kind=kLoop, calls=%fused_computation.7 | loop fusion | flops 5503 | bytes 46592
  1.4 4.2 %collective-permute-start.2 = (bf16[1,16,344]{2,1,0:T(8,128)(2,1)S(1)}, bf16[1,16,344]{2,1,0:T(8,128)(2,1)S(1)}, u32[]{:S(2)}, u32[]{:S(2)}) collective-permute-start(bf16[1,16,344]{2,1,0:T(8,128)(2,1)S(1)} %get-tuple-element.14), channel_id=1, source_target_pairs={{0,24},{1,25},{2,26},{3,27},{4,28},{5,29},{6,30},{7,31},{8,16},{9,... | collective-permute-start | bytes 33032 | tf_op jit(solution)/shard_map/ppermute | solution.py:429
  5.5 0.0 collective-permute-start.1
  5.5 0.3 collective-permute-start
  7.8 0.6 %add_bitcast_fusion.refs_0_ = s32[1,3]{1,0:T(1,128)} fusion(s32[1]{0:T(128)S(6)} %copy.27, s32[1]{0:T(128)S(6)} %copy.26, s32[1]{0:T(128)S(6)} %copy.25), kind=kLoop, calls=%fused_computation.8 | loop fusion | flops 6 | bytes 24 | tf_op jit(solution)/shard_map/reshape | solution.py:459
  8.4 0.0 collective-permute-done.2
  8.4 0.6 %collective-permute-done.1 = bf16[1,16,344]{2,1,0:T(8,128)(2,1)S(1)} collective-permute-done((bf16[1,16,344]{2,1,0:T(8,128)(2,1)S(1)}, bf16[1,16,344]{2,1,0:T(8,128)(2,1)S(1)}, u32[]{:S(2)}, u32[]{:S(2)}) %collective-permute-start.1) | collective-permute-done | bytes 11040 | tf_op jit(solution)/shard_map/ppermute | solution.py:429
  9.0 0.0 collective-permute-done
  9.0 2.2 %collective-permute-start.5 = (bf16[4,16,344]{2,1,0:T(8,128)(2,1)S(1)}, bf16[4,16,344]{2,1,0:T(8,128)(2,1)S(1)}, u32[]{:S(2)}, u32[]{:S(2)}) collective-permute-start(bf16[4,16,344]{2,1,0:T(8,128)(2,1)S(1)} %pad_maximum_fusion), channel_id=1, source_target_pairs={{0,5},{1,4},{2,7},{3,6},{4,1},{5,0},{6,3},{7,2},{8,13},{9,12},{10,... | collective-permute-start | bytes 132104 | tf_op jit(solution)/shard_map/ppermute | solution.py:429
  11.2 0.2 collective-permute-start.4
  11.5 0.3 collective-permute-start.3
  11.7 2.7 %collective-permute-done.3 = bf16[4,16,344]{2,1,0:T(8,128)(2,1)S(1)} collective-permute-done((bf16[4,16,344]{2,1,0:T(8,128)(2,1)S(1)}, bf16[4,16,344]{2,1,0:T(8,128)(2,1)S(1)}, u32[]{:S(2)}, u32[]{:S(2)}) %collective-permute-start.3) | collective-permute-done | bytes 44064 | tf_op jit(solution)/shard_map/ppermute | solution.py:429
  14.4 0.0 collective-permute-done.4
  14.4 0.0 collective-permute-done.5
  14.5 0.0 copy-start
  14.5 3.9 %collective-permute-start.6 = (bf16[16,16,344]{2,1,0:T(8,128)(2,1)S(1)}, bf16[16,16,344]{2,1,0:T(8,128)(2,1)S(1)}, u32[]{:S(2)}, u32[]{:S(2)}) collective-permute-start(bf16[16,16,344]{2,1,0:T(8,128)(2,1)S(1)} %constant_dynamic-update-slice_fusion.refs_1_), channel_id=1, source_target_pairs={{0,2},{1,3},{2,0},{3,1},{4,6},{5,7},{6,4},{7,5},{8,10},{9,11},{10,... | collective-permute-start | bytes 528392 | tf_op jit(solution)/shard_map/ppermute | solution.py:429
  18.4 1.1 %collective-permute-done.6.refs_2_ = bf16[16,16,344]{2,1,0:T(8,128)(2,1)S(1)} collective-permute-done((bf16[16,16,344]{2,1,0:T(8,128)(2,1)S(1)}, bf16[16,16,344]{2,1,0:T(8,128)(2,1)S(1)}, u32[]{:S(2)}, u32[]{:S(2)}) %collective-permute-start.6) | collective-permute-done | bytes 176160 | tf_op jit(solution)/shard_map/ppermute | solution.py:429
  19.4 0.0 copy-start.1
  19.4 0.0 copy-done
  19.4 0.7 %copy-done.1 = bf16[16,16,344]{2,1,0:T(8,128)(2,1)} copy-done((bf16[16,16,344]{2,1,0:T(8,128)(2,1)}, bf16[16,16,344]{2,1,0:T(8,128)(2,1)S(1)}, u32[]{:S(2)}) %copy-start.1) | copy-done | bytes 176152
  20.1 24.9 %shard_map.175 = (f32[1,344,1032]{2,1,0:T(8,128)}, f32[25,1,1032]{2,1,0:T(1,128)}, f32[1,344,1032]{2,1,0:T(8,128)}) custom-call(s32[1,3]{1,0:T(1,128)} %add_bitcast_fusion.refs_0_, bf16[16,16,344]{2,1,0:T(8,128)(2,1)} %copy-done, bf16[16,16,344]{2,1,0:T(8,128)(2,1)} %copy-done.1, bf16[336,256]{1,0:T(8,128)(2,1)} %constant.12.clone.refs_3_, ...), custom_call_target="tpu_custom_call" | custom-call | flops 7270563840 | bytes 8520192 | tf_op jit(solution)/shard_map/pallas_call | solution.py:378
  (7 shorter events, 0.1 us)
Async XLA Ops:
  1.4 7.0 %collective-permute-start.2 = (bf16[1,16,344]{2,1,0:T(8,128)(2,1)S(1)}, bf16[1,16,344]{2,1,0:T(8,128)(2,1)S(1)}, u32[]{:S(2)}, u32[]{:S(2)}) collective-permute-start(bf16[1,16,344]{2,1,0:T(8,128)(2,1)S(1)} %get-tuple-element.14), channel_id=1, source_target_pairs={{0,24},{1,25},{2,26},{3,27},{4,28},{5,29},{6,30},{7,31},{8,16},{9,... | collective-permute-start | bytes 33032 | tf_op jit(solution)/shard_map/ppermute | solution.py:429
  5.5 3.4 %collective-permute-start.1 = (bf16[1,16,344]{2,1,0:T(8,128)(2,1)S(1)}, bf16[1,16,344]{2,1,0:T(8,128)(2,1)S(1)}, u32[]{:S(2)}, u32[]{:S(2)}) collective-permute-start(bf16[1,16,344]{2,1,0:T(8,128)(2,1)S(1)} %get-tuple-element.14), channel_id=1, source_target_pairs={{0,16},{1,17},{2,18},{3,19},{4,20},{5,21},{6,22},{7,23},{8,24},{9,... | collective-permute-start | bytes 33032 | tf_op jit(solution)/shard_map/ppermute | solution.py:429
  5.5 3.4 %collective-permute-start = (bf16[1,16,344]{2,1,0:T(8,128)(2,1)S(1)}, bf16[1,16,344]{2,1,0:T(8,128)(2,1)S(1)}, u32[]{:S(2)}, u32[]{:S(2)}) collective-permute-start(bf16[1,16,344]{2,1,0:T(8,128)(2,1)S(1)} %get-tuple-element.14), channel_id=1, source_target_pairs={{0,8},{1,9},{2,10},{3,11},{4,12},{5,13},{6,14},{7,15},{8,0},{9,1},... | collective-permute-start | bytes 33032 | tf_op jit(solution)/shard_map/ppermute | solution.py:429
  9.0 5.4 %collective-permute-start.5 = (bf16[4,16,344]{2,1,0:T(8,128)(2,1)S(1)}, bf16[4,16,344]{2,1,0:T(8,128)(2,1)S(1)}, u32[]{:S(2)}, u32[]{:S(2)}) collective-permute-start(bf16[4,16,344]{2,1,0:T(8,128)(2,1)S(1)} %pad_maximum_fusion), channel_id=1, source_target_pairs={{0,5},{1,4},{2,7},{3,6},{4,1},{5,0},{6,3},{7,2},{8,13},{9,12},{10,... | collective-permute-start | bytes 132104 | tf_op jit(solution)/shard_map/ppermute | solution.py:429
  11.2 3.2 %collective-permute-start.4 = (bf16[4,16,344]{2,1,0:T(8,128)(2,1)S(1)}, bf16[4,16,344]{2,1,0:T(8,128)(2,1)S(1)}, u32[]{:S(2)}, u32[]{:S(2)}) collective-permute-start(bf16[4,16,344]{2,1,0:T(8,128)(2,1)S(1)} %pad_maximum_fusion), channel_id=1, source_target_pairs={{0,4},{1,5},{2,6},{3,7},{4,0},{5,1},{6,2},{7,3},{8,12},{9,13},{10,... | collective-permute-start | bytes 132104 | tf_op jit(solution)/shard_map/ppermute | solution.py:429
  11.5 2.9 %collective-permute-start.3 = (bf16[4,16,344]{2,1,0:T(8,128)(2,1)S(1)}, bf16[4,16,344]{2,1,0:T(8,128)(2,1)S(1)}, u32[]{:S(2)}, u32[]{:S(2)}) collective-permute-start(bf16[4,16,344]{2,1,0:T(8,128)(2,1)S(1)} %pad_maximum_fusion), channel_id=1, source_target_pairs={{0,1},{1,0},{2,3},{3,2},{4,5},{5,4},{6,7},{7,6},{8,9},{9,8},{10,11... | collective-permute-start | bytes 132104 | tf_op jit(solution)/shard_map/ppermute | solution.py:429
  14.5 5.0 %copy-start = (bf16[16,16,344]{2,1,0:T(8,128)(2,1)}, bf16[16,16,344]{2,1,0:T(8,128)(2,1)S(1)}, u32[]{:S(2)}) copy-start(bf16[16,16,344]{2,1,0:T(8,128)(2,1)S(1)} %constant_dynamic-update-slice_fusion.refs_1_) | copy-start | bytes 528388
  14.5 5.0 %collective-permute-start.6 = (bf16[16,16,344]{2,1,0:T(8,128)(2,1)S(1)}, bf16[16,16,344]{2,1,0:T(8,128)(2,1)S(1)}, u32[]{:S(2)}, u32[]{:S(2)}) collective-permute-start(bf16[16,16,344]{2,1,0:T(8,128)(2,1)S(1)} %constant_dynamic-update-slice_fusion.refs_1_), channel_id=1, source_target_pairs={{0,2},{1,3},{2,0},{3,1},{4,6},{5,7},{6,4},{7,5},{8,10},{9,11},{10,... | collective-permute-start | bytes 528392 | tf_op jit(solution)/shard_map/ppermute | solution.py:429
  19.4 0.7 %copy-start.1 = (bf16[16,16,344]{2,1,0:T(8,128)(2,1)}, bf16[16,16,344]{2,1,0:T(8,128)(2,1)S(1)}, u32[]{:S(2)}) copy-start(bf16[16,16,344]{2,1,0:T(8,128)(2,1)S(1)} %collective-permute-done.6.refs_2_) | copy-start | bytes 528388

commit v9 on v8

--- a/solution.py
+++ b/solution.py
@@ -95,7 +95,9 @@
     pieces = len(offsets)
     flags, refs = refs[0], refs[1:]
     layer, half_units, radius = flags[:, 0:1], flags[:, 1:2], flags[:, 2:3]
-    x_refs, in_hbm, refs, constants = refs[:pieces], refs[pieces : pieces + 6], refs[pieces + 6 : -6], refs[-6:]
+    count = pieces + 6
+    in_hbm, refs, in_vmem = refs[:count], refs[count:-count], refs[-count:]
+    x_refs, constants = in_vmem[:pieces], in_vmem[pieces:]
     (
     teach_up,
     teach_dw,
@@ -153,10 +155,10 @@
         ]
 
     staged = [
-        pltpu.make_async_copy(src, dst, in_sems.at[n]) for n, (src, dst) in enumerate(zip(in_hbm, constants))
+        pltpu.make_async_copy(src, dst, in_sems.at[n]) for n, (src, dst) in enumerate(zip(in_hbm, in_vmem))
     ]
     first_copies = copies(0)
-    for copy in [first_copies[1], *staged, first_copies[0], first_copies[2], *copies(2), *copies(1)]:
+    for copy in [first_copies[1], *staged, first_copies[0], first_copies[2]]:
         copy.start()
 
     dw_pad[...] = jnp.zeros_like(dw_pad)
@@ -277,6 +279,8 @@
         x_first[second] = dot(turn_half, x_first[second]).astype(BF16)
     for copy in copies(0)[::2]:
         copy.wait()
+    for copy in copies(2) + copies(1):
+        copy.start()
     first = []
     interleave(teacher(0, x_first, first))
     branch = sum(first)
@@ -382,7 +386,7 @@
             jax.ShapeDtypeStruct((taps, 1, own), F32),
             jax.ShapeDtypeStruct((1, channels, own), F32),
         ),
-        in_specs=[vmem] * (1 + len(pieces)) + [anywhere] * 12,
+        in_specs=[vmem] + [anywhere] * (len(pieces) + 12),
         out_specs=(anywhere, anywhere, anywhere),
         scratch_shapes=[
             pltpu.VMEM((3, channels, hid), BF16),
@@ -409,9 +413,9 @@
             pltpu.VMEM((channels, window), F32),
             pltpu.VMEM((tap_rows, window), F32),
             pltpu.SemaphoreType.DMA((3, 3)),
-            pltpu.SemaphoreType.DMA((len(constants),)),
+            pltpu.SemaphoreType.DMA((len(pieces) + len(constants),)),
             pltpu.SemaphoreType.DMA((3,)),
-            *[pltpu.VMEM(array.shape, BF16) for array in constants],
+            *[pltpu.VMEM(array.shape, BF16) for array in (*pieces, *constants)],
         ],
         compiler_params=pltpu.CompilerParams(vmem_limit_bytes=60 * 2**20),
         cost_estimate=pl.CostEstimate(
@@ -433,7 +437,10 @@
         offset = sum(pieces, [])
         if mask != masks[-1]:
             block = jnp.concatenate(parts, axis=0)
-        if mask == masks[-2]:
+        if mask == masks[0]:
+            block, flags = lax.optimization_barrier((block, flags))
+            flags = jnp.concatenate(flags).reshape(1, 3)
+        elif mask == masks[1]:
             block, flags = lax.optimization_barrier((block, flags))
     return parts, pieces, flags
 
@@ -456,8 +463,8 @@
     batch, own_cells, channels = first_maps.shape
     images = parts * batch
     weights = (teach_up, teach_dw, teach_down, cand_up, cand_dw, cand_down)
-    flags = jnp.concatenate([layer_of, expand_half, radius]).reshape(1, 3)
-    scalars = (flags, parts, images, weights)
+    flags = (layer_of, expand_half, radius)
+    scalars = (jnp.concatenate(flags).reshape(1, 3), parts, images, weights)
     if batch == 1 and images == 2 and own_cells % 16 == 0 and devices & (devices - 1) == 0:
         core = parts * (cands > 1)
         near = (parts - 1) | (2 * core)

time: 45.7 us -> 44.2 us (0.967)
  Pallas kernels: 24.9 us -> 23.4 us
    pallas_call x1, Pallas kernels: 24.9 us -> 23.4 us  [local_grads(): pl.pallas_call(functools.partial(grads_kernel, dims, offsets), out_shape=...]
    unnamed x1 -> x0, other arithmetic: 0.74 us -> none
    convert_element_type x0 -> x1, other arithmetic: none -> 0.74 us  [body(): first_maps.astype(BF16)]
  transfers between devices with their start and end apart: 7 -> 7, of which waited for: 3 -> 5; matrix products, arithmetic and copies ran while one was open for 1% -> 2% of each run, Pallas kernels for 0% -> 0%
where the time goes in v9:
time: 44.2 us; the launch traced here: 43.6 us
  Pallas kernels  23.4 us (53%)
  starting transfers between devices  11 us (25%)
  waiting for transfers between devices  4.3 us (10%)
  between operations  2.77 us (6%)
  other arithmetic  1.46 us (3%)
  local copies, waits for them, and re-layouts  0.66 us (1%)
    pallas_call x1, Pallas kernels, local_grads(): pl.pallas_call(functools.partial(grads_kernel, dims, offsets), out_shape=...  23.4 us
    ppermute x7, starting transfers between devices, exchange(): lax.ppermute(block, ('cand', 'img'), [(source, source ^ d) for source in...  11 us
    ppermute x7, waiting for transfers between devices, exchange(): lax.ppermute(block, ('cand', 'img'), [(source, source ^ d) for source in...  4.3 us
  transfers between devices with their start and end apart: 7, of which 5 were waited for; matrix products, arithmetic and copies ran while one was open for 2% of the time, Pallas kernels for 0%

profile of v9, /device:TPU:1, one launch (start us, length us, event | category | flops | bytes accessed | tf_op | source)
XLA Modules:
  0.0 43.6 jit_solution(8040334628506646335)
XLA Ops:
  0.6 0.7 %convert_element_type.3 = bf16[1,16,344]{2,1,0:T(8,128)(2,1)S(1)} convert(f32[1,16,344]{2,1,0:T(8,128)} %param.16) | non-fusion elementwise | flops 5504 | bytes 33024 | tf_op jit(solution)/shard_map/convert_element_type | solution.py:472
  1.4 4.2 %collective-permute-start.2 = (bf16[1,16,344]{2,1,0:T(8,128)(2,1)S(1)}, bf16[1,16,344]{2,1,0:T(8,128)(2,1)S(1)}, u32[]{:S(2)}, u32[]{:S(2)}) collective-permute-start(bf16[1,16,344]{2,1,0:T(8,128)(2,1)S(1)} %convert_element_type.3), channel_id=1, source_target_pairs={{0,24},{1,25},{2,26},{3,27},{4,28},{5,29},{6,30},{7,31},{8,16},{9,... | collective-permute-start | bytes 33032 | tf_op jit(solution)/shard_map/ppermute | solution.py:433
  5.5 0.0 collective-permute-start.1
  5.5 0.3 collective-permute-start
  7.8 0.0 collective-permute-done.2
  7.8 1.2 %collective-permute-done.1 = bf16[1,16,344]{2,1,0:T(8,128)(2,1)S(1)} collective-permute-done((bf16[1,16,344]{2,1,0:T(8,128)(2,1)S(1)}, bf16[1,16,344]{2,1,0:T(8,128)(2,1)S(1)}, u32[]{:S(2)}, u32[]{:S(2)}) %collective-permute-start.1) | collective-permute-done | bytes 11040 | tf_op jit(solution)/shard_map/ppermute | solution.py:433
  9.0 0.0 collective-permute-done
  9.0 2.2 %collective-permute-start.5 = (bf16[4,16,344]{2,1,0:T(8,128)(2,1)S(1)}, bf16[4,16,344]{2,1,0:T(8,128)(2,1)S(1)}, u32[]{:S(2)}, u32[]{:S(2)}) collective-permute-start(bf16[4,16,344]{2,1,0:T(8,128)(2,1)S(1)} %pad_maximum_fusion.1), channel_id=1, source_target_pairs={{0,5},{1,4},{2,7},{3,6},{4,1},{5,0},{6,3},{7,2},{8,13},{9,12},{10,... | collective-permute-start | bytes 132104 | tf_op jit(solution)/shard_map/ppermute | solution.py:433
  11.2 0.2 collective-permute-start.4
  11.5 0.3 collective-permute-start.3
  11.7 0.7 %add_bitcast_fusion.refs_0_ = s32[1,3]{1,0:T(1,128)} fusion(s32[1]{0:T(128)S(6)} %copy.21, s32[1]{0:T(128)S(6)} %copy.20, s32[1]{0:T(128)S(6)} %copy.19), kind=kLoop, calls=%fused_computation.2 | loop fusion | flops 6 | bytes 24 | tf_op jit(solution)/shard_map/reshape | solution.py:442
  12.4 0.5 %collective-permute-done.5 = bf16[4,16,344]{2,1,0:T(8,128)(2,1)S(1)} collective-permute-done((bf16[4,16,344]{2,1,0:T(8,128)(2,1)S(1)}, bf16[4,16,344]{2,1,0:T(8,128)(2,1)S(1)}, u32[]{:S(2)}, u32[]{:S(2)}) %collective-permute-start.5) | collective-permute-done | bytes 44064 | tf_op jit(solution)/shard_map/ppermute | solution.py:433
  12.9 1.3 %collective-permute-done.4 = bf16[4,16,344]{2,1,0:T(8,128)(2,1)S(1)} collective-permute-done((bf16[4,16,344]{2,1,0:T(8,128)(2,1)S(1)}, bf16[4,16,344]{2,1,0:T(8,128)(2,1)S(1)}, u32[]{:S(2)}, u32[]{:S(2)}) %collective-permute-start.4) | collective-permute-done | bytes 44064 | tf_op jit(solution)/shard_map/ppermute | solution.py:433
  14.2 0.2 collective-permute-done.3
  14.4 0.0 copy-start
  14.5 3.9 %collective-permute-start.6 = (bf16[16,16,344]{2,1,0:T(8,128)(2,1)S(1)}, bf16[16,16,344]{2,1,0:T(8,128)(2,1)S(1)}, u32[]{:S(2)}, u32[]{:S(2)}) collective-permute-start(bf16[16,16,344]{2,1,0:T(8,128)(2,1)S(1)} %pad_maximum_fusion.refs_1_), channel_id=1, source_target_pairs={{0,2},{1,3},{2,0},{3,1},{4,6},{5,7},{6,4},{7,5},{8,10},{9,11},{10,... | collective-permute-start | bytes 528392 | tf_op jit(solution)/shard_map/ppermute | solution.py:433
  18.3 1.1 %collective-permute-done.6.refs_2_ = bf16[16,16,344]{2,1,0:T(8,128)(2,1)S(1)} collective-permute-done((bf16[16,16,344]{2,1,0:T(8,128)(2,1)S(1)}, bf16[16,16,344]{2,1,0:T(8,128)(2,1)S(1)}, u32[]{:S(2)}, u32[]{:S(2)}) %collective-permute-start.6) | collective-permute-done | bytes 176160 | tf_op jit(solution)/shard_map/ppermute | solution.py:433
  19.4 0.0 copy-start.1
  19.4 0.0 copy-done
  19.4 0.7 %copy-done.1 = bf16[16,16,344]{2,1,0:T(8,128)(2,1)} copy-done((bf16[16,16,344]{2,1,0:T(8,128)(2,1)}, bf16[16,16,344]{2,1,0:T(8,128)(2,1)S(1)}, u32[]{:S(2)}) %copy-start.1) | copy-done | bytes 176152
  20.1 23.4 %shard_map.175 = (f32[1,344,1032]{2,1,0:T(8,128)}, f32[25,1,1032]{2,1,0:T(1,128)}, f32[1,344,1032]{2,1,0:T(8,128)}) custom-call(s32[1,3]{1,0:T(1,128)} %add_bitcast_fusion.refs_0_, bf16[16,16,344]{2,1,0:T(8,128)(2,1)} %copy-done, bf16[16,16,344]{2,1,0:T(8,128)(2,1)} %copy-done.1, bf16[336,256]{1,0:T(8,128)(2,1)} %constant.12.clone.refs_3_, ...), custom_call_target="tpu_custom_call" | custom-call | flops 7270563840 | bytes 8520192 | tf_op jit(solution)/shard_map/pallas_call | solution.py:382
  (2 shorter events, 0.1 us)
Async XLA Ops:
  1.4 6.4 %collective-permute-start.2 = (bf16[1,16,344]{2,1,0:T(8,128)(2,1)S(1)}, bf16[1,16,344]{2,1,0:T(8,128)(2,1)S(1)}, u32[]{:S(2)}, u32[]{:S(2)}) collective-permute-start(bf16[1,16,344]{2,1,0:T(8,128)(2,1)S(1)} %convert_element_type.3), channel_id=1, source_target_pairs={{0,24},{1,25},{2,26},{3,27},{4,28},{5,29},{6,30},{7,31},{8,16},{9,... | collective-permute-start | bytes 33032 | tf_op jit(solution)/shard_map/ppermute | solution.py:433
  5.5 3.4 %collective-permute-start.1 = (bf16[1,16,344]{2,1,0:T(8,128)(2,1)S(1)}, bf16[1,16,344]{2,1,0:T(8,128)(2,1)S(1)}, u32[]{:S(2)}, u32[]{:S(2)}) collective-permute-start(bf16[1,16,344]{2,1,0:T(8,128)(2,1)S(1)} %convert_element_type.3), channel_id=1, source_target_pairs={{0,16},{1,17},{2,18},{3,19},{4,20},{5,21},{6,22},{7,23},{8,24},{9,... | collective-permute-start | bytes 33032 | tf_op jit(solution)/shard_map/ppermute | solution.py:433
  5.5 3.4 %collective-permute-start = (bf16[1,16,344]{2,1,0:T(8,128)(2,1)S(1)}, bf16[1,16,344]{2,1,0:T(8,128)(2,1)S(1)}, u32[]{:S(2)}, u32[]{:S(2)}) collective-permute-start(bf16[1,16,344]{2,1,0:T(8,128)(2,1)S(1)} %convert_element_type.3), channel_id=1, source_target_pairs={{0,8},{1,9},{2,10},{3,11},{4,12},{5,13},{6,14},{7,15},{8,0},{9,1},... | collective-permute-start | bytes 33032 | tf_op jit(solution)/shard_map/ppermute | solution.py:433
  9.0 3.9 %collective-permute-start.5 = (bf16[4,16,344]{2,1,0:T(8,128)(2,1)S(1)}, bf16[4,16,344]{2,1,0:T(8,128)(2,1)S(1)}, u32[]{:S(2)}, u32[]{:S(2)}) collective-permute-start(bf16[4,16,344]{2,1,0:T(8,128)(2,1)S(1)} %pad_maximum_fusion.1), channel_id=1, source_target_pairs={{0,5},{1,4},{2,7},{3,6},{4,1},{5,0},{6,3},{7,2},{8,13},{9,12},{10,... | collective-permute-start | bytes 132104 | tf_op jit(solution)/shard_map/ppermute | solution.py:433
  11.2 2.9 %collective-permute-start.4 = (bf16[4,16,344]{2,1,0:T(8,128)(2,1)S(1)}, bf16[4,16,344]{2,1,0:T(8,128)(2,1)S(1)}, u32[]{:S(2)}, u32[]{:S(2)}) collective-permute-start(bf16[4,16,344]{2,1,0:T(8,128)(2,1)S(1)} %pad_maximum_fusion.1), channel_id=1, source_target_pairs={{0,4},{1,5},{2,6},{3,7},{4,0},{5,1},{6,2},{7,3},{8,12},{9,13},{10,... | collective-permute-start | bytes 132104 | tf_op jit(solution)/shard_map/ppermute | solution.py:433
  11.5 2.9 %collective-permute-start.3 = (bf16[4,16,344]{2,1,0:T(8,128)(2,1)S(1)}, bf16[4,16,344]{2,1,0:T(8,128)(2,1)S(1)}, u32[]{:S(2)}, u32[]{:S(2)}) collective-permute-start(bf16[4,16,344]{2,1,0:T(8,128)(2,1)S(1)} %pad_maximum_fusion.1), channel_id=1, source_target_pairs={{0,1},{1,0},{2,3},{3,2},{4,5},{5,4},{6,7},{7,6},{8,9},{9,8},{10,11... | collective-permute-start | bytes 132104 | tf_op jit(solution)/shard_map/ppermute | solution.py:433
  14.4 5.0 %copy-start = (bf16[16,16,344]{2,1,0:T(8,128)(2,1)}, bf16[16,16,344]{2,1,0:T(8,128)(2,1)S(1)}, u32[]{:S(2)}) copy-start(bf16[16,16,344]{2,1,0:T(8,128)(2,1)S(1)} %pad_maximum_fusion.refs_1_) | copy-start | bytes 528388
  14.5 5.0 %collective-permute-start.6 = (bf16[16,16,344]{2,1,0:T(8,128)(2,1)S(1)}, bf16[16,16,344]{2,1,0:T(8,128)(2,1)S(1)}, u32[]{:S(2)}, u32[]{:S(2)}) collective-permute-start(bf16[16,16,344]{2,1,0:T(8,128)(2,1)S(1)} %pad_maximum_fusion.refs_1_), channel_id=1, source_target_pairs={{0,2},{1,3},{2,0},{3,1},{4,6},{5,7},{6,4},{7,5},{8,10},{9,11},{10,... | collective-permute-start | bytes 528392 | tf_op jit(solution)/shard_map/ppermute | solution.py:433
  19.4 0.7 %copy-start.1 = (bf16[16,16,344]{2,1,0:T(8,128)(2,1)}, bf16[16,16,344]{2,1,0:T(8,128)(2,1)S(1)}, u32[]{:S(2)}) copy-start(bf16[16,16,344]{2,1,0:T(8,128)(2,1)S(1)} %collective-permute-done.6.refs_2_) | copy-start | bytes 528388

commit v10 on v9

--- a/solution.py
+++ b/solution.py
@@ -15,8 +15,8 @@
 LANES = 128
 UNIT = 1024
 BACK_UNIT = 640
-DEPTH = 2
-STAGGER = 5
+DEPTH = 3
+STAGGER = 2
 
 
 def round_up(value, step):
@@ -197,7 +197,7 @@
             weights = jnp.where(keep, weights, 0.0)
         dw_pad[slot, :taps, :hid] = weights
 
-    def forward(slot, lhs, up, down, cols, save, results):
+    def forward(slot, lhs, up, down, cols, save, results, copy=None):
         keep = save is not None
         pre = dot(lhs[...], up[:, cols])
         yield
@@ -231,12 +231,14 @@
                 act[here, save] = acts[-1]
                 slope_k[here, save] = (more_k + wide_k - wide_k * bend_k).astype(BF16)
         yield
+        if copy is not None:
+            copy.wait()
         results.append(dot_nt(down[:, cols], jnp.concatenate(acts, axis=0)))
 
-    def teacher(slot, lhs, results):
+    def teacher(slot, lhs, results, copy=None):
         bounds = list(range(0, max(hid - UNIT // 2, 1), UNIT)) + [hid]
         return [
-            forward(slot, lhs, up_buf.at[slot], down_buf.at[slot], slice(lo, hi), None, results)
+            forward(slot, lhs, up_buf.at[slot], down_buf.at[slot], slice(lo, hi), None, results, copy if lo == 0 else None)
             for lo, hi in zip(bounds, bounds[1:])
         ]
 
@@ -277,12 +279,11 @@
     for m in range(maps):
         second = slice(m * cells + half_cells, (m + 1) * cells)
         x_first[second] = dot(turn_half, x_first[second]).astype(BF16)
-    for copy in copies(0)[::2]:
-        copy.wait()
+    first_copies[0].wait()
     for copy in copies(2) + copies(1):
         copy.start()
     first = []
-    interleave(teacher(0, x_first, first))
+    interleave(teacher(0, x_first, first, first_copies[2]))
     branch = sum(first)
     x_next[...] = (x_first[...].astype(F32) + jnp.transpose(branch)).astype(BF16)
     x_now[...] = jnp.where(layer == 0, x_first[...], x_next[...])

time: 44.2 us -> 43.4 us (0.982)
  Pallas kernels: 23.4 us -> 22.7 us
    pallas_call x1, Pallas kernels: 23.4 us -> 22.7 us  [local_grads(): pl.pallas_call(functools.partial(grads_kernel, dims, offsets), out_shape=...]
where the time goes in v10:
time: 43.4 us; the launch traced here: 42.9 us
  Pallas kernels  22.7 us (52%)
  starting transfers between devices  11 us (25%)
  waiting for transfers between devices  4.3 us (10%)
  between operations  2.77 us (6%)
  other arithmetic  1.46 us (3%)
  local copies, waits for them, and re-layouts  0.66 us (2%)
    pallas_call x1, Pallas kernels, local_grads(): pl.pallas_call(functools.partial(grads_kernel, dims, offsets), out_shape=...  22.7 us
    ppermute x7, starting transfers between devices, exchange(): lax.ppermute(block, ('cand', 'img'), [(source, source ^ d) for source in...  11 us
    ppermute x7, waiting for transfers between devices, exchange(): lax.ppermute(block, ('cand', 'img'), [(source, source ^ d) for source in...  4.3 us
  transfers between devices with their start and end apart: 7, of which 5 were waited for; matrix products, arithmetic and copies ran while one was open for 2% of the time, Pallas kernels for 0%

profile of v10, /device:TPU:1, one launch (start us, length us, event | category | flops | bytes accessed | tf_op | source)
XLA Modules:
  0.0 42.9 jit_solution(18335073081917423725)
XLA Ops:
  0.6 0.7 %convert_element_type.3 = bf16[1,16,344]{2,1,0:T(8,128)(2,1)S(1)} convert(f32[1,16,344]{2,1,0:T(8,128)} %param.16) | non-fusion elementwise | flops 5504 | bytes 33024 | tf_op jit(solution)/shard_map/convert_element_type | solution.py:473
  1.4 4.2 %collective-permute-start.2 = (bf16[1,16,344]{2,1,0:T(8,128)(2,1)S(1)}, bf16[1,16,344]{2,1,0:T(8,128)(2,1)S(1)}, u32[]{:S(2)}, u32[]{:S(2)}) collective-permute-start(bf16[1,16,344]{2,1,0:T(8,128)(2,1)S(1)} %convert_element_type.3), channel_id=1, source_target_pairs={{0,24},{1,25},{2,26},{3,27},{4,28},{5,29},{6,30},{7,31},{8,16},{9,... | collective-permute-start | bytes 33032 | tf_op jit(solution)/shard_map/ppermute | solution.py:434
  5.5 0.0 collective-permute-start.1
  5.5 0.3 collective-permute-start
  7.8 0.0 collective-permute-done.2
  7.8 1.2 %collective-permute-done.1 = bf16[1,16,344]{2,1,0:T(8,128)(2,1)S(1)} collective-permute-done((bf16[1,16,344]{2,1,0:T(8,128)(2,1)S(1)}, bf16[1,16,344]{2,1,0:T(8,128)(2,1)S(1)}, u32[]{:S(2)}, u32[]{:S(2)}) %collective-permute-start.1) | collective-permute-done | bytes 11040 | tf_op jit(solution)/shard_map/ppermute | solution.py:434
  9.0 0.0 collective-permute-done
  9.0 2.2 %collective-permute-start.5 = (bf16[4,16,344]{2,1,0:T(8,128)(2,1)S(1)}, bf16[4,16,344]{2,1,0:T(8,128)(2,1)S(1)}, u32[]{:S(2)}, u32[]{:S(2)}) collective-permute-start(bf16[4,16,344]{2,1,0:T(8,128)(2,1)S(1)} %pad_maximum_fusion.1), channel_id=1, source_target_pairs={{0,5},{1,4},{2,7},{3,6},{4,1},{5,0},{6,3},{7,2},{8,13},{9,12},{10,... | collective-permute-start | bytes 132104 | tf_op jit(solution)/shard_map/ppermute | solution.py:434
  11.2 0.2 collective-permute-start.4
  11.5 0.3 collective-permute-start.3
  11.7 0.7 %add_bitcast_fusion.refs_0_ = s32[1,3]{1,0:T(1,128)} fusion(s32[1]{0:T(128)S(6)} %copy.21, s32[1]{0:T(128)S(6)} %copy.20, s32[1]{0:T(128)S(6)} %copy.19), kind=kLoop, calls=%fused_computation.2 | loop fusion | flops 6 | bytes 24 | tf_op jit(solution)/shard_map/reshape | solution.py:443
  12.4 0.5 %collective-permute-done.5 = bf16[4,16,344]{2,1,0:T(8,128)(2,1)S(1)} collective-permute-done((bf16[4,16,344]{2,1,0:T(8,128)(2,1)S(1)}, bf16[4,16,344]{2,1,0:T(8,128)(2,1)S(1)}, u32[]{:S(2)}, u32[]{:S(2)}) %collective-permute-start.5) | collective-permute-done | bytes 44064 | tf_op jit(solution)/shard_map/ppermute | solution.py:434
  12.9 1.3 %collective-permute-done.4 = bf16[4,16,344]{2,1,0:T(8,128)(2,1)S(1)} collective-permute-done((bf16[4,16,344]{2,1,0:T(8,128)(2,1)S(1)}, bf16[4,16,344]{2,1,0:T(8,128)(2,1)S(1)}, u32[]{:S(2)}, u32[]{:S(2)}) %collective-permute-start.4) | collective-permute-done | bytes 44064 | tf_op jit(solution)/shard_map/ppermute | solution.py:434
  14.2 0.2 collective-permute-done.3
  14.4 0.0 copy-start
  14.5 3.9 %collective-permute-start.6 = (bf16[16,16,344]{2,1,0:T(8,128)(2,1)S(1)}, bf16[16,16,344]{2,1,0:T(8,128)(2,1)S(1)}, u32[]{:S(2)}, u32[]{:S(2)}) collective-permute-start(bf16[16,16,344]{2,1,0:T(8,128)(2,1)S(1)} %pad_maximum_fusion.refs_1_), channel_id=1, source_target_pairs={{0,2},{1,3},{2,0},{3,1},{4,6},{5,7},{6,4},{7,5},{8,10},{9,11},{10,... | collective-permute-start | bytes 528392 | tf_op jit(solution)/shard_map/ppermute | solution.py:434
  18.3 1.1 %collective-permute-done.6.refs_2_ = bf16[16,16,344]{2,1,0:T(8,128)(2,1)S(1)} collective-permute-done((bf16[16,16,344]{2,1,0:T(8,128)(2,1)S(1)}, bf16[16,16,344]{2,1,0:T(8,128)(2,1)S(1)}, u32[]{:S(2)}, u32[]{:S(2)}) %collective-permute-start.6) | collective-permute-done | bytes 176160 | tf_op jit(solution)/shard_map/ppermute | solution.py:434
  19.4 0.0 copy-start.1
  19.4 0.0 copy-done
  19.4 0.7 %copy-done.1 = bf16[16,16,344]{2,1,0:T(8,128)(2,1)} copy-done((bf16[16,16,344]{2,1,0:T(8,128)(2,1)}, bf16[16,16,344]{2,1,0:T(8,128)(2,1)S(1)}, u32[]{:S(2)}) %copy-start.1) | copy-done | bytes 176152
  20.1 22.7 %shard_map.175 = (f32[1,344,1032]{2,1,0:T(8,128)}, f32[25,1,1032]{2,1,0:T(1,128)}, f32[1,344,1032]{2,1,0:T(8,128)}) custom-call(s32[1,3]{1,0:T(1,128)} %add_bitcast_fusion.refs_0_, bf16[16,16,344]{2,1,0:T(8,128)(2,1)} %copy-done, bf16[16,16,344]{2,1,0:T(8,128)(2,1)} %copy-done.1, bf16[336,256]{1,0:T(8,128)(2,1)} %constant.12.clone.refs_3_, ...), custom_call_target="tpu_custom_call" | custom-call | flops 7270563840 | bytes 8520192 | tf_op jit(solution)/shard_map/pallas_call | solution.py:383
  (2 shorter events, 0.1 us)
Async XLA Ops:
  1.4 6.4 %collective-permute-start.2 = (bf16[1,16,344]{2,1,0:T(8,128)(2,1)S(1)}, bf16[1,16,344]{2,1,0:T(8,128)(2,1)S(1)}, u32[]{:S(2)}, u32[]{:S(2)}) collective-permute-start(bf16[1,16,344]{2,1,0:T(8,128)(2,1)S(1)} %convert_element_type.3), channel_id=1, source_target_pairs={{0,24},{1,25},{2,26},{3,27},{4,28},{5,29},{6,30},{7,31},{8,16},{9,... | collective-permute-start | bytes 33032 | tf_op jit(solution)/shard_map/ppermute | solution.py:434
  5.5 3.4 %collective-permute-start.1 = (bf16[1,16,344]{2,1,0:T(8,128)(2,1)S(1)}, bf16[1,16,344]{2,1,0:T(8,128)(2,1)S(1)}, u32[]{:S(2)}, u32[]{:S(2)}) collective-permute-start(bf16[1,16,344]{2,1,0:T(8,128)(2,1)S(1)} %convert_element_type.3), channel_id=1, source_target_pairs={{0,16},{1,17},{2,18},{3,19},{4,20},{5,21},{6,22},{7,23},{8,24},{9,... | collective-permute-start | bytes 33032 | tf_op jit(solution)/shard_map/ppermute | solution.py:434
  5.5 3.4 %collective-permute-start = (bf16[1,16,344]{2,1,0:T(8,128)(2,1)S(1)}, bf16[1,16,344]{2,1,0:T(8,128)(2,1)S(1)}, u32[]{:S(2)}, u32[]{:S(2)}) collective-permute-start(bf16[1,16,344]{2,1,0:T(8,128)(2,1)S(1)} %convert_element_type.3), channel_id=1, source_target_pairs={{0,8},{1,9},{2,10},{3,11},{4,12},{5,13},{6,14},{7,15},{8,0},{9,1},... | collective-permute-start | bytes 33032 | tf_op jit(solution)/shard_map/ppermute | solution.py:434
  9.0 3.9 %collective-permute-start.5 = (bf16[4,16,344]{2,1,0:T(8,128)(2,1)S(1)}, bf16[4,16,344]{2,1,0:T(8,128)(2,1)S(1)}, u32[]{:S(2)}, u32[]{:S(2)}) collective-permute-start(bf16[4,16,344]{2,1,0:T(8,128)(2,1)S(1)} %pad_maximum_fusion.1), channel_id=1, source_target_pairs={{0,5},{1,4},{2,7},{3,6},{4,1},{5,0},{6,3},{7,2},{8,13},{9,12},{10,... | collective-permute-start | bytes 132104 | tf_op jit(solution)/shard_map/ppermute | solution.py:434
  11.2 2.9 %collective-permute-start.4 = (bf16[4,16,344]{2,1,0:T(8,128)(2,1)S(1)}, bf16[4,16,344]{2,1,0:T(8,128)(2,1)S(1)}, u32[]{:S(2)}, u32[]{:S(2)}) collective-permute-start(bf16[4,16,344]{2,1,0:T(8,128)(2,1)S(1)} %pad_maximum_fusion.1), channel_id=1, source_target_pairs={{0,4},{1,5},{2,6},{3,7},{4,0},{5,1},{6,2},{7,3},{8,12},{9,13},{10,... | collective-permute-start | bytes 132104 | tf_op jit(solution)/shard_map/ppermute | solution.py:434
  11.5 2.9 %collective-permute-start.3 = (bf16[4,16,344]{2,1,0:T(8,128)(2,1)S(1)}, bf16[4,16,344]{2,1,0:T(8,128)(2,1)S(1)}, u32[]{:S(2)}, u32[]{:S(2)}) collective-permute-start(bf16[4,16,344]{2,1,0:T(8,128)(2,1)S(1)} %pad_maximum_fusion.1), channel_id=1, source_target_pairs={{0,1},{1,0},{2,3},{3,2},{4,5},{5,4},{6,7},{7,6},{8,9},{9,8},{10,11... | collective-permute-start | bytes 132104 | tf_op jit(solution)/shard_map/ppermute | solution.py:434
  14.4 5.0 %copy-start = (bf16[16,16,344]{2,1,0:T(8,128)(2,1)}, bf16[16,16,344]{2,1,0:T(8,128)(2,1)S(1)}, u32[]{:S(2)}) copy-start(bf16[16,16,344]{2,1,0:T(8,128)(2,1)S(1)} %pad_maximum_fusion.refs_1_) | copy-start | bytes 528388
  14.5 5.0 %collective-permute-start.6 = (bf16[16,16,344]{2,1,0:T(8,128)(2,1)S(1)}, bf16[16,16,344]{2,1,0:T(8,128)(2,1)S(1)}, u32[]{:S(2)}, u32[]{:S(2)}) collective-permute-start(bf16[16,16,344]{2,1,0:T(8,128)(2,1)S(1)} %pad_maximum_fusion.refs_1_), channel_id=1, source_target_pairs={{0,2},{1,3},{2,0},{3,1},{4,6},{5,7},{6,4},{7,5},{8,10},{9,11},{10,... | collective-permute-start | bytes 528392 | tf_op jit(solution)/shard_map/ppermute | solution.py:434
  19.4 0.7 %copy-start.1 = (bf16[16,16,344]{2,1,0:T(8,128)(2,1)}, bf16[16,16,344]{2,1,0:T(8,128)(2,1)S(1)}, u32[]{:S(2)}) copy-start(bf16[16,16,344]{2,1,0:T(8,128)(2,1)S(1)} %collective-permute-done.6.refs_2_) | copy-start | bytes 528388

commit v11 on v10

--- a/solution.py
+++ b/solution.py
@@ -14,7 +14,7 @@
 BF16 = jnp.bfloat16
 LANES = 128
 UNIT = 1024
-BACK_UNIT = 640
+BACK_UNIT = 384
 DEPTH = 3
 STAGGER = 2
 
@@ -310,7 +310,7 @@
         for shift in shifts:
             @pl.when(offset == shift)
             def _():
-                out[...] = wide[:, shift : shift + own]
+                out[...] = (pltpu.roll(wide[...], window - shift, 1) if shift else wide[...])[:, :own]
         pltpu.make_async_copy(out, grad.at[0], out_sems.at[n]).start()
 
     wide_up[...] = dot(err_turned[...], act[...])

time: 43.4 us -> 44.2 us (1.018)
  Pallas kernels: 22.7 us -> 23.5 us
    pallas_call x1, Pallas kernels: 22.7 us -> 23.5 us  [local_grads(): pl.pallas_call(functools.partial(grads_kernel, dims, offsets), out_shape=...]
  transfers between devices with their start and end apart: 7 -> 7, of which waited for: 5 -> 5; matrix products, arithmetic and copies ran while one was open for 2% -> 1% of each run, Pallas kernels for 0% -> 0%
where the time goes in v11:
time: 44.2 us; the launch traced here: 43.7 us
  Pallas kernels  23.5 us (53%)
  starting transfers between devices  11 us (25%)
  waiting for transfers between devices  4.3 us (10%)
  between operations  2.77 us (6%)
  other arithmetic  1.46 us (3%)
  local copies, waits for them, and re-layouts  0.66 us (1%)
    pallas_call x1, Pallas kernels, local_grads(): pl.pallas_call(functools.partial(grads_kernel, dims, offsets), out_shape=...  23.5 us
    ppermute x7, starting transfers between devices, exchange(): lax.ppermute(block, ('cand', 'img'), [(source, source ^ d) for source in...  11 us
    ppermute x7, waiting for transfers between devices, exchange(): lax.ppermute(block, ('cand', 'img'), [(source, source ^ d) for source in...  4.3 us
  transfers between devices with their start and end apart: 7, of which 5 were waited for; matrix products, arithmetic and copies ran while one was open for 1% of the time, Pallas kernels for 0%

profile of v11, /device:TPU:1, one launch (start us, length us, event | category | flops | bytes accessed | tf_op | source)
XLA Modules:
  0.0 43.7 jit_solution(4895640067762699173)
XLA Ops:
  0.6 0.7 %convert_element_type.3 = bf16[1,16,344]{2,1,0:T(8,128)(2,1)S(1)} convert(f32[1,16,344]{2,1,0:T(8,128)} %param.16) | non-fusion elementwise | flops 5504 | bytes 33024 | tf_op jit(solution)/shard_map/convert_element_type | solution.py:473
  1.4 4.2 %collective-permute-start.2 = (bf16[1,16,344]{2,1,0:T(8,128)(2,1)S(1)}, bf16[1,16,344]{2,1,0:T(8,128)(2,1)S(1)}, u32[]{:S(2)}, u32[]{:S(2)}) collective-permute-start(bf16[1,16,344]{2,1,0:T(8,128)(2,1)S(1)} %convert_element_type.3), channel_id=1, source_target_pairs={{0,24},{1,25},{2,26},{3,27},{4,28},{5,29},{6,30},{7,31},{8,16},{9,... | collective-permute-start | bytes 33032 | tf_op jit(solution)/shard_map/ppermute | solution.py:434
  5.5 0.0 collective-permute-start.1
  5.5 0.3 collective-permute-start
  7.8 0.0 collective-permute-done.2
  7.8 1.2 %collective-permute-done.1 = bf16[1,16,344]{2,1,0:T(8,128)(2,1)S(1)} collective-permute-done((bf16[1,16,344]{2,1,0:T(8,128)(2,1)S(1)}, bf16[1,16,344]{2,1,0:T(8,128)(2,1)S(1)}, u32[]{:S(2)}, u32[]{:S(2)}) %collective-permute-start.1) | collective-permute-done | bytes 11040 | tf_op jit(solution)/shard_map/ppermute | solution.py:434
  9.0 0.0 collective-permute-done
  9.0 2.2 %collective-permute-start.5 = (bf16[4,16,344]{2,1,0:T(8,128)(2,1)S(1)}, bf16[4,16,344]{2,1,0:T(8,128)(2,1)S(1)}, u32[]{:S(2)}, u32[]{:S(2)}) collective-permute-start(bf16[4,16,344]{2,1,0:T(8,128)(2,1)S(1)} %pad_maximum_fusion.1), channel_id=1, source_target_pairs={{0,5},{1,4},{2,7},{3,6},{4,1},{5,0},{6,3},{7,2},{8,13},{9,12},{10,... | collective-permute-start | bytes 132104 | tf_op jit(solution)/shard_map/ppermute | solution.py:434
  11.2 0.2 collective-permute-start.4
  11.5 0.3 collective-permute-start.3
  11.7 0.7 %add_bitcast_fusion.refs_0_ = s32[1,3]{1,0:T(1,128)} fusion(s32[1]{0:T(128)S(6)} %copy.21, s32[1]{0:T(128)S(6)} %copy.20, s32[1]{0:T(128)S(6)} %copy.19), kind=kLoop, calls=%fused_computation.2 | loop fusion | flops 6 | bytes 24 | tf_op jit(solution)/shard_map/reshape | solution.py:443
  12.4 0.5 %collective-permute-done.5 = bf16[4,16,344]{2,1,0:T(8,128)(2,1)S(1)} collective-permute-done((bf16[4,16,344]{2,1,0:T(8,128)(2,1)S(1)}, bf16[4,16,344]{2,1,0:T(8,128)(2,1)S(1)}, u32[]{:S(2)}, u32[]{:S(2)}) %collective-permute-start.5) | collective-permute-done | bytes 44064 | tf_op jit(solution)/shard_map/ppermute | solution.py:434
  12.9 1.3 %collective-permute-done.4 = bf16[4,16,344]{2,1,0:T(8,128)(2,1)S(1)} collective-permute-done((bf16[4,16,344]{2,1,0:T(8,128)(2,1)S(1)}, bf16[4,16,344]{2,1,0:T(8,128)(2,1)S(1)}, u32[]{:S(2)}, u32[]{:S(2)}) %collective-permute-start.4) | collective-permute-done | bytes 44064 | tf_op jit(solution)/shard_map/ppermute | solution.py:434
  14.2 0.2 collective-permute-done.3
  14.4 0.0 copy-start
  14.5 3.9 %collective-permute-start.6 = (bf16[16,16,344]{2,1,0:T(8,128)(2,1)S(1)}, bf16[16,16,344]{2,1,0:T(8,128)(2,1)S(1)}, u32[]{:S(2)}, u32[]{:S(2)}) collective-permute-start(bf16[16,16,344]{2,1,0:T(8,128)(2,1)S(1)} %pad_maximum_fusion.refs_1_), channel_id=1, source_target_pairs={{0,2},{1,3},{2,0},{3,1},{4,6},{5,7},{6,4},{7,5},{8,10},{9,11},{10,... | collective-permute-start | bytes 528392 | tf_op jit(solution)/shard_map/ppermute | solution.py:434
  18.3 1.1 %collective-permute-done.6.refs_2_ = bf16[16,16,344]{2,1,0:T(8,128)(2,1)S(1)} collective-permute-done((bf16[16,16,344]{2,1,0:T(8,128)(2,1)S(1)}, bf16[16,16,344]{2,1,0:T(8,128)(2,1)S(1)}, u32[]{:S(2)}, u32[]{:S(2)}) %collective-permute-start.6) | collective-permute-done | bytes 176160 | tf_op jit(solution)/shard_map/ppermute | solution.py:434
  19.4 0.0 copy-start.1
  19.4 0.0 copy-done
  19.4 0.7 %copy-done.1 = bf16[16,16,344]{2,1,0:T(8,128)(2,1)} copy-done((bf16[16,16,344]{2,1,0:T(8,128)(2,1)}, bf16[16,16,344]{2,1,0:T(8,128)(2,1)S(1)}, u32[]{:S(2)}) %copy-start.1) | copy-done | bytes 176152
  20.1 23.5 %shard_map.175 = (f32[1,344,1032]{2,1,0:T(8,128)}, f32[25,1,1032]{2,1,0:T(1,128)}, f32[1,344,1032]{2,1,0:T(8,128)}) custom-call(s32[1,3]{1,0:T(1,128)} %add_bitcast_fusion.refs_0_, bf16[16,16,344]{2,1,0:T(8,128)(2,1)} %copy-done, bf16[16,16,344]{2,1,0:T(8,128)(2,1)} %copy-done.1, bf16[336,256]{1,0:T(8,128)(2,1)} %constant.12.clone.refs_3_, ...), custom_call_target="tpu_custom_call" | custom-call | flops 7270563840 | bytes 8520192 | tf_op jit(solution)/shard_map/pallas_call | solution.py:383
  (2 shorter events, 0.1 us)
Async XLA Ops:
  1.4 6.4 %collective-permute-start.2 = (bf16[1,16,344]{2,1,0:T(8,128)(2,1)S(1)}, bf16[1,16,344]{2,1,0:T(8,128)(2,1)S(1)}, u32[]{:S(2)}, u32[]{:S(2)}) collective-permute-start(bf16[1,16,344]{2,1,0:T(8,128)(2,1)S(1)} %convert_element_type.3), channel_id=1, source_target_pairs={{0,24},{1,25},{2,26},{3,27},{4,28},{5,29},{6,30},{7,31},{8,16},{9,... | collective-permute-start | bytes 33032 | tf_op jit(solution)/shard_map/ppermute | solution.py:434
  5.5 3.4 %collective-permute-start.1 = (bf16[1,16,344]{2,1,0:T(8,128)(2,1)S(1)}, bf16[1,16,344]{2,1,0:T(8,128)(2,1)S(1)}, u32[]{:S(2)}, u32[]{:S(2)}) collective-permute-start(bf16[1,16,344]{2,1,0:T(8,128)(2,1)S(1)} %convert_element_type.3), channel_id=1, source_target_pairs={{0,16},{1,17},{2,18},{3,19},{4,20},{5,21},{6,22},{7,23},{8,24},{9,... | collective-permute-start | bytes 33032 | tf_op jit(solution)/shard_map/ppermute | solution.py:434
  5.5 3.4 %collective-permute-start = (bf16[1,16,344]{2,1,0:T(8,128)(2,1)S(1)}, bf16[1,16,344]{2,1,0:T(8,128)(2,1)S(1)}, u32[]{:S(2)}, u32[]{:S(2)}) collective-permute-start(bf16[1,16,344]{2,1,0:T(8,128)(2,1)S(1)} %convert_element_type.3), channel_id=1, source_target_pairs={{0,8},{1,9},{2,10},{3,11},{4,12},{5,13},{6,14},{7,15},{8,0},{9,1},... | collective-permute-start | bytes 33032 | tf_op jit(solution)/shard_map/ppermute | solution.py:434
  9.0 3.9 %collective-permute-start.5 = (bf16[4,16,344]{2,1,0:T(8,128)(2,1)S(1)}, bf16[4,16,344]{2,1,0:T(8,128)(2,1)S(1)}, u32[]{:S(2)}, u32[]{:S(2)}) collective-permute-start(bf16[4,16,344]{2,1,0:T(8,128)(2,1)S(1)} %pad_maximum_fusion.1), channel_id=1, source_target_pairs={{0,5},{1,4},{2,7},{3,6},{4,1},{5,0},{6,3},{7,2},{8,13},{9,12},{10,... | collective-permute-start | bytes 132104 | tf_op jit(solution)/shard_map/ppermute | solution.py:434
  11.2 2.9 %collective-permute-start.4 = (bf16[4,16,344]{2,1,0:T(8,128)(2,1)S(1)}, bf16[4,16,344]{2,1,0:T(8,128)(2,1)S(1)}, u32[]{:S(2)}, u32[]{:S(2)}) collective-permute-start(bf16[4,16,344]{2,1,0:T(8,128)(2,1)S(1)} %pad_maximum_fusion.1), channel_id=1, source_target_pairs={{0,4},{1,5},{2,6},{3,7},{4,0},{5,1},{6,2},{7,3},{8,12},{9,13},{10,... | collective-permute-start | bytes 132104 | tf_op jit(solution)/shard_map/ppermute | solution.py:434
  11.5 2.9 %collective-permute-start.3 = (bf16[4,16,344]{2,1,0:T(8,128)(2,1)S(1)}, bf16[4,16,344]{2,1,0:T(8,128)(2,1)S(1)}, u32[]{:S(2)}, u32[]{:S(2)}) collective-permute-start(bf16[4,16,344]{2,1,0:T(8,128)(2,1)S(1)} %pad_maximum_fusion.1), channel_id=1, source_target_pairs={{0,1},{1,0},{2,3},{3,2},{4,5},{5,4},{6,7},{7,6},{8,9},{9,8},{10,11... | collective-permute-start | bytes 132104 | tf_op jit(solution)/shard_map/ppermute | solution.py:434
  14.4 5.0 %copy-start = (bf16[16,16,344]{2,1,0:T(8,128)(2,1)}, bf16[16,16,344]{2,1,0:T(8,128)(2,1)S(1)}, u32[]{:S(2)}) copy-start(bf16[16,16,344]{2,1,0:T(8,128)(2,1)S(1)} %pad_maximum_fusion.refs_1_) | copy-start | bytes 528388
  14.5 5.0 %collective-permute-start.6 = (bf16[16,16,344]{2,1,0:T(8,128)(2,1)S(1)}, bf16[16,16,344]{2,1,0:T(8,128)(2,1)S(1)}, u32[]{:S(2)}, u32[]{:S(2)}) collective-permute-start(bf16[16,16,344]{2,1,0:T(8,128)(2,1)S(1)} %pad_maximum_fusion.refs_1_), channel_id=1, source_target_pairs={{0,2},{1,3},{2,0},{3,1},{4,6},{5,7},{6,4},{7,5},{8,10},{9,11},{10,... | collective-permute-start | bytes 528392 | tf_op jit(solution)/shard_map/ppermute | solution.py:434
  19.4 0.7 %copy-start.1 = (bf16[16,16,344]{2,1,0:T(8,128)(2,1)}, bf16[16,16,344]{2,1,0:T(8,128)(2,1)S(1)}, u32[]{:S(2)}) copy-start(bf16[16,16,344]{2,1,0:T(8,128)(2,1)S(1)} %collective-permute-done.6.refs_2_) | copy-start | bytes 528388

commit v12 on v10

--- a/solution.py
+++ b/solution.py
@@ -14,7 +14,7 @@
 BF16 = jnp.bfloat16
 LANES = 128
 UNIT = 1024
-BACK_UNIT = 640
+BACK_UNIT = 1152
 DEPTH = 3
 STAGGER = 2
 

time: 43.4 us -> 43.7 us (level)
  no operation moved by 1% of the time
where the time goes in v12:
time: 43.7 us; the launch traced here: 43.1 us
  Pallas kernels  22.9 us (52%)
  starting transfers between devices  11 us (25%)
  waiting for transfers between devices  4.3 us (10%)
  between operations  2.77 us (6%)
  other arithmetic  1.46 us (3%)
  local copies, waits for them, and re-layouts  0.66 us (2%)
    pallas_call x1, Pallas kernels, local_grads(): pl.pallas_call(functools.partial(grads_kernel, dims, offsets), out_shape=...  22.9 us
    ppermute x7, starting transfers between devices, exchange(): lax.ppermute(block, ('cand', 'img'), [(source, source ^ d) for source in...  11 us
    ppermute x7, waiting for transfers between devices, exchange(): lax.ppermute(block, ('cand', 'img'), [(source, source ^ d) for source in...  4.3 us
  transfers between devices with their start and end apart: 7, of which 5 were waited for; matrix products, arithmetic and copies ran while one was open for 2% of the time, Pallas kernels for 0%

profile of v12, /device:TPU:1, one launch (start us, length us, event | category | flops | bytes accessed | tf_op | source)
XLA Modules:
  0.0 43.1 jit_solution(15572305647511731312)
XLA Ops:
  0.6 0.7 %convert_element_type.3 = bf16[1,16,344]{2,1,0:T(8,128)(2,1)S(1)} convert(f32[1,16,344]{2,1,0:T(8,128)} %param.16) | non-fusion elementwise | flops 5504 | bytes 33024 | tf_op jit(solution)/shard_map/convert_element_type | solution.py:473
  1.4 4.2 %collective-permute-start.2 = (bf16[1,16,344]{2,1,0:T(8,128)(2,1)S(1)}, bf16[1,16,344]{2,1,0:T(8,128)(2,1)S(1)}, u32[]{:S(2)}, u32[]{:S(2)}) collective-permute-start(bf16[1,16,344]{2,1,0:T(8,128)(2,1)S(1)} %convert_element_type.3), channel_id=1, source_target_pairs={{0,24},{1,25},{2,26},{3,27},{4,28},{5,29},{6,30},{7,31},{8,16},{9,... | collective-permute-start | bytes 33032 | tf_op jit(solution)/shard_map/ppermute | solution.py:434
  5.5 0.0 collective-permute-start.1
  5.5 0.3 collective-permute-start
  7.8 0.0 collective-permute-done.2
  7.8 1.2 %collective-permute-done.1 = bf16[1,16,344]{2,1,0:T(8,128)(2,1)S(1)} collective-permute-done((bf16[1,16,344]{2,1,0:T(8,128)(2,1)S(1)}, bf16[1,16,344]{2,1,0:T(8,128)(2,1)S(1)}, u32[]{:S(2)}, u32[]{:S(2)}) %collective-permute-start.1) | collective-permute-done | bytes 11040 | tf_op jit(solution)/shard_map/ppermute | solution.py:434
  9.0 0.0 collective-permute-done
  9.0 2.2 %collective-permute-start.5 = (bf16[4,16,344]{2,1,0:T(8,128)(2,1)S(1)}, bf16[4,16,344]{2,1,0:T(8,128)(2,1)S(1)}, u32[]{:S(2)}, u32[]{:S(2)}) collective-permute-start(bf16[4,16,344]{2,1,0:T(8,128)(2,1)S(1)} %pad_maximum_fusion.1), channel_id=1, source_target_pairs={{0,5},{1,4},{2,7},{3,6},{4,1},{5,0},{6,3},{7,2},{8,13},{9,12},{10,... | collective-permute-start | bytes 132104 | tf_op jit(solution)/shard_map/ppermute | solution.py:434
  11.2 0.2 collective-permute-start.4
  11.5 0.3 collective-permute-start.3
  11.7 0.7 %add_bitcast_fusion.refs_0_ = s32[1,3]{1,0:T(1,128)} fusion(s32[1]{0:T(128)S(6)} %copy.21, s32[1]{0:T(128)S(6)} %copy.20, s32[1]{0:T(128)S(6)} %copy.19), kind=kLoop, calls=%fused_computation.2 | loop fusion | flops 6 | bytes 24 | tf_op jit(solution)/shard_map/reshape | solution.py:443
  12.4 0.5 %collective-permute-done.5 = bf16[4,16,344]{2,1,0:T(8,128)(2,1)S(1)} collective-permute-done((bf16[4,16,344]{2,1,0:T(8,128)(2,1)S(1)}, bf16[4,16,344]{2,1,0:T(8,128)(2,1)S(1)}, u32[]{:S(2)}, u32[]{:S(2)}) %collective-permute-start.5) | collective-permute-done | bytes 44064 | tf_op jit(solution)/shard_map/ppermute | solution.py:434
  12.9 1.3 %collective-permute-done.4 = bf16[4,16,344]{2,1,0:T(8,128)(2,1)S(1)} collective-permute-done((bf16[4,16,344]{2,1,0:T(8,128)(2,1)S(1)}, bf16[4,16,344]{2,1,0:T(8,128)(2,1)S(1)}, u32[]{:S(2)}, u32[]{:S(2)}) %collective-permute-start.4) | collective-permute-done | bytes 44064 | tf_op jit(solution)/shard_map/ppermute | solution.py:434
  14.2 0.2 collective-permute-done.3
  14.4 0.0 copy-start
  14.5 3.9 %collective-permute-start.6 = (bf16[16,16,344]{2,1,0:T(8,128)(2,1)S(1)}, bf16[16,16,344]{2,1,0:T(8,128)(2,1)S(1)}, u32[]{:S(2)}, u32[]{:S(2)}) collective-permute-start(bf16[16,16,344]{2,1,0:T(8,128)(2,1)S(1)} %pad_maximum_fusion.refs_1_), channel_id=1, source_target_pairs={{0,2},{1,3},{2,0},{3,1},{4,6},{5,7},{6,4},{7,5},{8,10},{9,11},{10,... | collective-permute-start | bytes 528392 | tf_op jit(solution)/shard_map/ppermute | solution.py:434
  18.3 1.1 %collective-permute-done.6.refs_2_ = bf16[16,16,344]{2,1,0:T(8,128)(2,1)S(1)} collective-permute-done((bf16[16,16,344]{2,1,0:T(8,128)(2,1)S(1)}, bf16[16,16,344]{2,1,0:T(8,128)(2,1)S(1)}, u32[]{:S(2)}, u32[]{:S(2)}) %collective-permute-start.6) | collective-permute-done | bytes 176160 | tf_op jit(solution)/shard_map/ppermute | solution.py:434
  19.4 0.0 copy-start.1
  19.4 0.0 copy-done
  19.4 0.7 %copy-done.1 = bf16[16,16,344]{2,1,0:T(8,128)(2,1)} copy-done((bf16[16,16,344]{2,1,0:T(8,128)(2,1)}, bf16[16,16,344]{2,1,0:T(8,128)(2,1)S(1)}, u32[]{:S(2)}) %copy-start.1) | copy-done | bytes 176152
  20.1 22.9 %shard_map.175 = (f32[1,344,1032]{2,1,0:T(8,128)}, f32[25,1,1032]{2,1,0:T(1,128)}, f32[1,344,1032]{2,1,0:T(8,128)}) custom-call(s32[1,3]{1,0:T(1,128)} %add_bitcast_fusion.refs_0_, bf16[16,16,344]{2,1,0:T(8,128)(2,1)} %copy-done, bf16[16,16,344]{2,1,0:T(8,128)(2,1)} %copy-done.1, bf16[336,256]{1,0:T(8,128)(2,1)} %constant.12.clone.refs_3_, ...), custom_call_target="tpu_custom_call" | custom-call | flops 7270563840 | bytes 8520192 | tf_op jit(solution)/shard_map/pallas_call | solution.py:383
  (2 shorter events, 0.1 us)
Async XLA Ops:
  1.4 6.4 %collective-permute-start.2 = (bf16[1,16,344]{2,1,0:T(8,128)(2,1)S(1)}, bf16[1,16,344]{2,1,0:T(8,128)(2,1)S(1)}, u32[]{:S(2)}, u32[]{:S(2)}) collective-permute-start(bf16[1,16,344]{2,1,0:T(8,128)(2,1)S(1)} %convert_element_type.3), channel_id=1, source_target_pairs={{0,24},{1,25},{2,26},{3,27},{4,28},{5,29},{6,30},{7,31},{8,16},{9,... | collective-permute-start | bytes 33032 | tf_op jit(solution)/shard_map/ppermute | solution.py:434
  5.5 3.4 %collective-permute-start.1 = (bf16[1,16,344]{2,1,0:T(8,128)(2,1)S(1)}, bf16[1,16,344]{2,1,0:T(8,128)(2,1)S(1)}, u32[]{:S(2)}, u32[]{:S(2)}) collective-permute-start(bf16[1,16,344]{2,1,0:T(8,128)(2,1)S(1)} %convert_element_type.3), channel_id=1, source_target_pairs={{0,16},{1,17},{2,18},{3,19},{4,20},{5,21},{6,22},{7,23},{8,24},{9,... | collective-permute-start | bytes 33032 | tf_op jit(solution)/shard_map/ppermute | solution.py:434
  5.5 3.4 %collective-permute-start = (bf16[1,16,344]{2,1,0:T(8,128)(2,1)S(1)}, bf16[1,16,344]{2,1,0:T(8,128)(2,1)S(1)}, u32[]{:S(2)}, u32[]{:S(2)}) collective-permute-start(bf16[1,16,344]{2,1,0:T(8,128)(2,1)S(1)} %convert_element_type.3), channel_id=1, source_target_pairs={{0,8},{1,9},{2,10},{3,11},{4,12},{5,13},{6,14},{7,15},{8,0},{9,1},... | collective-permute-start | bytes 33032 | tf_op jit(solution)/shard_map/ppermute | solution.py:434
  9.0 3.9 %collective-permute-start.5 = (bf16[4,16,344]{2,1,0:T(8,128)(2,1)S(1)}, bf16[4,16,344]{2,1,0:T(8,128)(2,1)S(1)}, u32[]{:S(2)}, u32[]{:S(2)}) collective-permute-start(bf16[4,16,344]{2,1,0:T(8,128)(2,1)S(1)} %pad_maximum_fusion.1), channel_id=1, source_target_pairs={{0,5},{1,4},{2,7},{3,6},{4,1},{5,0},{6,3},{7,2},{8,13},{9,12},{10,... | collective-permute-start | bytes 132104 | tf_op jit(solution)/shard_map/ppermute | solution.py:434
  11.2 2.9 %collective-permute-start.4 = (bf16[4,16,344]{2,1,0:T(8,128)(2,1)S(1)}, bf16[4,16,344]{2,1,0:T(8,128)(2,1)S(1)}, u32[]{:S(2)}, u32[]{:S(2)}) collective-permute-start(bf16[4,16,344]{2,1,0:T(8,128)(2,1)S(1)} %pad_maximum_fusion.1), channel_id=1, source_target_pairs={{0,4},{1,5},{2,6},{3,7},{4,0},{5,1},{6,2},{7,3},{8,12},{9,13},{10,... | collective-permute-start | bytes 132104 | tf_op jit(solution)/shard_map/ppermute | solution.py:434
  11.5 2.9 %collective-permute-start.3 = (bf16[4,16,344]{2,1,0:T(8,128)(2,1)S(1)}, bf16[4,16,344]{2,1,0:T(8,128)(2,1)S(1)}, u32[]{:S(2)}, u32[]{:S(2)}) collective-permute-start(bf16[4,16,344]{2,1,0:T(8,128)(2,1)S(1)} %pad_maximum_fusion.1), channel_id=1, source_target_pairs={{0,1},{1,0},{2,3},{3,2},{4,5},{5,4},{6,7},{7,6},{8,9},{9,8},{10,11... | collective-permute-start | bytes 132104 | tf_op jit(solution)/shard_map/ppermute | solution.py:434
  14.4 5.0 %copy-start = (bf16[16,16,344]{2,1,0:T(8,128)(2,1)}, bf16[16,16,344]{2,1,0:T(8,128)(2,1)S(1)}, u32[]{:S(2)}) copy-start(bf16[16,16,344]{2,1,0:T(8,128)(2,1)S(1)} %pad_maximum_fusion.refs_1_) | copy-start | bytes 528388
  14.5 5.0 %collective-permute-start.6 = (bf16[16,16,344]{2,1,0:T(8,128)(2,1)S(1)}, bf16[16,16,344]{2,1,0:T(8,128)(2,1)S(1)}, u32[]{:S(2)}, u32[]{:S(2)}) collective-permute-start(bf16[16,16,344]{2,1,0:T(8,128)(2,1)S(1)} %pad_maximum_fusion.refs_1_), channel_id=1, source_target_pairs={{0,2},{1,3},{2,0},{3,1},{4,6},{5,7},{6,4},{7,5},{8,10},{9,11},{10,... | collective-permute-start | bytes 528392 | tf_op jit(solution)/shard_map/ppermute | solution.py:434
  19.4 0.7 %copy-start.1 = (bf16[16,16,344]{2,1,0:T(8,128)(2,1)}, bf16[16,16,344]{2,1,0:T(8,128)(2,1)S(1)}, u32[]{:S(2)}) copy-start(bf16[16,16,344]{2,1,0:T(8,128)(2,1)S(1)} %collective-permute-done.6.refs_2_) | copy-start | bytes 528388
